TPU v7x, 128 devices: a whole 4x4x4 slice. The times are simulated.
128 devices in a mesh: gx: 16 (over y, z), gy: 8 (over x, core).
Axes of the slice: x: 4, y: 4, z: 4, core: 2. Of those that a mesh axis runs over, the one named last changes fastest.
Arguments:
- ensemble: float32 [80, 1048576], P(None, ('gx', 'gy')), may hold values from -6 to 6
- measured_line_locations: int32 [4, 2048], P(None, ('gx', 'gy')), may hold values from 0 to 8191
- obs_values: float32 [4, 2048], P(None, ('gx', 'gy')), may hold values from -8 to 8
- obs_error: float32 [4, 2048], P(None, ('gx', 'gy')), may hold values from 0.3 to 3
- obs_count: int32 [4, 128], P(None, ('gx', 'gy')), may hold values from 5 to 16, as said below
- obs_blocks: int32 [4, 8, 2048], replicated, may hold values from 0 to 1023, as said below
- loc_weights: float32 [4, 8, 2048], replicated, may hold values from 0.1 to 1
Outputs:
- posterior: float32 [80, 1048576], P(None, ('gx', 'gy'))
Inputs may be any that keep to these rules, and one draw needn't show every extreme that they name: `obs_count`: live slots of a device in a batch; slots from this count on are padding. In every batch some device has all 16 slots live. `obs_blocks`: block s holds global rows s * 1024 to s * 1024 + 1023. Every block in the list of an observation of device (i, j) lies on one of the devices (i + a mod 16, j + c mod 8) with a, c in -1, 0, 1 (periodic along both axes); entry 0 lies on the owning device. Entries may repeat.
All inputs are finite; a program needn't handle non-finite values.
Results may differ from a plain program's by a relative error of at most 0.0001.
Values sent between devices are 32-bit elements; how exact they have to be, the bound alone decides.
No kernel may reach another device: no remote copies, remote signals or barrier semaphores. Data moves between devices by JAX's collectives and lax.ppermute only.
A program may use at most 64 MiB of HBM per device.

v0:
```python
import jax
import jax.numpy as jnp
from jax import lax
from jax.sharding import PartitionSpec as P

BLK = 1024
BATCHES = 4


EPS = 1e-05


def with_halo(cells, sides, width):
    for axis, dim in sides:
        count = lax.axis_size(axis)
        head = lax.slice_in_dim(cells, 0, width, axis=dim)
        tail = lax.slice_in_dim(cells, cells.shape[dim] - width, cells.shape[dim], axis=dim)
        cells = jnp.concatenate(
            [
                lax.ppermute(tail, axis, [(i, (i + 1) % count) for i in range(count)]),
                cells,
                lax.ppermute(head, axis, [((i + 1) % count, i) for i in range(count)]),
            ],
            axis=dim,
        )
    return cells


def block_gain(scaled, increment, blocks, weights, owned):
    matches = (blocks[:, None, :] == owned[None, :, None]).astype(jnp.float32)
    coef = jnp.sum(weights[:, None, :] * matches, axis=0)
    return jnp.einsum("so,ko,mo->skm", coef, scaled, increment, precision=lax.Precision.HIGHEST)


def shards(
    ensemble, measured_line_locations, obs_values, obs_error, obs_count, obs_blocks, loc_weights
):
    members, rows_here = ensemble.shape
    slots_here = measured_line_locations.shape[1]
    blocks_here = rows_here // BLK
    grid_extent_east = lax.axis_size("gx")
    size_y = lax.axis_size("gy")
    index_x = lax.axis_index("gx")
    grid_index_north = lax.axis_index("gy")
    device = index_x * size_y + grid_index_north
    owned = device * blocks_here + jnp.arange(blocks_here, dtype=jnp.int32)
    within = jnp.arange(slots_here, dtype=jnp.int32)
    offsets = jnp.arange(3, dtype=jnp.int32) - 1
    near_x = (index_x + offsets[:, None]) % grid_extent_east
    near_y = (grid_index_north + offsets[None, :]) % size_y
    neighbour = (near_x * size_y + near_y).reshape(9)
    indices = (neighbour[:, None] * slots_here + within[None, :]).reshape(9 * slots_here)
    present_sweep_value = ensemble
    for group_of_sets in range(BATCHES):
        predicted_measurement = jnp.take(
            present_sweep_value, measured_line_locations[group_of_sets], axis=1
        )
        prior_average = jnp.mean(predicted_measurement, axis=0)
        measured_spread_vector = predicted_measurement - prior_average
        obs_var = (
            jnp.sum(measured_spread_vector * measured_spread_vector, axis=0) / (members - 1) + EPS
        )
        error = obs_error[group_of_sets]
        increment = (
            obs_var / (obs_var + error) * (obs_values[group_of_sets] - prior_average)
            + (jnp.sqrt(error / (obs_var + error)) - 1.0) * measured_spread_vector
        )
        live = (within < obs_count[group_of_sets, 0]).astype(jnp.float32)
        scaled = measured_spread_vector * (live / ((members - 1) * obs_var))
        message_bundle = jnp.stack([scaled, increment]).reshape(1, 1, 2 * members * slots_here)
        beside_all = with_halo(message_bundle, (("gx", 0), ("gy", 1)), 1)
        beside_all = beside_all.reshape(9, 2, members, slots_here)
        near_scaled = jnp.transpose(beside_all[:, 0], (1, 0, 2)).reshape(members, 9 * slots_here)
        near_increment = jnp.transpose(beside_all[:, 1], (1, 0, 2)).reshape(members, 9 * slots_here)
        blocks = jnp.take(obs_blocks[group_of_sets], indices, axis=1)
        weights = jnp.take(loc_weights[group_of_sets], indices, axis=1)
        kalman_gain_factor = block_gain(near_scaled, near_increment, blocks, weights, owned)
        member_deviation = (present_sweep_value - jnp.mean(present_sweep_value, axis=0)).reshape(
            members, blocks_here, BLK
        )
        state_adjust = jnp.einsum(
            "bnt,nbf->tbf", kalman_gain_factor, member_deviation, precision=lax.Precision.HIGHEST
        )
        present_sweep_value = present_sweep_value + state_adjust.reshape(members, rows_here)
    return present_sweep_value


def solution(mesh):
    in_specs = (
        P(None, ("gx", "gy")),
        P(None, ("gx", "gy")),
        P(None, ("gx", "gy")),
        P(None, ("gx", "gy")),
        P(None, ("gx", "gy")),
        P(),
        P(),
    )
    out_specs = P(None, ("gx", "gy"))
    return jax.shard_map(shards, mesh=mesh, in_specs=in_specs, out_specs=out_specs, check_vma=False)
```

profile of v0, /device:TPU:0, one launch (start us, length us, event | category | flops | bytes accessed | tf_op | source)
XLA Modules:
  0.0 185.8 jit_solution(5339435213409895682)
XLA Ops:
  0.0 1.4 compare_and_fusion
  1.4 4.9 %copy.91 = f32[80,8192]{0,1:T(8,128)} copy(f32[80,8192]{1,0:T(8,128)} %param.13) | data formatting | bytes 5242880 | tf_op args[0]
  6.9 2.7 %gather_fusion = f32[16,80]{1,0:T(8,128)S(1)} fusion(f32[80,8192]{0,1:T(8,128)} %copy.91, s32[1024]{0:T(1024)S(1)} %get-tuple-element.79), kind=kCustom, calls=%fused_computation.clone | custom fusion | bytes 10304 | tf_op jit(solution)/shard_map/jit(_take)/gather | solution.py:55
  12.3 2.1 %collective-permute-start = (f32[1,1,2560]{2,1,0:T(1,128)S(1)}, f32[1,1,2560]{2,1,0:T(1,128)S(1)}, u32[]{:S(2)}, u32[]{:S(2)}) collective-permute-start(f32[1,1,2560]{2,1,0:T(1,128)S(1)} %reshape.325), channel_id=1, source_target_pairs={{0,8},{8,16},{16,24},{24,32},{32,40},{40,48},{48,56},{56,64},{64,7... | collective-permute-start | bytes 30728 | tf_op jit(solution)/shard_map/ppermute | solution.py:20
  14.4 4.7 %collective-permute-start.1 = (f32[1,1,2560]{2,1,0:T(1,128)S(1)}, f32[1,1,2560]{2,1,0:T(1,128)S(1)}, u32[]{:S(2)}, u32[]{:S(2)}) collective-permute-start(f32[1,1,2560]{2,1,0:T(1,128)S(1)} %reshape.325), channel_id=1, source_target_pairs={{8,0},{16,8},{24,16},{32,24},{40,32},{48,40},{56,48},{64,56},{72,6... | collective-permute-start | bytes 30728 | tf_op jit(solution)/shard_map/ppermute | solution.py:22
  21.4 1.3 copy.146
  22.8 2.0 %gather_fusion.7 = s32[144,8]{1,0:T(8,128)S(1)} fusion(s32[8,2048]{0,1:T(8,128)} %bitcast.285, s32[1024]{0:T(1024)S(1)} %pad_clamp_fusion.3), kind=kCustom, calls=%fused_computation.7.clone | custom fusion | bytes 9792 | tf_op jit(solution)/shard_map/jit(_take)/gather | solution.py:75
  24.8 1.3 copy.148
  26.1 1.9 %gather_fusion.10 = s32[144,8]{1,0:T(8,128)S(1)} fusion(s32[8,2048]{0,1:T(8,128)} %bitcast.286, s32[1024]{0:T(1024)S(1)} %pad_clamp_fusion.3), kind=kCustom, calls=%fused_computation.8.clone | custom fusion | bytes 9792 | tf_op jit(solution)/shard_map/jit(_take)/gather | solution.py:75
  28.2 1.3 copy.143
  29.5 1.9 %gather_fusion.2 = f32[144,8]{1,0:T(8,128)S(1)} fusion(f32[8,2048]{0,1:T(8,128)} %bitcast.287, s32[1024]{0:T(1024)S(1)} %pad_clamp_fusion.3), kind=kCustom, calls=%fused_computation.2.clone | custom fusion | bytes 9792 | tf_op jit(solution)/shard_map/jit(_take)/gather | solution.py:76
  31.4 1.3 copy.145
  32.7 1.9 %gather_fusion.5 = f32[144,8]{1,0:T(8,128)S(1)} fusion(f32[8,2048]{0,1:T(8,128)} %bitcast.288, s32[1024]{0:T(1024)S(1)} %pad_clamp_fusion.3), kind=kCustom, calls=%fused_computation.9.clone | custom fusion | bytes 9792 | tf_op jit(solution)/shard_map/jit(_take)/gather | solution.py:76
  35.9 1.9 %gather_fusion.8 = f32[144,8]{1,0:T(8,128)S(1)} fusion(f32[8,2048]{0,1:T(8,128)} %bitcast.289, s32[1024]{0:T(1024)S(1)} %pad_clamp_fusion.3), kind=kCustom, calls=%fused_computation.10.clone | custom fusion | bytes 9792 | tf_op jit(solution)/shard_map/jit(_take)/gather | solution.py:76
  39.1 1.9 %gather_fusion.11 = f32[144,8]{1,0:T(8,128)S(1)} fusion(f32[8,2048]{0,1:T(8,128)} %bitcast.284, s32[1024]{0:T(1024)S(1)} %pad_clamp_fusion.3), kind=kCustom, calls=%fused_computation.11.clone | custom fusion | bytes 9792 | tf_op jit(solution)/shard_map/jit(_take)/gather | solution.py:76
  41.7 1.7 broadcast_subtract_fusion.3
  44.2 2.9 %collective-permute-start.3 = (f32[3,1,2560]{2,1,0:T(1,128)S(1)}, f32[3,1,2560]{2,1,0:T(1,128)S(1)}, u32[]{:S(2)}, u32[]{:S(2)}) collective-permute-start(f32[3,1,2560]{2,1,0:T(1,128)S(1)} %constant_dynamic-update-slice_fusion), channel_id=1, source_target_pairs={{1,0},{2,1},{3,2},{4,3},{5,4},{6,5},{7,6},{0,7},{9,8},{10,9},{11,1... | collective-permute-start | bytes 92168 | tf_op jit(solution)/shard_map/ppermute | solution.py:22
  52.5 1.5 convolution_bitcast_fusion.6
  54.0 3.9 %fusion.3 = f32[80,8,1024]{2,0,1:T(8,128)} fusion(f32[8,80,80]{2,1,0:T(8,128)S(1)} %convolution_bitcast_fusion.6, f32[10,8,8,1024]{3,2,1,0:T(8,128)S(1)} %bitcast.281), kind=kOutput, calls=%fused_computation.25 | convolution fusion | flops 629145600 | bytes 5447680 | tf_op jit(solution)/shard_map/bnt,nbf->tbf/dot_general | solution.py:81
  58.0 4.7 %copy.134 = f32[80,8,1024]{0,2,1:T(8,128)} copy(f32[80,8,1024]{2,0,1:T(8,128)} %fusion.3) | data formatting | bytes 5242880 | tf_op jit(solution)/shard_map/reshape | solution.py:84
  62.7 6.4 %fusion.36 = (f32[8192]{0:T(1024)S(1)}, f32[80,8192]{0,1:T(8,128)}) fusion(f32[80,8192]{0,1:T(8,128)} %copy.91, f32[80,8,1024]{0,2,1:T(8,128)} %copy.134), kind=kLoop, calls=%fused_computation.179 | loop fusion | flops 1302528 | bytes 7897088 | tf_op jit(solution)/shard_map/reduce_sum | solution.py:78
  69.2 2.9 %gather_fusion.3 = f32[16,80]{1,0:T(8,128)S(1)} fusion(f32[80,8192]{0,1:T(8,128)} %get-tuple-element.23, s32[1024]{0:T(1024)} %get-tuple-element.78), kind=kCustom, calls=%fused_computation.3.clone | custom fusion | bytes 10304 | tf_op jit(solution)/shard_map/jit(_take)/gather | solution.py:55
  73.5 5.4 %collective-permute-start.5 = (f32[1,1,2560]{2,1,0:T(1,128)S(1)}, f32[1,1,2560]{2,1,0:T(1,128)S(1)}, u32[]{:S(2)}, u32[]{:S(2)}) collective-permute-start(f32[1,1,2560]{2,1,0:T(1,128)S(1)} %reshape.332), channel_id=1, source_target_pairs={{8,0},{16,8},{24,16},{32,24},{40,32},{48,40},{56,48},{64,56},{72,6... | collective-permute-start | bytes 30728 | tf_op jit(solution)/shard_map/ppermute | solution.py:22
  78.9 1.6 collective-permute-done.4
  80.6 2.9 %collective-permute-start.7 = (f32[3,1,2560]{2,1,0:T(1,128)S(1)}, f32[3,1,2560]{2,1,0:T(1,128)S(1)}, u32[]{:S(2)}, u32[]{:S(2)}) collective-permute-start(f32[3,1,2560]{2,1,0:T(1,128)S(1)} %constant_dynamic-update-slice_fusion.3), channel_id=1, source_target_pairs={{1,0},{2,1},{3,2},{4,3},{5,4},{6,5},{7,6},{0,7},{9,8},{10,9},{11,1... | collective-permute-start | bytes 92168 | tf_op jit(solution)/shard_map/ppermute | solution.py:22
  83.5 4.2 %broadcast_subtract_fusion.2 = f32[80,8192]{0,1:T(8,128)} fusion(f32[80,8192]{0,1:T(8,128)} %get-tuple-element.23, f32[8192]{0:T(1024)S(1)} %broadcast_multiply_fusion.2), kind=kLoop, calls=%fused_computation.21 | loop fusion | flops 655360 | bytes 5275648 | tf_op jit(solution)/shard_map/sub | solution.py:78
  88.4 1.7 convolution_bitcast_fusion.5
  90.2 6.5 %convolution_bitcast_fusion.2 = f32[80,8,1024]{2,0,1:T(8,128)S(1)} fusion(f32[80,8,1024]{0,2,1:T(8,128)} %bitcast.279, f32[8,80,80]{2,1,0:T(8,128)S(1)} %convolution_bitcast_fusion.5), kind=kOutput, calls=%fused_computation.24 | convolution fusion | flops 629145600 | bytes 5447680 | tf_op jit(solution)/shard_map/bnt,nbf->tbf/dot_general | solution.py:81
  96.7 3.4 %copy.135 = f32[80,8,1024]{0,2,1:T(8,128)} copy(f32[80,8,1024]{2,0,1:T(8,128)S(1)} %convolution_bitcast_fusion.2) | data formatting | bytes 5242880 | tf_op jit(solution)/shard_map/reshape | solution.py:84
  100.1 6.5 %fusion.35 = (f32[8192]{0:T(1024)S(1)}, f32[80,8192]{0,1:T(8,128)}) fusion(f32[80,8192]{0,1:T(8,128)} %get-tuple-element.23, f32[80,8,1024]{0,2,1:T(8,128)} %copy.135), kind=kLoop, calls=%fused_computation.178 | loop fusion | flops 1302528 | bytes 7897088 | tf_op jit(solution)/shard_map/reduce_sum | solution.py:78
  106.5 2.9 %gather_fusion.6 = f32[16,80]{1,0:T(8,128)S(1)} fusion(f32[80,8192]{0,1:T(8,128)} %get-tuple-element.19, s32[1024]{0:T(1024)} %get-tuple-element.77), kind=kCustom, calls=%fused_computation.4.clone | custom fusion | bytes 10304 | tf_op jit(solution)/shard_map/jit(_take)/gather | solution.py:55
  110.8 5.6 %collective-permute-start.9 = (f32[1,1,2560]{2,1,0:T(1,128)S(1)}, f32[1,1,2560]{2,1,0:T(1,128)S(1)}, u32[]{:S(2)}, u32[]{:S(2)}) collective-permute-start(f32[1,1,2560]{2,1,0:T(1,128)S(1)} %reshape.339), channel_id=1, source_target_pairs={{8,0},{16,8},{24,16},{32,24},{40,32},{48,40},{56,48},{64,56},{72,6... | collective-permute-start | bytes 30728 | tf_op jit(solution)/shard_map/ppermute | solution.py:22
  116.4 1.4 collective-permute-done.8
  117.9 2.9 %collective-permute-start.11 = (f32[3,1,2560]{2,1,0:T(1,128)S(1)}, f32[3,1,2560]{2,1,0:T(1,128)S(1)}, u32[]{:S(2)}, u32[]{:S(2)}) collective-permute-start(f32[3,1,2560]{2,1,0:T(1,128)S(1)} %constant_dynamic-update-slice_fusion.6), channel_id=1, source_target_pairs={{1,0},{2,1},{3,2},{4,3},{5,4},{6,5},{7,6},{0,7},{9,8},{10,9},{11,1... | collective-permute-start | bytes 92168 | tf_op jit(solution)/shard_map/ppermute | solution.py:22
  120.8 4.1 %broadcast_subtract_fusion.1 = f32[80,8192]{0,1:T(8,128)} fusion(f32[80,8192]{0,1:T(8,128)} %get-tuple-element.19, f32[8192]{0:T(1024)S(1)} %broadcast_multiply_fusion.1), kind=kLoop, calls=%fused_computation.20 | loop fusion | flops 655360 | bytes 5275648 | tf_op jit(solution)/shard_map/sub | solution.py:78
  125.7 1.7 convolution_bitcast_fusion.4
  127.4 6.5 %convolution_bitcast_fusion.1 = f32[80,8,1024]{2,0,1:T(8,128)S(1)} fusion(f32[80,8,1024]{0,2,1:T(8,128)} %bitcast.280, f32[8,80,80]{2,1,0:T(8,128)S(1)} %convolution_bitcast_fusion.4), kind=kOutput, calls=%fused_computation.23 | convolution fusion | flops 629145600 | bytes 5447680 | tf_op jit(solution)/shard_map/bnt,nbf->tbf/dot_general | solution.py:81
  134.0 3.4 %copy.136 = f32[80,8,1024]{0,2,1:T(8,128)} copy(f32[80,8,1024]{2,0,1:T(8,128)S(1)} %convolution_bitcast_fusion.1) | data formatting | bytes 5242880 | tf_op jit(solution)/shard_map/reshape | solution.py:84
  137.4 6.4 %fusion.34 = (f32[8192]{0:T(1024)S(1)}, f32[80,8192]{0,1:T(8,128)}) fusion(f32[80,8192]{0,1:T(8,128)} %get-tuple-element.19, f32[80,8,1024]{0,2,1:T(8,128)} %copy.136), kind=kLoop, calls=%fused_computation.177 | loop fusion | flops 1302528 | bytes 7897088 | tf_op jit(solution)/shard_map/reduce_sum | solution.py:78
  143.8 2.9 %gather_fusion.9 = f32[16,80]{1,0:T(8,128)S(1)} fusion(f32[80,8192]{0,1:T(8,128)} %get-tuple-element.15, s32[1024]{0:T(1024)} %get-tuple-element.76), kind=kCustom, calls=%fused_computation.5.clone | custom fusion | bytes 10304 | tf_op jit(solution)/shard_map/jit(_take)/gather | solution.py:55
  148.1 5.9 %collective-permute-start.13 = (f32[1,1,2560]{2,1,0:T(1,128)S(1)}, f32[1,1,2560]{2,1,0:T(1,128)S(1)}, u32[]{:S(2)}, u32[]{:S(2)}) collective-permute-start(f32[1,1,2560]{2,1,0:T(1,128)S(1)} %reshape.346), channel_id=1, source_target_pairs={{8,0},{16,8},{24,16},{32,24},{40,32},{48,40},{56,48},{64,56},{72,6... | collective-permute-start | bytes 30728 | tf_op jit(solution)/shard_map/ppermute | solution.py:22
  155.4 3.0 %collective-permute-start.15 = (f32[3,1,2560]{2,1,0:T(1,128)S(1)}, f32[3,1,2560]{2,1,0:T(1,128)S(1)}, u32[]{:S(2)}, u32[]{:S(2)}) collective-permute-start(f32[3,1,2560]{2,1,0:T(1,128)S(1)} %constant_dynamic-update-slice_fusion.9), channel_id=1, source_target_pairs={{1,0},{2,1},{3,2},{4,3},{5,4},{6,5},{7,6},{0,7},{9,8},{10,9},{11,1... | collective-permute-start | bytes 92168 | tf_op jit(solution)/shard_map/ppermute | solution.py:22
  158.3 4.2 %broadcast_subtract_fusion = f32[80,8192]{0,1:T(8,128)} fusion(f32[80,8192]{0,1:T(8,128)} %get-tuple-element.15, f32[8192]{0:T(1024)S(1)} %broadcast_multiply_fusion), kind=kLoop, calls=%fused_computation.19 | loop fusion | flops 655360 | bytes 5275648 | tf_op jit(solution)/shard_map/sub | solution.py:78
  163.2 1.7 convolution_bitcast_fusion.3
  164.9 6.5 %convolution_bitcast_fusion = f32[80,8,1024]{2,0,1:T(8,128)S(1)} fusion(f32[80,8,1024]{0,2,1:T(8,128)} %bitcast.278, f32[8,80,80]{2,1,0:T(8,128)S(1)} %convolution_bitcast_fusion.3), kind=kOutput, calls=%fused_computation.22 | convolution fusion | flops 629145600 | bytes 5447680 | tf_op jit(solution)/shard_map/bnt,nbf->tbf/dot_general | solution.py:81
  171.5 3.4 %copy.137 = f32[80,8,1024]{0,2,1:T(8,128)} copy(f32[80,8,1024]{2,0,1:T(8,128)S(1)} %convolution_bitcast_fusion) | data formatting | bytes 5242880 | tf_op jit(solution)/shard_map/reshape | solution.py:84
  174.9 5.9 %bitcast_add_fusion = f32[80,8192]{0,1:T(8,128)} fusion(f32[80,8192]{0,1:T(8,128)} %get-tuple-element.15, f32[80,8,1024]{0,2,1:T(8,128)} %copy.137), kind=kLoop, calls=%fused_computation.12 | loop fusion | flops 655360 | bytes 7864320 | tf_op jit(solution)/shard_map/add | solution.py:84
  180.7 5.1 %copy.126 = f32[80,8192]{1,0:T(8,128)} copy(f32[80,8192]{0,1:T(8,128)} %bitcast_add_fusion) | data formatting | bytes 5242880 | tf_op jit(solution)/shard_map/add | solution.py:84
  (153 shorter events, 23.0 us)
Async XLA Ops:
  0.0 10.0 %copy-start.10 = (s32[4,1]{0,1:T(1,128)S(1)}, s32[4,1]{0,1:T(1,128)}, u32[]{:S(2)}) copy-start(s32[4,1]{0,1:T(1,128)} %param.17) | copy-start | bytes 52
  0.0 19.4 %copy-start.2 = (s32[4,8,2048]{2,1,0:T(8,128)S(1)}, s32[4,8,2048]{2,1,0:T(8,128)}, u32[]{:S(2)}) copy-start(s32[4,8,2048]{2,1,0:T(8,128)} %param.18) | copy-start | bytes 786436
  6.3 21.9 %copy-start.3 = (f32[4,8,2048]{2,1,0:T(8,128)S(1)}, f32[4,8,2048]{2,1,0:T(8,128)}, u32[]{:S(2)}) copy-start(f32[4,8,2048]{2,1,0:T(8,128)} %param.19) | copy-start | bytes 786436
  12.3 31.8 %collective-permute-start = (f32[1,1,2560]{2,1,0:T(1,128)S(1)}, f32[1,1,2560]{2,1,0:T(1,128)S(1)}, u32[]{:S(2)}, u32[]{:S(2)}) collective-permute-start(f32[1,1,2560]{2,1,0:T(1,128)S(1)} %reshape.325), channel_id=1, source_target_pairs={{0,8},{8,16},{16,24},{24,32},{32,40},{40,48},{48,56},{56,64},{64,7... | collective-permute-start | bytes 30728 | tf_op jit(solution)/shard_map/ppermute | solution.py:20
  14.4 29.8 %collective-permute-start.1 = (f32[1,1,2560]{2,1,0:T(1,128)S(1)}, f32[1,1,2560]{2,1,0:T(1,128)S(1)}, u32[]{:S(2)}, u32[]{:S(2)}) collective-permute-start(f32[1,1,2560]{2,1,0:T(1,128)S(1)} %reshape.325), channel_id=1, source_target_pairs={{8,0},{16,8},{24,16},{32,24},{40,32},{48,40},{56,48},{64,56},{72,6... | collective-permute-start | bytes 30728 | tf_op jit(solution)/shard_map/ppermute | solution.py:22
  22.7 18.8 %copy-start = (f32[80,8192]{1,0:T(8,128)S(1)}, f32[80,8192]{1,0:T(8,128)}, u32[]{:S(2)}) copy-start(f32[80,8192]{1,0:T(8,128)} %param.13) | copy-start | bytes 7864324
  43.4 10.6 %copy-start.1 = (f32[80,8192]{1,0:T(8,128)S(1)}, f32[80,8192]{1,0:T(8,128)}, u32[]{:S(2)}) copy-start(f32[80,8192]{1,0:T(8,128)} %broadcast_subtract_fusion.3) | copy-start | bytes 7864324
  44.2 4.5 %collective-permute-start.2 = (f32[3,1,2560]{2,1,0:T(1,128)S(1)}, f32[3,1,2560]{2,1,0:T(1,128)S(1)}, u32[]{:S(2)}, u32[]{:S(2)}) collective-permute-start(f32[3,1,2560]{2,1,0:T(1,128)S(1)} %constant_dynamic-update-slice_fusion), channel_id=1, source_target_pairs={{0,1},{1,2},{2,3},{3,4},{4,5},{5,6},{6,7},{7,0},{8,9},{9,10},{10,1... | collective-permute-start | bytes 92168 | tf_op jit(solution)/shard_map/ppermute | solution.py:20
  44.2 4.5 %collective-permute-start.3 = (f32[3,1,2560]{2,1,0:T(1,128)S(1)}, f32[3,1,2560]{2,1,0:T(1,128)S(1)}, u32[]{:S(2)}, u32[]{:S(2)}) collective-permute-start(f32[3,1,2560]{2,1,0:T(1,128)S(1)} %constant_dynamic-update-slice_fusion), channel_id=1, source_target_pairs={{1,0},{2,1},{3,2},{4,3},{5,4},{6,5},{7,6},{0,7},{9,8},{10,9},{11,1... | collective-permute-start | bytes 92168 | tf_op jit(solution)/shard_map/ppermute | solution.py:22
  62.7 9.3 %copy-start.9 = (pred[16]{0:T(512)(128)(4,1)S(1)}, pred[16]{0:T(512)(128)(4,1)}, u32[]{:S(2)}) copy-start(pred[16]{0:T(512)(128)(4,1)} %get-tuple-element.58) | copy-start | bytes 52
  62.7 9.7 %copy-start.11 = (f32[4,16]{1,0:T(4,128)S(1)}, f32[4,16]{1,0:T(4,128)}, u32[]{:S(2)}) copy-start(f32[4,16]{1,0:T(4,128)} %param.15) | copy-start | bytes 772
  62.7 9.7 %copy-start.12 = (f32[4,16]{1,0:T(4,128)S(1)}, f32[4,16]{1,0:T(4,128)}, u32[]{:S(2)}) copy-start(f32[4,16]{1,0:T(4,128)} %param.16) | copy-start | bytes 772
  73.4 7.1 %collective-permute-start.4 = (f32[1,1,2560]{2,1,0:T(1,128)S(1)}, f32[1,1,2560]{2,1,0:T(1,128)S(1)}, u32[]{:S(2)}, u32[]{:S(2)}) collective-permute-start(f32[1,1,2560]{2,1,0:T(1,128)S(1)} %reshape.332), channel_id=1, source_target_pairs={{0,8},{8,16},{16,24},{24,32},{32,40},{40,48},{48,56},{56,64},{64,7... | collective-permute-start | bytes 30728 | tf_op jit(solution)/shard_map/ppermute | solution.py:20
  73.5 7.0 %collective-permute-start.5 = (f32[1,1,2560]{2,1,0:T(1,128)S(1)}, f32[1,1,2560]{2,1,0:T(1,128)S(1)}, u32[]{:S(2)}, u32[]{:S(2)}) collective-permute-start(f32[1,1,2560]{2,1,0:T(1,128)S(1)} %reshape.332), channel_id=1, source_target_pairs={{8,0},{16,8},{24,16},{32,24},{40,32},{48,40},{56,48},{64,56},{72,6... | collective-permute-start | bytes 30728 | tf_op jit(solution)/shard_map/ppermute | solution.py:22
  80.6 7.9 %copy-start.6 = (f32[8,144]{1,0:T(8,128)S(1)}, f32[8,144]{1,0:T(8,128)}, u32[]{:S(2)}) copy-start(f32[8,144]{1,0:T(8,128)} %get-tuple-element.8) | copy-start | bytes 13828
  80.6 7.2 %collective-permute-start.6 = (f32[3,1,2560]{2,1,0:T(1,128)S(1)}, f32[3,1,2560]{2,1,0:T(1,128)S(1)}, u32[]{:S(2)}, u32[]{:S(2)}) collective-permute-start(f32[3,1,2560]{2,1,0:T(1,128)S(1)} %constant_dynamic-update-slice_fusion.3), channel_id=1, source_target_pairs={{0,1},{1,2},{2,3},{3,4},{4,5},{5,6},{6,7},{7,0},{8,9},{9,10},{10,1... | collective-permute-start | bytes 92168 | tf_op jit(solution)/shard_map/ppermute | solution.py:20
  80.6 7.1 %collective-permute-start.7 = (f32[3,1,2560]{2,1,0:T(1,128)S(1)}, f32[3,1,2560]{2,1,0:T(1,128)S(1)}, u32[]{:S(2)}, u32[]{:S(2)}) collective-permute-start(f32[3,1,2560]{2,1,0:T(1,128)S(1)} %constant_dynamic-update-slice_fusion.3), channel_id=1, source_target_pairs={{1,0},{2,1},{3,2},{4,3},{5,4},{6,5},{7,6},{0,7},{9,8},{10,9},{11,1... | collective-permute-start | bytes 92168 | tf_op jit(solution)/shard_map/ppermute | solution.py:22
  100.1 9.3 %copy-start.8 = (pred[16]{0:T(512)(128)(4,1)S(1)}, pred[16]{0:T(512)(128)(4,1)}, u32[]{:S(2)}) copy-start(pred[16]{0:T(512)(128)(4,1)} %get-tuple-element.62) | copy-start | bytes 52
  110.8 7.1 %collective-permute-start.8 = (f32[1,1,2560]{2,1,0:T(1,128)S(1)}, f32[1,1,2560]{2,1,0:T(1,128)S(1)}, u32[]{:S(2)}, u32[]{:S(2)}) collective-permute-start(f32[1,1,2560]{2,1,0:T(1,128)S(1)} %reshape.339), channel_id=1, source_target_pairs={{0,8},{8,16},{16,24},{24,32},{32,40},{40,48},{48,56},{56,64},{64,7... | collective-permute-start | bytes 30728 | tf_op jit(solution)/shard_map/ppermute | solution.py:20
  110.8 7.0 %collective-permute-start.9 = (f32[1,1,2560]{2,1,0:T(1,128)S(1)}, f32[1,1,2560]{2,1,0:T(1,128)S(1)}, u32[]{:S(2)}, u32[]{:S(2)}) collective-permute-start(f32[1,1,2560]{2,1,0:T(1,128)S(1)} %reshape.339), channel_id=1, source_target_pairs={{8,0},{16,8},{24,16},{32,24},{40,32},{48,40},{56,48},{64,56},{72,6... | collective-permute-start | bytes 30728 | tf_op jit(solution)/shard_map/ppermute | solution.py:22
  117.8 7.8 %copy-start.5 = (f32[8,144]{1,0:T(8,128)S(1)}, f32[8,144]{1,0:T(8,128)}, u32[]{:S(2)}) copy-start(f32[8,144]{1,0:T(8,128)} %get-tuple-element.10) | copy-start | bytes 13828
  117.9 7.1 %collective-permute-start.10 = (f32[3,1,2560]{2,1,0:T(1,128)S(1)}, f32[3,1,2560]{2,1,0:T(1,128)S(1)}, u32[]{:S(2)}, u32[]{:S(2)}) collective-permute-start(f32[3,1,2560]{2,1,0:T(1,128)S(1)} %constant_dynamic-update-slice_fusion.6), channel_id=1, source_target_pairs={{0,1},{1,2},{2,3},{3,4},{4,5},{5,6},{6,7},{7,0},{8,9},{9,10},{10,1... | collective-permute-start | bytes 92168 | tf_op jit(solution)/shard_map/ppermute | solution.py:20
  117.9 7.1 %collective-permute-start.11 = (f32[3,1,2560]{2,1,0:T(1,128)S(1)}, f32[3,1,2560]{2,1,0:T(1,128)S(1)}, u32[]{:S(2)}, u32[]{:S(2)}) collective-permute-start(f32[3,1,2560]{2,1,0:T(1,128)S(1)} %constant_dynamic-update-slice_fusion.6), channel_id=1, source_target_pairs={{1,0},{2,1},{3,2},{4,3},{5,4},{6,5},{7,6},{0,7},{9,8},{10,9},{11,1... | collective-permute-start | bytes 92168 | tf_op jit(solution)/shard_map/ppermute | solution.py:22
  137.4 9.3 %copy-start.7 = (pred[16]{0:T(512)(128)(4,1)S(1)}, pred[16]{0:T(512)(128)(4,1)}, u32[]{:S(2)}) copy-start(pred[16]{0:T(512)(128)(4,1)} %get-tuple-element.12) | copy-start | bytes 52
  148.0 7.3 %collective-permute-start.12 = (f32[1,1,2560]{2,1,0:T(1,128)S(1)}, f32[1,1,2560]{2,1,0:T(1,128)S(1)}, u32[]{:S(2)}, u32[]{:S(2)}) collective-permute-start(f32[1,1,2560]{2,1,0:T(1,128)S(1)} %reshape.346), channel_id=1, source_target_pairs={{0,8},{8,16},{16,24},{24,32},{32,40},{40,48},{48,56},{56,64},{64,7... | collective-permute-start | bytes 30728 | tf_op jit(solution)/shard_map/ppermute | solution.py:20
  148.1 7.3 %collective-permute-start.13 = (f32[1,1,2560]{2,1,0:T(1,128)S(1)}, f32[1,1,2560]{2,1,0:T(1,128)S(1)}, u32[]{:S(2)}, u32[]{:S(2)}) collective-permute-start(f32[1,1,2560]{2,1,0:T(1,128)S(1)} %reshape.346), channel_id=1, source_target_pairs={{8,0},{16,8},{24,16},{32,24},{40,32},{48,40},{56,48},{64,56},{72,6... | collective-permute-start | bytes 30728 | tf_op jit(solution)/shard_map/ppermute | solution.py:22
  155.4 7.9 %copy-start.4 = (f32[8,144]{1,0:T(8,128)S(1)}, f32[8,144]{1,0:T(8,128)}, u32[]{:S(2)}) copy-start(f32[8,144]{1,0:T(8,128)} %get-tuple-element.6) | copy-start | bytes 13828
  155.4 7.1 %collective-permute-start.14 = (f32[3,1,2560]{2,1,0:T(1,128)S(1)}, f32[3,1,2560]{2,1,0:T(1,128)S(1)}, u32[]{:S(2)}, u32[]{:S(2)}) collective-permute-start(f32[3,1,2560]{2,1,0:T(1,128)S(1)} %constant_dynamic-update-slice_fusion.9), channel_id=1, source_target_pairs={{0,1},{1,2},{2,3},{3,4},{4,5},{5,6},{6,7},{7,0},{8,9},{9,10},{10,1... | collective-permute-start | bytes 92168 | tf_op jit(solution)/shard_map/ppermute | solution.py:20
  155.4 7.1 %collective-permute-start.15 = (f32[3,1,2560]{2,1,0:T(1,128)S(1)}, f32[3,1,2560]{2,1,0:T(1,128)S(1)}, u32[]{:S(2)}, u32[]{:S(2)}) collective-permute-start(f32[3,1,2560]{2,1,0:T(1,128)S(1)} %constant_dynamic-update-slice_fusion.9), channel_id=1, source_target_pairs={{1,0},{2,1},{3,2},{4,3},{5,4},{6,5},{7,6},{0,7},{9,8},{10,9},{11,1... | collective-permute-start | bytes 92168 | tf_op jit(solution)/shard_map/ppermute | solution.py:22
where the time goes:
time: 187 us; the launch traced here: 186 us
  local copies, waits for them, and re-layouts  65.1 us (35%)
  other arithmetic  49 us (26%)
  starting transfers between devices  35.6 us (19%)
  matrix products  30.3 us (16%)
  waiting for transfers between devices  5.29 us (3%)
    ppermute x8, starting transfers between devices, with_halo(): lax.ppermute(head, axis, [((i + 1) % count, i) for i in range(count)])  33.3 us
    dot_general x4, matrix products, shards(): jnp.einsum('bnt,nbf->tbf', kalman_gain_factor, member_deviation, precisio...  23.6 us
    reduce_sum x4, other arithmetic, shards(): jnp.mean(present_sweep_value, axis=0)  19.5 us
    reshape x4, local copies, waits for them, and re-layouts, shards(): state_adjust.reshape(members, rows_here)  14.9 us
    sub x4, other arithmetic, shards(): present_sweep_value - jnp.mean(present_sweep_value, axis=0)  14.2 us
    unnamed x43, local copies, waits for them, and re-layouts  13.5 us
    gather x4, local copies, waits for them, and re-layouts, shards(): jnp.take(present_sweep_value, measured_line_locations[group_of_sets], axi...  11.4 us
    gather x4, local copies, waits for them, and re-layouts, shards(): weights = jnp.take(loc_weights[group_of_sets], indices, axis=1)  7.54 us
  transfers between devices with their start and end apart: 16, of which 5 were waited for; matrix products, arithmetic and copies ran while one was open for 21% of the time, Pallas kernels for 0%

commit v1 on v0

v1 whole, which is shorter than its diff:
```python
import jax
import jax.numpy as jnp
from jax import lax
from jax.experimental import pallas as pl
from jax.experimental.pallas import tpu as pltpu
from jax.sharding import PartitionSpec as P

BLK = 1024
BATCHES = 4
EPS = 1e-05
F32 = jnp.float32
BF16 = jnp.bfloat16
VMEM = pltpu.VMEM
SMEM = pltpu.SMEM
NT = (((1,), (1,)), ((), ()))
NN = (((1,), (0,)), ((), ()))
TN = (((0,), (0,)), ((), ()))


def split(x):
    high = x.astype(BF16)
    return high, (x - high.astype(F32)).astype(BF16)


def dot3(a, b, dims):
    ah, al = a
    bh, bl = b
    d = lambda p, q: lax.dot_general(p, q, dims, preferred_element_type=F32)
    return d(ah, bh) + (d(ah, bl) + d(al, bh))


def column(row, slots):
    i = lax.broadcasted_iota(jnp.int32, (slots, slots), 0)
    j = lax.broadcasted_iota(jnp.int32, (slots, slots), 1)
    return jnp.sum(jnp.where(i == j, row, jnp.zeros_like(row)), axis=1, keepdims=True)


def message(measured, values, error, count):
    slots, members = measured.shape
    mean = jnp.sum(measured, axis=1, keepdims=True) / members
    anomaly = measured - mean
    var = jnp.sum(anomaly * anomaly, axis=1, keepdims=True) / (members - 1) + EPS
    error = column(error, slots)
    values = column(values, slots)
    increment = (
        var / (var + error) * (values - mean) + (jnp.sqrt(error / (var + error)) - 1.0) * anomaly
    )
    live = (lax.broadcasted_iota(jnp.int32, (slots, 1), 0) < count).astype(F32)
    scaled = anomaly * (live / ((members - 1) * var))
    scaled = scaled - jnp.sum(scaled, axis=1, keepdims=True) / members
    return scaled, increment


def gather_kernel(loc, count, ens, values, error, measured, msg):
    members = ens.shape[0]
    batches, slots = loc.shape
    lane = lax.broadcasted_iota(jnp.int32, (members, 128), 1)
    acc = jnp.zeros((members, 128), F32)
    for j in range(batches * slots):
        c = loc[j // slots, j % slots]
        tile = ens[:, pl.ds(pl.multiple_of((c // 128) * 128, 128), 128)]
        acc = jnp.where(lane == j, pltpu.roll(tile, (j - c % 128 + 128) % 128, 1), acc)
    rows = jnp.transpose(acc)[: batches * slots]
    measured[...] = rows
    scaled, increment = message(rows[:slots], values[0:1, :], error[0:1, :], count[0, 0])
    msg[:slots] = scaled
    msg[slots:] = increment


def coef_kernel(loc, place, blocks, weights, coef, col_coef):
    batches, slots = loc.shape
    nb = coef.shape[1]
    lane = lax.broadcasted_iota(jnp.int32, (nb, 128), 1)
    row = lax.broadcasted_iota(jnp.int32, (nb, 128), 0)
    first = place[3] * nb
    north = place[4]
    span = 3 * slots
    for b in range(batches):
        lo = jnp.zeros((nb, 128), F32)
        hi = jnp.zeros((nb, 128), F32)
        for a in range(3):
            at = pl.ds(pl.multiple_of(place[a] * 128, 128), 128)
            bl = blocks[b, :, at] - first
            w = weights[b, :, at]
            tile = jnp.zeros((nb, 128), F32)
            for s in range(nb):
                one = jnp.sum(jnp.where(bl == s, w, 0.0), axis=0, keepdims=True)
                tile = jnp.where(row == s, one, tile)
            tile = pltpu.roll(tile, (a * span - (north - 1) * slots + 256) % 128, 1)
            keep = (lane >= a * span) & (lane < (a + 1) * span)
            lo = jnp.where(keep, tile, lo)
            over = (a + 1) * span - 128
            if over > 0:
                hi = jnp.where(lane < over, tile, hi)
        coef[b, :, 0:128] = lo
        coef[b, :, 128:256] = hi
    for b in range(batches - 1):
        for r in range((b + 1) * slots, batches * slots):
            s = loc[r // slots, r % slots] // BLK
            col_coef[b, r : r + 1, :] = coef[b, pl.ds(s, 1), :]


def near(groups, slots):
    scaled = [g[k * 2 * slots : k * 2 * slots + slots] for g in groups for k in range(3)]
    increment = [g[k * 2 * slots + slots : (k + 1) * 2 * slots] for g in groups for k in range(3)]
    return split(jnp.concatenate(scaled, axis=0)), split(jnp.concatenate(increment, axis=0))


def step_kernel(batch, count, west, here, east, measured, col_coef, values, error, out, msg):
    slots = values.shape[1]
    scaled, increment = near((west[...], here[...], east[...]), slots)
    nobs = scaled[0].shape[0]
    begin = (batch + 1) * slots
    rows = measured[begin:]
    s = dot3(split(rows), scaled, NT)
    p = s * col_coef[batch, begin:, :nobs]
    rows = rows + dot3(split(p), increment, NN)
    out[begin:] = rows
    b = batch + 1
    scaled, increment = message(rows[:slots], values[b : b + 1, :], error[b : b + 1, :], count[b, 0])
    msg[:slots] = scaled
    msg[slots:] = increment


def map_kernel(batch, slots, west, here, east, coef, maps, out):
    nb = coef.shape[1]
    members = west.shape[1]
    scaled, increment = near((west[...], here[...], east[...]), slots)
    nobs = scaled[0].shape[0]
    i = lax.broadcasted_iota(jnp.int32, (members, members), 0)
    j = lax.broadcasted_iota(jnp.int32, (members, members), 1)
    for k in range(nb):
        e = jnp.where(i == j, 1.0, 0.0) if maps is None else maps[k]
        s = dot3(split(e), scaled, NT)
        p = s * coef[batch, k : k + 1, :nobs]
        out[k] = e + dot3(split(p), increment, NN)


def final_kernel(batch, slots, west, here, east, coef, maps, ens, out):
    members = west.shape[1]
    scaled, increment = near((west[...], here[...], east[...]), slots)
    nobs = scaled[0].shape[0]
    i = lax.broadcasted_iota(jnp.int32, (members, members), 0)
    j = lax.broadcasted_iota(jnp.int32, (members, members), 1)
    e = maps[0]
    s = dot3(split(e), scaled, NT)
    p = s * coef[batch, pl.ds(pl.program_id(0), 1), :nobs]
    d = e - jnp.where(i == j, 1.0, 0.0) + dot3(split(p), increment, NN)
    dh, dl = split(d)
    x = ens[...]
    xh, xl = split(x)
    left = jnp.concatenate([dh, dl, dh], axis=0)
    right = jnp.concatenate([xh, xh, xl], axis=0)
    out[...] = x + lax.dot_general(left, right, TN, preferred_element_type=F32)


def shift(x, axis, step):
    n = lax.axis_size(axis)
    return lax.ppermute(x, axis, [(i, (i + step) % n) for i in range(n)])


def shards(ensemble, loc, values, error, count, blocks, weights):
    members, rows_here = ensemble.shape
    batches, slots = loc.shape
    nb = rows_here // BLK
    nx, ny = lax.axis_size("gx"), lax.axis_size("gy")
    ix, iy = lax.axis_index("gx"), lax.axis_index("gy")
    vm = pl.BlockSpec(memory_space=VMEM)
    sm = pl.BlockSpec(memory_space=SMEM)
    params = pltpu.CompilerParams(vmem_limit_bytes=32 * 1024 * 1024)
    shape = lambda *s: jax.ShapeDtypeStruct(s, F32)
    nrows = batches * slots

    measured, msg = pl.pallas_call(
        gather_kernel,
        out_shape=(shape(nrows, members), shape(2 * slots, members)),
        in_specs=[sm, sm, vm, vm, vm],
        out_specs=(vm, vm),
        compiler_params=params,
        name="gather_columns",
    )(loc, count, ensemble, values, error)

    place = jnp.stack([(ix + nx - 1) % nx, ix, (ix + 1) % nx, ix * ny + iy, iy]).astype(jnp.int32)
    coef, col_coef = pl.pallas_call(
        coef_kernel,
        out_shape=(shape(batches, nb, 256), shape(batches - 1, nrows, 256)),
        in_specs=[sm, sm, vm, vm],
        out_specs=(vm, vm),
        compiler_params=params,
        name="list_coefficients",
    )(loc, place, blocks, weights)

    maps = None
    for b in range(batches):
        south, north = shift(msg, "gy", 1), shift(msg, "gy", -1)
        line = jnp.concatenate([south, msg, north], axis=0)
        halo = (shift(line, "gx", 1), line, shift(line, "gx", -1))
        if b < batches - 1:
            measured, msg = pl.pallas_call(
                lambda *refs, b=b: step_kernel(b, *refs),
                out_shape=(shape(nrows, members), shape(2 * slots, members)),
                in_specs=[sm] + [vm] * 7,
                out_specs=(vm, vm),
                compiler_params=params,
                name="step_columns",
            )(count, *halo, measured, col_coef, values, error)
            given = () if maps is None else (maps,)
            body = (
                (lambda w, h, e, c, o, b=b: map_kernel(b, slots, w, h, e, c, None, o))
                if maps is None
                else (lambda w, h, e, c, m, o, b=b: map_kernel(b, slots, w, h, e, c, m, o))
            )
            maps = pl.pallas_call(
                body,
                out_shape=shape(nb, members, members),
                in_specs=[vm] * (4 + len(given)),
                out_specs=vm,
                compiler_params=params,
                cost_estimate=pl.CostEstimate(flops=10**9, bytes_accessed=10**6, transcendentals=0),
                name="compose_maps",
            )(*halo, coef, *given)
        else:
            posterior = pl.pallas_call(
                lambda *refs, b=b: final_kernel(b, slots, *refs),
                out_shape=shape(members, rows_here),
                grid=(nb,),
                in_specs=[vm] * 4
                + [
                    pl.BlockSpec((1, members, members), lambda k: (k, 0, 0)),
                    pl.BlockSpec((members, BLK), lambda k: (0, k)),
                ],
                out_specs=pl.BlockSpec((members, BLK), lambda k: (0, k)),
                compiler_params=params,
                name="apply_maps",
            )(*halo, coef, maps, ensemble)
    return posterior


def solution(mesh):
    split_specs = P(None, ("gx", "gy"))
    in_specs = (split_specs,) * 5 + (P(), P())
    return jax.shard_map(
        shards, mesh=mesh, in_specs=in_specs, out_specs=split_specs, check_vma=False
    )
```

time: 187 us -> 73.3 us (0.39)
  local copies, waits for them, and re-layouts: 65.1 us -> 4.67 us
  other arithmetic: 49 us -> 0 us
  matrix products: 30.3 us -> 0 us
  waiting for transfers between devices: 5.29 us -> 25.3 us
  Pallas kernels: 0 us -> 18.4 us
  starting transfers between devices: 35.6 us -> 24.7 us
    dot_general x8 -> x0, matrix products: 30.3 us -> none  [the longest x4 23.6 us: shards(): jnp.einsum('bnt,nbf->tbf', kalman_gain_factor, member_deviation, precisio...]
    gather x12 -> x0, local copies, waits for them, and re-layouts: 24.1 us -> none  [the longest x4 11.4 us: shards(): jnp.take(present_sweep_value, measured_line_locations[group_of_sets], axi...]
    reduce_sum x13 -> x0, other arithmetic: 21.7 us -> none  [the longest x4 19.5 us: shards(): jnp.mean(present_sweep_value, axis=0)]
    ppermute x16, waiting for transfers between devices: 5.29 us -> 25.3 us  [shift(): return lax.ppermute(x, axis, [(i, (i + step) % n) for i in range(n)])]
    pallas_call x0 -> x9, Pallas kernels: none -> 18.4 us  [the longest x1 6.47 us: shards(): pl.pallas_call(lambda *refs, b=b: final_kernel(b, slots, *refs), out_shap...]
    reshape x12 -> x0, local copies, waits for them, and re-layouts: 16.3 us -> none  [the longest x4 14.9 us: shards(): state_adjust.reshape(members, rows_here)]
    sub x4 -> x0, other arithmetic: 14.2 us -> none  [shards(): present_sweep_value - jnp.mean(present_sweep_value, axis=0)]
    ppermute x16, starting transfers between devices: 35.6 us -> 24.7 us  [shift(): return lax.ppermute(x, axis, [(i, (i + step) % n) for i in range(n)])]
  transfers between devices with their start and end apart: 16 -> 16, of which waited for: 5 -> 11; matrix products, arithmetic and copies ran while one was open for 21% -> 0% of each run, Pallas kernels for 0% -> 9%
where the time goes in v1:
time: 73.3 us; the launch traced here: 73.1 us
  waiting for transfers between devices  25.3 us (35%)
  starting transfers between devices  24.7 us (34%)
  Pallas kernels  18.4 us (25%)
  local copies, waits for them, and re-layouts  4.67 us (6%)
    ppermute x16, waiting for transfers between devices, shift(): return lax.ppermute(x, axis, [(i, (i + step) % n) for i in range(n)])  25.3 us
    ppermute x16, starting transfers between devices, shift(): return lax.ppermute(x, axis, [(i, (i + step) % n) for i in range(n)])  24.7 us
    pallas_call x1, Pallas kernels, shards(): pl.pallas_call(lambda *refs, b=b: final_kernel(b, slots, *refs), out_shap...  6.47 us
    pallas_call x3, Pallas kernels, shards(): pl.pallas_call(body, out_shape=shape(nb, members, members), in_specs=[vm]...  5.18 us
    unnamed x29, local copies, waits for them, and re-layouts  4.58 us
    pallas_call x3, Pallas kernels, shards(): pl.pallas_call(lambda *refs, b=b: step_kernel(b, *refs), out_shape=(shape...  3.84 us
    pallas_call x1, Pallas kernels, shards(): pl.pallas_call(gather_kernel, out_shape=(shape(nrows, members), shape(2 *...  1.73 us
  transfers between devices with their start and end apart: 16, of which 11 were waited for; matrix products, arithmetic and copies ran while one was open for 0% of the time, Pallas kernels for 9%

profile of v1, /device:TPU:0, one launch (start us, length us, event | category | flops | bytes accessed | tf_op | source)
XLA Modules:
  0.0 73.1 jit_solution(3517386084114217014)
XLA Ops:
  0.0 0.8 %copy.11.count.refs_0_ = s32[4,1]{1,0:T(4,128)S(1)} copy(s32[4,1]{0,1:T(1,128)} %param.11) | data formatting | bytes 32 | tf_op args[4]
  0.8 1.7 %copy-done = f32[80,8192]{1,0:T(8,128)S(1)} copy-done((f32[80,8192]{1,0:T(8,128)S(1)}, f32[80,8192]{1,0:T(8,128)}, u32[]{:S(2)}) %copy-start) | copy-done | bytes 2621464
  2.5 0.7 copy-done.4
  3.2 0.7 copy-done.6
  3.9 0.7 copy-done.8
  4.6 1.7 %gather_columns.1 = (f32[64,80]{1,0:T(8,128)S(1)}, f32[32,80]{1,0:T(8,128)S(1)}) custom-call(s32[4,16]{1,0:T(4,128)S(1)} %copy-done.8, s32[4,1]{1,0:T(4,128)S(1)} %copy.11.count.refs_0_, f32[80,8192]{1,0:T(8,128)S(1)} %copy-done, f32[4,16]{1,0:T(4,128)S(1)} %copy-done.4, f32[4,16]{1,0:T(4,128)S(1)} %copy-done.6), custom_call_target="tpu_custom_call" | custom-call | tf_op jit(solution)/shard_map/gather_columns/pallas_call | solution.py:174
  6.3 0.0 collective-permute-start
  6.3 3.0 %collective-permute-start.1 = (f32[32,80]{1,0:T(8,128)S(1)}, f32[32,80]{1,0:T(8,128)S(1)}, u32[]{:S(2)}, u32[]{:S(2)}) collective-permute-start(f32[32,80]{1,0:T(8,128)S(1)} %get-tuple-element.14), channel_id=1, source_target_pairs={{0,7},{1,0},{2,1},{3,2},{4,3},{5,4},{6,5},{7,6},{8,15},{9,8},{10,9... | collective-permute-start | bytes 30728 | tf_op jit(solution)/shard_map/ppermute | solution.py:159
  9.3 1.4 %collective-permute-done = f32[32,80]{1,0:T(8,128)S(1)} collective-permute-done((f32[32,80]{1,0:T(8,128)S(1)}, f32[32,80]{1,0:T(8,128)S(1)}, u32[]{:S(2)}, u32[]{:S(2)}) %collective-permute-start) | collective-permute-done | bytes 10272 | tf_op jit(solution)/shard_map/ppermute | solution.py:159
  10.7 0.0 collective-permute-done.1
  10.7 6.6 %collective-permute-start.3 = (f32[96,80]{1,0:T(8,128)S(1)}, f32[96,80]{1,0:T(8,128)S(1)}, u32[]{:S(2)}, u32[]{:S(2)}) collective-permute-start(f32[96,80]{1,0:T(8,128)S(1)} %constant_dynamic-update-slice_fusion.refs_2_.h), channel_id=1, source_target_pairs={{0,120},{8,0},{16,8},{24,16},{32,24},{40,32},{48,40},{56,48},{64,5... | collective-permute-start | bytes 92168 | tf_op jit(solution)/shard_map/ppermute | solution.py:159
  17.3 0.0 collective-permute-start.2
  17.3 0.1 stack.23.place
  17.4 1.2 %list_coefficients.1 = (f32[4,8,256]{2,1,0:T(8,128)S(1)}, f32[3,64,256]{2,1,0:T(8,128)S(1)}) custom-call(s32[4,16]{1,0:T(4,128)S(1)} %copy-done.9, s32[5]{0:T(128)S(1)} %stack.23.place, s32[4,8,2048]{2,1,0:T(8,128)S(1)} %copy-done.2, f32[4,8,2048]{2,1,0:T(8,128)S(1)} %copy-done.3), custom_call_target="tpu_custom_call" | custom-call | tf_op jit(solution)/shard_map/list_coefficients/pallas_call | solution.py:184
  18.6 0.5 collective-permute-done.3.refs_3_.e
  19.1 5.7 %collective-permute-done.2.refs_1_.w = f32[96,80]{1,0:T(8,128)S(1)} collective-permute-done((f32[96,80]{1,0:T(8,128)S(1)}, f32[96,80]{1,0:T(8,128)S(1)}, u32[]{:S(2)}, u32[]{:S(2)}) %collective-permute-start.2) | collective-permute-done | bytes 30752 | tf_op jit(solution)/shard_map/ppermute | solution.py:159
  24.7 1.2 %step_columns.3 = (f32[64,80]{1,0:T(8,128)S(1)}, f32[32,80]{1,0:T(8,128)S(1)}) custom-call(s32[4,1]{1,0:T(4,128)S(1)} %copy.11.count.refs_0_, f32[96,80]{1,0:T(8,128)S(1)} %collective-permute-done.2.refs_1_.w, f32[96,80]{1,0:T(8,128)S(1)} %constant_dynamic-update-slice_fusion.refs_2_.h, f32[96,80]{1,0:T(8,128)S(1)} %collective-permute-done.3.refs_3_.e, ...), custom_call_target="tpu_custom_call" | custom-call | tf_op jit(solution)/shard_map/step_columns/pallas_call | solution.py:199
  25.9 0.0 collective-permute-start.4
  25.9 3.0 %collective-permute-start.5 = (f32[32,80]{1,0:T(8,128)S(1)}, f32[32,80]{1,0:T(8,128)S(1)}, u32[]{:S(2)}, u32[]{:S(2)}) collective-permute-start(f32[32,80]{1,0:T(8,128)S(1)} %get-tuple-element.17), channel_id=1, source_target_pairs={{0,7},{1,0},{2,1},{3,2},{4,3},{5,4},{6,5},{7,6},{8,15},{9,8},{10,9... | collective-permute-start | bytes 30728 | tf_op jit(solution)/shard_map/ppermute | solution.py:159
  28.9 1.4 %collective-permute-done.4 = f32[32,80]{1,0:T(8,128)S(1)} collective-permute-done((f32[32,80]{1,0:T(8,128)S(1)}, f32[32,80]{1,0:T(8,128)S(1)}, u32[]{:S(2)}, u32[]{:S(2)}) %collective-permute-start.4) | collective-permute-done | bytes 10272 | tf_op jit(solution)/shard_map/ppermute | solution.py:159
  30.3 0.0 collective-permute-done.5
  30.3 0.1 collective-permute-start.7
  30.4 2.0 %collective-permute-start.6 = (f32[96,80]{1,0:T(8,128)S(1)}, f32[96,80]{1,0:T(8,128)S(1)}, u32[]{:S(2)}, u32[]{:S(2)}) collective-permute-start(f32[96,80]{1,0:T(8,128)S(1)} %constant_dynamic-update-slice_fusion.3.refs_2_.h), channel_id=1, source_target_pairs={{0,8},{8,16},{16,24},{24,32},{32,40},{40,48},{48,56},{56,64},{64,7... | collective-permute-start | bytes 92168 | tf_op jit(solution)/shard_map/ppermute | solution.py:159
  32.4 2.1 %collective-permute-done.7.refs_3_.e = f32[96,80]{1,0:T(8,128)S(1)} collective-permute-done((f32[96,80]{1,0:T(8,128)S(1)}, f32[96,80]{1,0:T(8,128)S(1)}, u32[]{:S(2)}, u32[]{:S(2)}) %collective-permute-start.7) | collective-permute-done | bytes 30752 | tf_op jit(solution)/shard_map/ppermute | solution.py:159
  34.5 3.4 %collective-permute-done.6.refs_1_.w = f32[96,80]{1,0:T(8,128)S(1)} collective-permute-done((f32[96,80]{1,0:T(8,128)S(1)}, f32[96,80]{1,0:T(8,128)S(1)}, u32[]{:S(2)}, u32[]{:S(2)}) %collective-permute-start.6) | collective-permute-done | bytes 30752 | tf_op jit(solution)/shard_map/ppermute | solution.py:159
  37.9 1.1 %step_columns.4 = (f32[64,80]{1,0:T(8,128)S(1)}, f32[32,80]{1,0:T(8,128)S(1)}) custom-call(s32[4,1]{1,0:T(4,128)S(1)} %copy.11.count.refs_0_, f32[96,80]{1,0:T(8,128)S(1)} %collective-permute-done.6.refs_1_.w, f32[96,80]{1,0:T(8,128)S(1)} %constant_dynamic-update-slice_fusion.3.refs_2_.h, f32[96,80]{1,0:T(8,128)S(1)} %collective-permute-done.7.refs_3_.e, ...), custom_call_target="tpu_custom_call" | custom-call | tf_op jit(solution)/shard_map/step_columns/pallas_call | solution.py:199
  39.0 0.0 collective-permute-start.8
  39.0 3.0 %collective-permute-start.9 = (f32[32,80]{1,0:T(8,128)S(1)}, f32[32,80]{1,0:T(8,128)S(1)}, u32[]{:S(2)}, u32[]{:S(2)}) collective-permute-start(f32[32,80]{1,0:T(8,128)S(1)} %get-tuple-element.19), channel_id=1, source_target_pairs={{0,7},{1,0},{2,1},{3,2},{4,3},{5,4},{6,5},{7,6},{8,15},{9,8},{10,9... | collective-permute-start | bytes 30728 | tf_op jit(solution)/shard_map/ppermute | solution.py:159
  42.0 1.4 %collective-permute-done.8 = f32[32,80]{1,0:T(8,128)S(1)} collective-permute-done((f32[32,80]{1,0:T(8,128)S(1)}, f32[32,80]{1,0:T(8,128)S(1)}, u32[]{:S(2)}, u32[]{:S(2)}) %collective-permute-start.8) | collective-permute-done | bytes 10272 | tf_op jit(solution)/shard_map/ppermute | solution.py:159
  43.4 0.0 collective-permute-done.9
  43.4 0.1 collective-permute-start.11
  43.5 2.0 %collective-permute-start.10 = (f32[96,80]{1,0:T(8,128)S(1)}, f32[96,80]{1,0:T(8,128)S(1)}, u32[]{:S(2)}, u32[]{:S(2)}) collective-permute-start(f32[96,80]{1,0:T(8,128)S(1)} %constant_dynamic-update-slice_fusion.6.refs_2_.h), channel_id=1, source_target_pairs={{0,8},{8,16},{16,24},{24,32},{32,40},{40,48},{48,56},{56,64},{64,7... | collective-permute-start | bytes 92168 | tf_op jit(solution)/shard_map/ppermute | solution.py:159
  45.5 0.7 compose_maps.3.m
  46.2 1.4 %collective-permute-done.11.refs_3_.e = f32[96,80]{1,0:T(8,128)S(1)} collective-permute-done((f32[96,80]{1,0:T(8,128)S(1)}, f32[96,80]{1,0:T(8,128)S(1)}, u32[]{:S(2)}, u32[]{:S(2)}) %collective-permute-start.11) | collective-permute-done | bytes 30752 | tf_op jit(solution)/shard_map/ppermute | solution.py:159
  47.6 3.4 %collective-permute-done.10.refs_1_.w = f32[96,80]{1,0:T(8,128)S(1)} collective-permute-done((f32[96,80]{1,0:T(8,128)S(1)}, f32[96,80]{1,0:T(8,128)S(1)}, u32[]{:S(2)}, u32[]{:S(2)}) %collective-permute-start.10) | collective-permute-done | bytes 30752 | tf_op jit(solution)/shard_map/ppermute | solution.py:159
  51.0 1.5 %step_columns.5 = (f32[64,80]{1,0:T(8,128)}, f32[32,80]{1,0:T(8,128)S(1)}) custom-call(s32[4,1]{1,0:T(4,128)S(1)} %copy.11.count.refs_0_, f32[96,80]{1,0:T(8,128)S(1)} %collective-permute-done.10.refs_1_.w, f32[96,80]{1,0:T(8,128)S(1)} %constant_dynamic-update-slice_fusion.6.refs_2_.h, f32[96,80]{1,0:T(8,128)S(1)} %collective-permute-done.11.refs_3_.e, ...), custom_call_target="tpu_custom_call" | custom-call | tf_op jit(solution)/shard_map/step_columns/pallas_call | solution.py:199
  52.5 0.0 collective-permute-start.12
  52.5 2.2 %compose_maps.4.m = f32[8,80,80]{2,1,0:T(8,128)S(1)} custom-call(f32[96,80]{1,0:T(8,128)S(1)} %collective-permute-done.6.refs_1_.w, f32[96,80]{1,0:T(8,128)S(1)} %constant_dynamic-update-slice_fusion.3.refs_2_.h, f32[96,80]{1,0:T(8,128)S(1)} %collective-permute-done.7.refs_3_.e, f32[4,8,256]{2,1,0:T(8,128)S(1)} %get-tuple-element.22.c.refs_3_, ...), custom_call_target="tpu_custom_call" | custom-call | flops 1000000000 | bytes 1000000 | tf_op jit(solution)/shard_map/compose_maps/pallas_call | solution.py:213
  54.8 0.0 copy-start.1
  54.8 3.0 %collective-permute-start.13 = (f32[32,80]{1,0:T(8,128)S(1)}, f32[32,80]{1,0:T(8,128)S(1)}, u32[]{:S(2)}, u32[]{:S(2)}) collective-permute-start(f32[32,80]{1,0:T(8,128)S(1)} %get-tuple-element.21), channel_id=1, source_target_pairs={{0,7},{1,0},{2,1},{3,2},{4,3},{5,4},{6,5},{7,6},{8,15},{9,8},{10,9... | collective-permute-start | bytes 30728 | tf_op jit(solution)/shard_map/ppermute | solution.py:159
  57.8 0.0 collective-permute-done.12
  57.8 1.4 %collective-permute-done.13 = f32[32,80]{1,0:T(8,128)S(1)} collective-permute-done((f32[32,80]{1,0:T(8,128)S(1)}, f32[32,80]{1,0:T(8,128)S(1)}, u32[]{:S(2)}, u32[]{:S(2)}) %collective-permute-start.13) | collective-permute-done | bytes 10272 | tf_op jit(solution)/shard_map/ppermute | solution.py:159
  59.2 0.0 collective-permute-start.15
  59.2 2.0 %collective-permute-start.14 = (f32[96,80]{1,0:T(8,128)S(1)}, f32[96,80]{1,0:T(8,128)S(1)}, u32[]{:S(2)}, u32[]{:S(2)}) collective-permute-start(f32[96,80]{1,0:T(8,128)S(1)} %constant_dynamic-update-slice_fusion.9.refs_1_), channel_id=1, source_target_pairs={{0,8},{8,16},{16,24},{24,32},{32,40},{40,48},{48,56},{56,64},{64,7... | collective-permute-start | bytes 92168 | tf_op jit(solution)/shard_map/ppermute | solution.py:159
  61.2 2.2 %compose_maps.5.refs_4_ = f32[8,80,80]{2,1,0:T(8,128)S(1)} custom-call(f32[96,80]{1,0:T(8,128)S(1)} %collective-permute-done.10.refs_1_.w, f32[96,80]{1,0:T(8,128)S(1)} %constant_dynamic-update-slice_fusion.6.refs_2_.h, f32[96,80]{1,0:T(8,128)S(1)} %collective-permute-done.11.refs_3_.e, f32[4,8,256]{2,1,0:T(8,128)S(1)} %get-tuple-element.22.c.refs_3_, ...), custom_call_target="tpu_custom_call" | custom-call | flops 1000000000 | bytes 1000000 | tf_op jit(solution)/shard_map/compose_maps/pallas_call | solution.py:213
  63.5 0.0 collective-permute-done.15.refs_2_
  63.5 3.1 %collective-permute-done.14.refs_0_ = f32[96,80]{1,0:T(8,128)S(1)} collective-permute-done((f32[96,80]{1,0:T(8,128)S(1)}, f32[96,80]{1,0:T(8,128)S(1)}, u32[]{:S(2)}, u32[]{:S(2)}) %collective-permute-start.14) | collective-permute-done | bytes 30752 | tf_op jit(solution)/shard_map/ppermute | solution.py:159
  66.6 6.5 %apply_maps.1 = f32[80,8192]{1,0:T(8,128)} custom-call(f32[96,80]{1,0:T(8,128)S(1)} %collective-permute-done.14.refs_0_, f32[96,80]{1,0:T(8,128)S(1)} %constant_dynamic-update-slice_fusion.9.refs_1_, f32[96,80]{1,0:T(8,128)S(1)} %collective-permute-done.15.refs_2_, f32[4,8,256]{2,1,0:T(8,128)S(1)} %get-tuple-element.22.c.refs_3_, ...), custom_call_target="tpu_custom_call" | custom-call | tf_op jit(solution)/shard_map/apply_maps/pallas_call | solution.py:223
  (27 shorter events, 0.1 us)
Async XLA Ops:
  0.0 24.7 %copy-start.5 = (f32[4,16]{1,0:T(4,128)S(1)}, f32[4,16]{1,0:T(4,128)}, u32[]{:S(2)}) copy-start(f32[4,16]{1,0:T(4,128)} %refs_6_.5) | copy-start | bytes 772
  0.8 1.7 %copy-start = (f32[80,8192]{1,0:T(8,128)S(1)}, f32[80,8192]{1,0:T(8,128)}, u32[]{:S(2)}) copy-start(f32[80,8192]{1,0:T(8,128)} %refs_5_.1) | copy-start | bytes 7864324
  2.5 0.7 copy-start.4
  3.2 0.7 copy-start.6
  3.9 0.7 copy-start.8
  4.5 12.9 %copy-start.2 = (s32[4,8,2048]{2,1,0:T(8,128)S(1)}, s32[4,8,2048]{2,1,0:T(8,128)}, u32[]{:S(2)}) copy-start(s32[4,8,2048]{2,1,0:T(8,128)} %blocks.1) | copy-start | bytes 786436
  4.5 12.9 %copy-start.3 = (f32[4,8,2048]{2,1,0:T(8,128)S(1)}, f32[4,8,2048]{2,1,0:T(8,128)}, u32[]{:S(2)}) copy-start(f32[4,8,2048]{2,1,0:T(8,128)} %weights.1) | copy-start | bytes 786436
  4.5 12.9 %copy-start.9 = (s32[4,16]{1,0:T(4,128)S(1)}, s32[4,16]{1,0:T(4,128)}, u32[]{:S(2)}) copy-start(s32[4,16]{1,0:T(4,128)} %loc.3) | copy-start | bytes 772
  4.6 20.2 %copy-start.7 = (f32[4,16]{1,0:T(4,128)S(1)}, f32[4,16]{1,0:T(4,128)}, u32[]{:S(2)}) copy-start(f32[4,16]{1,0:T(4,128)} %refs_7_.5) | copy-start | bytes 772
  6.3 4.4 %collective-permute-start = (f32[32,80]{1,0:T(8,128)S(1)}, f32[32,80]{1,0:T(8,128)S(1)}, u32[]{:S(2)}, u32[]{:S(2)}) collective-permute-start(f32[32,80]{1,0:T(8,128)S(1)} %get-tuple-element.14), channel_id=1, source_target_pairs={{0,1},{1,2},{2,3},{3,4},{4,5},{5,6},{6,7},{7,0},{8,9},{9,10},{10,1... | collective-permute-start | bytes 30728 | tf_op jit(solution)/shard_map/ppermute | solution.py:159
  6.3 4.4 %collective-permute-start.1 = (f32[32,80]{1,0:T(8,128)S(1)}, f32[32,80]{1,0:T(8,128)S(1)}, u32[]{:S(2)}, u32[]{:S(2)}) collective-permute-start(f32[32,80]{1,0:T(8,128)S(1)} %get-tuple-element.14), channel_id=1, source_target_pairs={{0,7},{1,0},{2,1},{3,2},{4,3},{5,4},{6,5},{7,6},{8,15},{9,8},{10,9... | collective-permute-start | bytes 30728 | tf_op jit(solution)/shard_map/ppermute | solution.py:159
  10.7 8.4 %collective-permute-start.3 = (f32[96,80]{1,0:T(8,128)S(1)}, f32[96,80]{1,0:T(8,128)S(1)}, u32[]{:S(2)}, u32[]{:S(2)}) collective-permute-start(f32[96,80]{1,0:T(8,128)S(1)} %constant_dynamic-update-slice_fusion.refs_2_.h), channel_id=1, source_target_pairs={{0,120},{8,0},{16,8},{24,16},{32,24},{40,32},{48,40},{56,48},{64,5... | collective-permute-start | bytes 92168 | tf_op jit(solution)/shard_map/ppermute | solution.py:159
  17.3 7.4 %collective-permute-start.2 = (f32[96,80]{1,0:T(8,128)S(1)}, f32[96,80]{1,0:T(8,128)S(1)}, u32[]{:S(2)}, u32[]{:S(2)}) collective-permute-start(f32[96,80]{1,0:T(8,128)S(1)} %constant_dynamic-update-slice_fusion.refs_2_.h), channel_id=1, source_target_pairs={{0,8},{8,16},{16,24},{24,32},{32,40},{40,48},{48,56},{56,64},{64,7... | collective-permute-start | bytes 92168 | tf_op jit(solution)/shard_map/ppermute | solution.py:159
  25.9 4.4 %collective-permute-start.4 = (f32[32,80]{1,0:T(8,128)S(1)}, f32[32,80]{1,0:T(8,128)S(1)}, u32[]{:S(2)}, u32[]{:S(2)}) collective-permute-start(f32[32,80]{1,0:T(8,128)S(1)} %get-tuple-element.17), channel_id=1, source_target_pairs={{0,1},{1,2},{2,3},{3,4},{4,5},{5,6},{6,7},{7,0},{8,9},{9,10},{10,1... | collective-permute-start | bytes 30728 | tf_op jit(solution)/shard_map/ppermute | solution.py:159
  25.9 4.4 %collective-permute-start.5 = (f32[32,80]{1,0:T(8,128)S(1)}, f32[32,80]{1,0:T(8,128)S(1)}, u32[]{:S(2)}, u32[]{:S(2)}) collective-permute-start(f32[32,80]{1,0:T(8,128)S(1)} %get-tuple-element.17), channel_id=1, source_target_pairs={{0,7},{1,0},{2,1},{3,2},{4,3},{5,4},{6,5},{7,6},{8,15},{9,8},{10,9... | collective-permute-start | bytes 30728 | tf_op jit(solution)/shard_map/ppermute | solution.py:159
  30.3 4.2 %collective-permute-start.7 = (f32[96,80]{1,0:T(8,128)S(1)}, f32[96,80]{1,0:T(8,128)S(1)}, u32[]{:S(2)}, u32[]{:S(2)}) collective-permute-start(f32[96,80]{1,0:T(8,128)S(1)} %constant_dynamic-update-slice_fusion.3.refs_2_.h), channel_id=1, source_target_pairs={{0,120},{8,0},{16,8},{24,16},{32,24},{40,32},{48,40},{56,48},{64,5... | collective-permute-start | bytes 92168 | tf_op jit(solution)/shard_map/ppermute | solution.py:159
  30.4 7.5 %collective-permute-start.6 = (f32[96,80]{1,0:T(8,128)S(1)}, f32[96,80]{1,0:T(8,128)S(1)}, u32[]{:S(2)}, u32[]{:S(2)}) collective-permute-start(f32[96,80]{1,0:T(8,128)S(1)} %constant_dynamic-update-slice_fusion.3.refs_2_.h), channel_id=1, source_target_pairs={{0,8},{8,16},{16,24},{24,32},{32,40},{40,48},{48,56},{56,64},{64,7... | collective-permute-start | bytes 92168 | tf_op jit(solution)/shard_map/ppermute | solution.py:159
  39.0 4.4 %collective-permute-start.8 = (f32[32,80]{1,0:T(8,128)S(1)}, f32[32,80]{1,0:T(8,128)S(1)}, u32[]{:S(2)}, u32[]{:S(2)}) collective-permute-start(f32[32,80]{1,0:T(8,128)S(1)} %get-tuple-element.19), channel_id=1, source_target_pairs={{0,1},{1,2},{2,3},{3,4},{4,5},{5,6},{6,7},{7,0},{8,9},{9,10},{10,1... | collective-permute-start | bytes 30728 | tf_op jit(solution)/shard_map/ppermute | solution.py:159
  39.0 4.4 %collective-permute-start.9 = (f32[32,80]{1,0:T(8,128)S(1)}, f32[32,80]{1,0:T(8,128)S(1)}, u32[]{:S(2)}, u32[]{:S(2)}) collective-permute-start(f32[32,80]{1,0:T(8,128)S(1)} %get-tuple-element.19), channel_id=1, source_target_pairs={{0,7},{1,0},{2,1},{3,2},{4,3},{5,4},{6,5},{7,6},{8,15},{9,8},{10,9... | collective-permute-start | bytes 30728 | tf_op jit(solution)/shard_map/ppermute | solution.py:159
  43.4 4.2 %collective-permute-start.11 = (f32[96,80]{1,0:T(8,128)S(1)}, f32[96,80]{1,0:T(8,128)S(1)}, u32[]{:S(2)}, u32[]{:S(2)}) collective-permute-start(f32[96,80]{1,0:T(8,128)S(1)} %constant_dynamic-update-slice_fusion.6.refs_2_.h), channel_id=1, source_target_pairs={{0,120},{8,0},{16,8},{24,16},{32,24},{40,32},{48,40},{56,48},{64,5... | collective-permute-start | bytes 92168 | tf_op jit(solution)/shard_map/ppermute | solution.py:159
  43.5 7.5 %collective-permute-start.10 = (f32[96,80]{1,0:T(8,128)S(1)}, f32[96,80]{1,0:T(8,128)S(1)}, u32[]{:S(2)}, u32[]{:S(2)}) collective-permute-start(f32[96,80]{1,0:T(8,128)S(1)} %constant_dynamic-update-slice_fusion.6.refs_2_.h), channel_id=1, source_target_pairs={{0,8},{8,16},{16,24},{24,32},{32,40},{40,48},{48,56},{56,64},{64,7... | collective-permute-start | bytes 92168 | tf_op jit(solution)/shard_map/ppermute | solution.py:159
  52.5 5.2 %collective-permute-start.12 = (f32[32,80]{1,0:T(8,128)S(1)}, f32[32,80]{1,0:T(8,128)S(1)}, u32[]{:S(2)}, u32[]{:S(2)}) collective-permute-start(f32[32,80]{1,0:T(8,128)S(1)} %get-tuple-element.21), channel_id=1, source_target_pairs={{0,1},{1,2},{2,3},{3,4},{4,5},{5,6},{6,7},{7,0},{8,9},{9,10},{10,1... | collective-permute-start | bytes 30728 | tf_op jit(solution)/shard_map/ppermute | solution.py:159
  54.8 11.8 %copy-start.1 = (f32[80,8192]{1,0:T(8,128)S(1)}, f32[80,8192]{1,0:T(8,128)}, u32[]{:S(2)}) copy-start(f32[80,8192]{1,0:T(8,128)} %refs_5_.1) | copy-start | bytes 7864324
  54.8 4.4 %collective-permute-start.13 = (f32[32,80]{1,0:T(8,128)S(1)}, f32[32,80]{1,0:T(8,128)S(1)}, u32[]{:S(2)}, u32[]{:S(2)}) collective-permute-start(f32[32,80]{1,0:T(8,128)S(1)} %get-tuple-element.21), channel_id=1, source_target_pairs={{0,7},{1,0},{2,1},{3,2},{4,3},{5,4},{6,5},{7,6},{8,15},{9,8},{10,9... | collective-permute-start | bytes 30728 | tf_op jit(solution)/shard_map/ppermute | solution.py:159
  59.2 4.3 %collective-permute-start.15 = (f32[96,80]{1,0:T(8,128)S(1)}, f32[96,80]{1,0:T(8,128)S(1)}, u32[]{:S(2)}, u32[]{:S(2)}) collective-permute-start(f32[96,80]{1,0:T(8,128)S(1)} %constant_dynamic-update-slice_fusion.9.refs_1_), channel_id=1, source_target_pairs={{0,120},{8,0},{16,8},{24,16},{32,24},{40,32},{48,40},{56,48},{64,5... | collective-permute-start | bytes 92168 | tf_op jit(solution)/shard_map/ppermute | solution.py:159
  59.2 7.4 %collective-permute-start.14 = (f32[96,80]{1,0:T(8,128)S(1)}, f32[96,80]{1,0:T(8,128)S(1)}, u32[]{:S(2)}, u32[]{:S(2)}) collective-permute-start(f32[96,80]{1,0:T(8,128)S(1)} %constant_dynamic-update-slice_fusion.9.refs_1_), channel_id=1, source_target_pairs={{0,8},{8,16},{16,24},{24,32},{32,40},{40,48},{48,56},{56,64},{64,7... | collective-permute-start | bytes 92168 | tf_op jit(solution)/shard_map/ppermute | solution.py:159

commit v2 on v0

v2 whole, which is shorter than its diff:
```python
import jax
import jax.numpy as jnp
from jax import lax
from jax.experimental import pallas as pl
from jax.experimental.pallas import tpu as pltpu
from jax.sharding import PartitionSpec as P

BLK = 1024
EPS = 1e-05
ZN = 4
PAD = 8
F32 = jnp.float32
BF16 = jnp.bfloat16
VMEM = pltpu.VMEM
NT = (((1,), (1,)), ((), ()))
NN = (((1,), (0,)), ((), ()))
TN = (((0,), (0,)), ((), ()))


def split(x):
    high = x.astype(BF16)
    return high, (x - high.astype(F32)).astype(BF16)


def dot3(a, b, dims):
    ah, al = a
    bh, bl = b
    d = lambda p, q: lax.dot_general(p, q, dims, preferred_element_type=F32)
    return d(ah, bh) + (d(ah, bl) + d(al, bh))


def observe(rows):
    members = rows.shape[1] - PAD
    x = rows[:, :members]
    value, error, live = (rows[:, members + k : members + k + 1] for k in (1, 2, 3))
    mean = jnp.sum(x, axis=1, keepdims=True) / members
    anomaly = x - mean
    var = jnp.sum(anomaly * anomaly, axis=1, keepdims=True) / (members - 1) + EPS
    increment = (
        var / (var + error) * (value - mean) + (jnp.sqrt(error / (var + error)) - 1.0) * anomaly
    )
    centred = anomaly - jnp.sum(anomaly, axis=1, keepdims=True) / members
    return centred * (live / ((members - 1) * var)), increment


def width(batch, batches):
    return 2 * (batches - batch) + 1


def gather_kernel(loc_in, count_in, value_in, error_in, ens_in, out, loc, count, values, error, ens, sems):
    members = ens.shape[0]
    batches, slots = loc.shape
    n = batches * slots
    small = [(loc_in, loc), (count_in, count), (value_in, values), (error_in, error)]
    copies = [pltpu.make_async_copy(src, dst, sems.at[k]) for k, (src, dst) in enumerate(small)]
    for k in range(ens.shape[1] // BLK):
        at = pl.ds(k * BLK, BLK)
        copies.append(pltpu.make_async_copy(ens_in.at[:, at], ens.at[:, at], sems.at[4 + k]))
    for copy in copies:
        copy.start()
    device = lax.axis_index("gx") * lax.axis_size("gy") + lax.axis_index("gy")
    first = device * (ens.shape[1] // BLK)
    lane = lax.broadcasted_iota(jnp.int32, (members, 128), 1)
    lane8 = lax.broadcasted_iota(jnp.int32, (PAD, 128), 1)
    row8 = lax.broadcasted_iota(jnp.int32, (PAD, 128), 0)
    side = jnp.zeros((PAD, 128), F32)
    for copy in copies[:4]:
        copy.wait()
    for j in range(n):
        b, k = j // slots, j % slots
        block = (first + loc[b, k] // BLK).astype(F32)
        live = jnp.where(k < count[0, b], 1.0, 0.0).astype(F32)
        new = jnp.where(
            row8 == 0, block, jnp.where(row8 == 1, values[b, k], jnp.where(row8 == 2, error[b, k], live))
        )
        side = jnp.where(lane8 == j, new, side)
    for copy in copies[4:]:
        copy.wait()
    acc = jnp.zeros((members, 128), F32)
    for j in range(n):
        c = loc[j // slots, j % slots]
        tile = ens[:, pl.ds(pl.multiple_of((c // 128) * 128, 128), 128)]
        acc = jnp.where(lane == j, pltpu.roll(tile, (j - c % 128 + 128) % 128, 1), acc)
    out[...] = jnp.transpose(jnp.concatenate([acc, side], axis=0))[:n]


def pack_kernel(blocks, weights, list_blocks, list_weights, coef):
    batches, nlist = blocks.shape[:2]
    nb = coef.shape[1]
    lanes = list_blocks.shape[2]
    nx, ny = lax.axis_size("gx"), lax.axis_size("gy")
    ix, iy = lax.axis_index("gx"), lax.axis_index("gy")
    slots = blocks.shape[2] // (nx * ny)
    row_lanes = ny * slots
    first = (ix * ny + iy) * nb
    span = 3 * slots
    lane = lax.broadcasted_iota(jnp.int32, (nlist, 128), 1)
    row = lax.broadcasted_iota(jnp.int32, (nb, 128), 0)
    for b in range(batches):
        w = width(b, batches)
        held_b = [jnp.full((nlist, 128), -1, jnp.int32) for _ in range(lanes // 128)]
        held_w = [jnp.zeros((nlist, 128), F32) for _ in range(lanes // 128)]
        held_c = [jnp.zeros((nb, 128), F32) for _ in range(2)]

        def put(held, tile, d):
            tile = pltpu.roll(tile, (d * span - (iy - 1) * slots + 4 * 128) % 128, 1)
            begin, end = d * span, (d + 1) * span
            for t in range(begin // 128, (end - 1) // 128 + 1):
                keep = (lane >= begin - t * 128) & (lane < end - t * 128)
                held[t] = jnp.where(keep, tile, held[t])

        for d in range(w):
            near = (ix + d - w // 2 + nx) % nx
            at = pl.ds(pl.multiple_of(near * row_lanes, row_lanes), row_lanes)
            bl, wt = blocks[b, :, at], weights[b, :, at]
            put(held_b, bl, d)
            put(held_w, wt, d)
            if abs(d - w // 2) <= 1:
                tile = jnp.zeros((nb, 128), F32)
                for s in range(nb):
                    one = jnp.sum(jnp.where(bl == first + s, wt, 0.0), axis=0, keepdims=True)
                    tile = jnp.where(row == s, one, tile)
                put(held_c, tile, d - w // 2 + 1)
        for t in range(lanes // 128):
            list_blocks[b, :, t * 128 : (t + 1) * 128] = held_b[t]
            list_weights[b, :, t * 128 : (t + 1) * 128] = held_w[t]
        for t in range(2):
            coef[b, :, t * 128 : (t + 1) * 128] = held_c[t]


def along_z_kernel(slots, own, south, north, across, up, down):
    z = lax.axis_index("gx") % ZN
    mine, below, above = own[...], south[...], north[...]
    n = mine.shape[0]
    up[:n] = jnp.where(z == ZN - 1, below, mine)
    up[n:] = jnp.where(z == ZN - 1, mine, above)[: 2 * slots]
    down[:n] = jnp.where(z == 0, above, mine)
    down[n:] = jnp.where(z == 0, mine, below)[: 2 * slots]
    across[: 3 * slots] = jnp.where(z < 2, mine, below)[: 3 * slots]
    across[3 * slots :] = jnp.where(z < 2, above, mine)[: 3 * slots]


def window_kernel(batches, slots, own, south, north, across, up, down, first, rest):
    n = batches * slots
    source = {
        0: (own, 0),
        -4: (south, 0),
        4: (north, 0),
        -1: (up, 0),
        3: (up, n),
        1: (down, 0),
        -3: (down, n),
        -2: (across, 0),
        2: (across, 3 * slots),
    }
    at = 0
    for b in range(batches):
        half = batches - b
        for d in range(-half, half + 1):
            ref, begin = source[d]
            piece = ref[begin + b * slots : begin + (b + 1) * slots]
            if b == 0:
                first[(d + half) * slots : (d + half + 1) * slots] = piece
            else:
                rest[at : at + slots] = piece
                at += slots


def gathered(own, swapped, crossed, slots):
    even = lax.axis_index("gy") % 2 == 0
    a, b, mine = swapped[...], crossed[...], own[...]
    south = jnp.where(even, b, a)
    north = jnp.where(even, a, b)
    pieces = []
    for d in range(mine.shape[0] // slots):
        at = slice(d * slots, (d + 1) * slots)
        pieces += [south[at], mine[at], north[at]]
    return jnp.concatenate(pieces, axis=0)


def mask_of(batch, rest, list_blocks, list_weights, nobs):
    members = rest.shape[1] - PAD
    block = rest[:, members : members + 1].astype(jnp.int32)
    lanes = (nobs + 127) // 128 * 128
    mask = jnp.zeros((rest.shape[0], lanes), F32)
    for l in range(list_blocks.shape[1]):
        mask = mask + jnp.where(
            block == list_blocks[batch, l : l + 1, :lanes], list_weights[batch, l : l + 1, :lanes], 0.0
        )
    return mask


def compose(batch, maps, scaled, increment, coef):
    nb = coef.shape[1]
    members = scaled.shape[1]
    nobs = scaled.shape[0]
    scaled, increment = split(scaled), split(increment)
    s = dot3(split(maps), scaled, NT)
    p = jnp.concatenate(
        [s[k * members : (k + 1) * members] * coef[batch, k : k + 1, :nobs] for k in range(nb)], axis=0
    )
    return maps + dot3(split(p), increment, NN)


def unit(members):
    i = lax.broadcasted_iota(jnp.int32, (members, members), 0)
    j = lax.broadcasted_iota(jnp.int32, (members, members), 1)
    return jnp.where(i == j, 1.0, 0.0).astype(F32)


def mask_kernel(batch, nobs, rest, list_blocks, list_weights, mask):
    mask[...] = mask_of(batch, rest[...], list_blocks, list_weights, nobs)


def map_kernel(batch, scaled, increment, coef, maps, out):
    nb = coef.shape[1]
    start = jnp.concatenate([unit(scaled.shape[1])] * nb, axis=0) if maps is None else maps[...]
    out[...] = compose(batch, start, scaled[...], increment[...], coef)


def step_kernel(slots, own, swapped, crossed, rest, mask, nxt, left, center_s, center_i):
    members = rest.shape[1] - PAD
    scaled, increment = observe(gathered(own, swapped, crossed, slots))
    nobs = scaled.shape[0]
    mid = nobs // (6 * slots) * 3 * slots
    center_s[...] = scaled[mid - 3 * slots : mid + 6 * slots]
    center_i[...] = increment[mid - 3 * slots : mid + 6 * slots]
    rows = rest[...]
    x = rows[:, :members]
    p = dot3(split(x), split(scaled), NT) * mask[:, :nobs]
    x = x + dot3(split(p), split(increment), NN)
    k = nxt.shape[0]
    nxt[:, :members] = x[:k]
    nxt[:, members:] = rows[:k, members:]
    if left is not None:
        left[:, :members] = x[k:]
        left[:, members:] = rows[k:, members:]


def final_kernel(batch, slots, own, swapped, crossed, coef, maps, ens, out, result, sems):
    nb = coef.shape[1]
    members = ens.shape[0]
    scaled, increment = observe(gathered(own, swapped, crossed, slots))
    whole = compose(batch, maps[...], scaled, increment, coef)
    eye = unit(members)
    copies = []
    for k in range(nb):
        dh, dl = split(whole[k * members : (k + 1) * members] - eye)
        x = ens[:, k * BLK : (k + 1) * BLK]
        xh, xl = split(x)
        left = jnp.concatenate([dh, dl, dh], axis=0)
        right = jnp.concatenate([xh, xh, xl], axis=0)
        at = pl.ds(k * BLK, BLK)
        result[:, at] = x + lax.dot_general(left, right, TN, preferred_element_type=F32)
        copies.append(pltpu.make_async_copy(result.at[:, at], out.at[:, at], sems.at[k]))
        copies[-1].start()
    for copy in copies:
        copy.wait()


def permute(x, target):
    nx, ny = lax.axis_size("gx"), lax.axis_size("gy")
    pairs = []
    for i in range(nx):
        for j in range(ny):
            a, c = target(i, j)
            pairs.append((i * ny + j, (a % nx) * ny + c % ny))
    return lax.ppermute(x, ("gx", "gy"), pairs)


def shards(ensemble, loc, values, error, count, blocks, weights):
    members, rows_here = ensemble.shape
    batches, slots = loc.shape
    nb = rows_here // BLK
    n = batches * slots
    wide = members + PAD
    vm = pl.BlockSpec(memory_space=VMEM)
    hbm = pl.BlockSpec(memory_space=pltpu.HBM)
    tie = pl.BlockSpec(memory_space=pl.ANY)
    params = pltpu.CompilerParams(vmem_limit_bytes=40 * 1024 * 1024)
    shape = lambda *s: jax.ShapeDtypeStruct(s, F32)
    cost = lambda us: pl.CostEstimate(flops=us * 10**6, bytes_accessed=us * 10**5, transcendentals=0)

    own = pl.pallas_call(
        gather_kernel,
        out_shape=shape(n, wide),
        in_specs=[hbm] * 5,
        out_specs=vm,
        scratch_shapes=[
            pltpu.SMEM((batches, slots), jnp.int32),
            pltpu.SMEM((1, batches), jnp.int32),
            pltpu.SMEM((batches, slots), F32),
            pltpu.SMEM((batches, slots), F32),
            pltpu.VMEM((members, rows_here), F32),
            pltpu.SemaphoreType.DMA((4 + nb,)),
        ],
        compiler_params=pltpu.CompilerParams(vmem_limit_bytes=64 * 1024 * 1024 - 2**21),
        name="gather_columns",
    )(loc, count.reshape(1, batches), values, error, ensemble)

    lanes = (width(0, batches) * 3 * slots + 127) // 128 * 128
    list_blocks, list_weights, coef = pl.pallas_call(
        pack_kernel,
        out_shape=(
            jax.ShapeDtypeStruct((batches, blocks.shape[1], lanes), jnp.int32),
            shape(batches, blocks.shape[1], lanes),
            shape(batches, nb, 256),
        ),
        in_specs=[vm, vm],
        out_specs=(vm, vm, vm),
        compiler_params=params,
        cost_estimate=cost(1),
        name="pack_lists",
    )(blocks, weights)

    south = permute(own, lambda i, j: (i + ZN, j))
    north = permute(own, lambda i, j: (i - ZN, j))
    across, up, down = pl.pallas_call(
        lambda *refs: along_z_kernel(slots, *refs),
        out_shape=(shape(6 * slots, wide), shape(n + 2 * slots, wide), shape(n + 2 * slots, wide)),
        in_specs=[vm] * 3,
        out_specs=(vm,) * 3,
        compiler_params=params,
        name="select_along_z",
    )(own, south, north)
    turn = lambda k: (lambda i, j: (i // ZN * ZN + (i + k) % ZN, j))
    across = permute(across, turn(2))
    up = permute(up, turn(1))
    down = permute(down, turn(ZN - 1))
    total = sum(width(b, batches) for b in range(1, batches)) * slots
    here, rest = pl.pallas_call(
        lambda *refs: window_kernel(batches, slots, *refs),
        out_shape=(shape(width(0, batches) * slots, wide), shape(total, wide)),
        in_specs=[vm] * 6,
        out_specs=(vm, vm),
        compiler_params=params,
        name="lay_out_window",
    )(own, south, north, across, up, down)

    maps = None
    for b in range(batches):
        swapped = permute(here, lambda i, j: (i, j + 1 - 2 * (j % 2)))
        crossed = permute(here, lambda i, j: (i, j + 1 if j % 2 else j - 1))
        if b > 0:
            given = () if maps is None else (maps,)
            body = lambda s, i, c, *r, b=b: map_kernel(b - 1, s, i, c, r[0] if len(r) == 2 else None, r[-1])
            maps = pl.pallas_call(
                body,
                out_shape=shape(nb * members, members),
                in_specs=[vm] * (3 + len(given)),
                out_specs=vm,
                compiler_params=params,
                cost_estimate=cost(1),
                name="compose_maps",
            )(center_s, center_i, coef, *given)
        if b == batches - 1:
            break
        w = width(b, batches)
        nobs = w * 3 * slots
        mask = pl.pallas_call(
            lambda *refs, b=b, nobs=nobs: mask_kernel(b, nobs, *refs),
            out_shape=shape(rest.shape[0], (nobs + 127) // 128 * 128),
            in_specs=[vm] * 3,
            out_specs=vm,
            compiler_params=params,
            cost_estimate=cost(1),
            name="list_mask",
        )(rest, list_blocks, list_weights)
        k = width(b + 1, batches) * slots
        outs = [shape(k, wide), shape(9 * slots, members), shape(9 * slots, members)]
        last = rest.shape[0] == k
        if not last:
            outs.insert(1, shape(rest.shape[0] - k, wide))
            body = lambda *refs: step_kernel(slots, *refs[:5], *refs[-4:])
        else:
            body = lambda *refs: step_kernel(slots, *refs[:5], refs[-3], None, *refs[-2:])
        after = () if maps is None else (maps,)
        res = pl.pallas_call(
            body,
            out_shape=tuple(outs),
            in_specs=[vm] * 5 + [tie] * len(after),
            out_specs=(vm,) * len(outs),
            compiler_params=params,
            name="step_columns",
        )(here, swapped, crossed, rest, mask, *after)
        here, center_s, center_i = res[0], res[-2], res[-1]
        rest = None if last else res[1]

    return pl.pallas_call(
        lambda *refs: final_kernel(batches - 1, slots, *refs),
        out_shape=shape(members, rows_here),
        in_specs=[vm] * 6,
        out_specs=hbm,
        scratch_shapes=[pltpu.VMEM((members, rows_here), F32), pltpu.SemaphoreType.DMA((nb,))],
        compiler_params=params,
        name="apply_maps",
    )(here, swapped, crossed, coef, maps, ensemble)


def solution(mesh):
    split_specs = P(None, ("gx", "gy"))
    in_specs = (split_specs,) * 5 + (P(), P())
    return jax.shard_map(
        shards, mesh=mesh, in_specs=in_specs, out_specs=split_specs, check_vma=False
    )
```

time: 187 us -> 47.2 us (0.25)
  local copies, waits for them, and re-layouts: 65.1 us -> 0.77 us
  other arithmetic: 49 us -> 0 us
  matrix products: 30.3 us -> 0 us
  starting transfers between devices: 35.6 us -> 12.9 us
  waiting for transfers between devices: 5.29 us -> 19.6 us
  Pallas kernels: 0 us -> 13.7 us
    dot_general x8 -> x0, matrix products: 30.3 us -> none  [the longest x4 23.6 us: shards(): jnp.einsum('bnt,nbf->tbf', kalman_gain_factor, member_deviation, precisio...]
    gather x12 -> x0, local copies, waits for them, and re-layouts: 24.1 us -> none  [the longest x4 11.4 us: shards(): jnp.take(present_sweep_value, measured_line_locations[group_of_sets], axi...]
    ppermute x16 -> x13, starting transfers between devices: 35.6 us -> 12.9 us  [permute(): return lax.ppermute(x, ('gx', 'gy'), pairs)]
    reduce_sum x13 -> x0, other arithmetic: 21.7 us -> none  [the longest x4 19.5 us: shards(): jnp.mean(present_sweep_value, axis=0)]
    reshape x12 -> x0, local copies, waits for them, and re-layouts: 16.3 us -> none  [the longest x4 14.9 us: shards(): state_adjust.reshape(members, rows_here)]
    ppermute x16 -> x13, waiting for transfers between devices: 5.29 us -> 19.6 us  [permute(): return lax.ppermute(x, ('gx', 'gy'), pairs)]
    sub x4 -> x0, other arithmetic: 14.2 us -> none  [shards(): present_sweep_value - jnp.mean(present_sweep_value, axis=0)]
    pallas_call x0 -> x14, Pallas kernels: none -> 13.7 us  [the longest x1 3.42 us: shards(): pl.pallas_call(gather_kernel, out_shape=shape(n, wide), in_specs=[hbm] *...]
  transfers between devices with their start and end apart: 16 -> 13, of which waited for: 5 -> 7; matrix products, arithmetic and copies ran while one was open for 21% -> 0% of each run, Pallas kernels for 0% -> 9%
where the time goes in v2:
time: 47.2 us; the launch traced here: 47.1 us
  waiting for transfers between devices  19.6 us (42%)
  Pallas kernels  13.7 us (29%)
  starting transfers between devices  12.9 us (27%)
  local copies, waits for them, and re-layouts  0.77 us (2%)
    ppermute x13, waiting for transfers between devices, permute(): return lax.ppermute(x, ('gx', 'gy'), pairs)  19.6 us
    ppermute x13, starting transfers between devices, permute(): return lax.ppermute(x, ('gx', 'gy'), pairs)  12.9 us
    pallas_call x1, Pallas kernels, shards(): pl.pallas_call(gather_kernel, out_shape=shape(n, wide), in_specs=[hbm] *...  3.42 us
    pallas_call x3, Pallas kernels, shards(): pl.pallas_call(body, out_shape=shape(nb * members, members), in_specs=[vm...  3.39 us
    pallas_call x1, Pallas kernels, shards(): pl.pallas_call(lambda *refs: final_kernel(batches - 1, slots, *refs), out...  3.14 us
    pallas_call x3, Pallas kernels, shards(): pl.pallas_call(body, out_shape=tuple(outs), in_specs=[vm] * 5 + [tie] * l...  2.66 us
  transfers between devices with their start and end apart: 13, of which 7 were waited for; matrix products, arithmetic and copies ran while one was open for 0% of the time, Pallas kernels for 9%

profile of v2, /device:TPU:0, one launch (start us, length us, event | category | flops | bytes accessed | tf_op | source)
XLA Modules:
  0.0 47.1 jit_solution(4070430139754768170)
XLA Ops:
  0.0 0.0 copy-start.3
  0.0 0.0 copy-start.2
  0.0 3.4 %gather_columns.1.refs_0_ = f32[64,88]{1,0:T(8,128)} custom-call(s32[4,16]{1,0:T(4,128)} %loc_in.1, s32[1,4]{1,0:T(1,128)} %bitcast.1, f32[4,16]{1,0:T(4,128)} %value_in.1, f32[4,16]{1,0:T(4,128)} %error_in.1, f32[80,8192]{1,0:T(8,128)} %refs_5_.1), custom_call_target="tpu_custom_call" | custom-call | tf_op jit(solution)/shard_map/gather_columns/pallas_call | solution.py:284
  3.4 3.2 %collective-permute-start.1 = (f32[64,88]{1,0:T(8,128)}, f32[64,88]{1,0:T(8,128)S(1)}, u32[]{:S(2)}, u32[]{:S(2)}) collective-permute-start(f32[64,88]{1,0:T(8,128)} %gather_columns.1.refs_0_), channel_id=1, source_target_pairs={{0,96},{1,97},{2,98},{3,99},{4,100},{5,101},{6,102},{7,103},{8,104... | collective-permute-start | bytes 67592 | tf_op jit(solution)/shard_map/ppermute | solution.py:268
  6.6 0.0 collective-permute-start
  6.6 1.9 %collective-permute-done.1.refs_2_ = f32[64,88]{1,0:T(8,128)S(1)} collective-permute-done((f32[64,88]{1,0:T(8,128)}, f32[64,88]{1,0:T(8,128)S(1)}, u32[]{:S(2)}, u32[]{:S(2)}) %collective-permute-start.1) | collective-permute-done | bytes 22560 | tf_op jit(solution)/shard_map/ppermute | solution.py:268
  8.5 3.4 %collective-permute-done.refs_1_ = f32[64,88]{1,0:T(8,128)S(1)} collective-permute-done((f32[64,88]{1,0:T(8,128)}, f32[64,88]{1,0:T(8,128)S(1)}, u32[]{:S(2)}, u32[]{:S(2)}) %collective-permute-start) | collective-permute-done | bytes 22560 | tf_op jit(solution)/shard_map/ppermute | solution.py:268
  11.9 0.0 copy-start.1
  11.9 0.8 %copy-done.1 = f32[64,88]{1,0:T(8,128)S(1)} copy-done((f32[64,88]{1,0:T(8,128)S(1)}, f32[64,88]{1,0:T(8,128)}, u32[]{:S(2)}) %copy-start.1) | copy-done | bytes 22552
  12.7 4.0 %collective-permute-start.2 = (f32[96,88]{1,0:T(8,128)S(1)}, f32[96,88]{1,0:T(8,128)S(1)}, u32[]{:S(2)}, u32[]{:S(2)}) collective-permute-start(f32[96,88]{1,0:T(8,128)S(1)} %get-tuple-element.24), channel_id=1, source_target_pairs={{0,16},{1,17},{2,18},{3,19},{4,20},{5,21},{6,22},{7,23},{8,24},{9,... | collective-permute-start | bytes 101384 | tf_op jit(solution)/shard_map/ppermute | solution.py:268
  16.7 1.0 %collective-permute-start.3 = (f32[96,88]{1,0:T(8,128)S(1)}, f32[96,88]{1,0:T(8,128)S(1)}, u32[]{:S(2)}, u32[]{:S(2)}) collective-permute-start(f32[96,88]{1,0:T(8,128)S(1)} %get-tuple-element.25), channel_id=1, source_target_pairs={{0,8},{1,9},{2,10},{3,11},{4,12},{5,13},{6,14},{7,15},{8,16},{9,17... | collective-permute-start | bytes 101384 | tf_op jit(solution)/shard_map/ppermute | solution.py:268
  17.7 2.2 %collective-permute-start.4 = (f32[96,88]{1,0:T(8,128)S(1)}, f32[96,88]{1,0:T(8,128)S(1)}, u32[]{:S(2)}, u32[]{:S(2)}) collective-permute-start(f32[96,88]{1,0:T(8,128)S(1)} %get-tuple-element.26), channel_id=1, source_target_pairs={{0,24},{1,25},{2,26},{3,27},{4,28},{5,29},{6,30},{7,31},{8,0},{9,1... | collective-permute-start | bytes 101384 | tf_op jit(solution)/shard_map/ppermute | solution.py:268
  19.9 0.0 collective-permute-done.2.refs_3_
  19.9 2.1 %collective-permute-done.3.refs_4_ = f32[96,88]{1,0:T(8,128)S(1)} collective-permute-done((f32[96,88]{1,0:T(8,128)S(1)}, f32[96,88]{1,0:T(8,128)S(1)}, u32[]{:S(2)}, u32[]{:S(2)}) %collective-permute-start.3) | collective-permute-done | bytes 33824 | tf_op jit(solution)/shard_map/ppermute | solution.py:268
  22.0 0.0 collective-permute-done.4.refs_5_
  22.0 0.1 collective-permute-start.6
  22.1 1.6 %collective-permute-start.5 = (f32[144,88]{1,0:T(8,128)S(1)}, f32[144,88]{1,0:T(8,128)S(1)}, u32[]{:S(2)}, u32[]{:S(2)}) collective-permute-start(f32[144,88]{1,0:T(8,128)S(1)} %get-tuple-element.27.refs_0_), channel_id=1, source_target_pairs={{0,1},{1,0},{2,3},{3,2},{4,5},{5,4},{6,7},{7,6},{8,9},{9,8},{10,11... | collective-permute-start | bytes 152072 | tf_op jit(solution)/shard_map/ppermute | solution.py:268
  23.7 0.0 copy-done.3
  23.7 0.0 copy-done.2
  23.7 0.2 pack_lists.1
  23.9 0.4 list_mask.3.refs_4_
  24.4 0.0 copy-start
  24.4 2.7 %collective-permute-done.6.refs_2_ = f32[144,88]{1,0:T(8,128)S(1)} collective-permute-done((f32[144,88]{1,0:T(8,128)S(1)}, f32[144,88]{1,0:T(8,128)S(1)}, u32[]{:S(2)}, u32[]{:S(2)}) %collective-permute-start.6) | collective-permute-done | bytes 50720 | tf_op jit(solution)/shard_map/ppermute | solution.py:268
  27.1 0.0 collective-permute-done.5.refs_1_
  27.1 1.0 %step_columns.3 = (f32[112,88]{1,0:T(8,128)S(1)}, f32[128,88]{1,0:T(8,128)S(1)}, f32[144,80]{1,0:T(8,128)S(1)}, f32[144,80]{1,0:T(8,128)S(1)}) custom-call(f32[144,88]{1,0:T(8,128)S(1)} %get-tuple-element.27.refs_0_, f32[144,88]{1,0:T(8,128)S(1)} %collective-permute-done.5.refs_1_, f32[144,88]{1,0:T(8,128)S(1)} %collective-permute-done.6.refs_2_, ...), custom_call_target="tpu_custom_call" | custom-call | tf_op jit(solution)/shard_map/step_columns/pallas_call | solution.py:378
  28.1 0.1 collective-permute-start.8
  28.2 0.4 collective-permute-start.7
  28.6 0.2 list_mask.4.refs_4_
  28.8 1.1 %compose_maps.3.refs_5_.r_0_ = f32[640,80]{1,0:T(8,128)S(1)} custom-call(f32[144,80]{1,0:T(8,128)S(1)} %get-tuple-element.33.s, f32[144,80]{1,0:T(8,128)S(1)} %get-tuple-element.34.i, f32[4,8,256]{2,1,0:T(8,128)S(1)} %get-tuple-element.35.c.refs_3_), custom_call_target="tpu_custom_call" | custom-call | flops 1000000 | bytes 100000 | tf_op jit(solution)/shard_map/compose_maps/pallas_call | solution.py:347
  29.9 3.1 %collective-permute-done.8.refs_2_ = f32[112,88]{1,0:T(8,128)S(1)} collective-permute-done((f32[112,88]{1,0:T(8,128)S(1)}, f32[112,88]{1,0:T(8,128)S(1)}, u32[]{:S(2)}, u32[]{:S(2)}) %collective-permute-start.8) | collective-permute-done | bytes 39456 | tf_op jit(solution)/shard_map/ppermute | solution.py:268
  33.0 0.0 collective-permute-done.7.refs_1_
  33.0 0.9 %step_columns.4 = (f32[80,88]{1,0:T(8,128)S(1)}, f32[48,88]{1,0:T(8,128)S(1)}, f32[144,80]{1,0:T(8,128)S(1)}, f32[144,80]{1,0:T(8,128)S(1)}) custom-call(f32[112,88]{1,0:T(8,128)S(1)} %get-tuple-element.31.refs_0_, f32[112,88]{1,0:T(8,128)S(1)} %collective-permute-done.7.refs_1_, f32[112,88]{1,0:T(8,128)S(1)} %collective-permute-done.8.refs_2_, ...), custom_call_target="tpu_custom_call" | custom-call | tf_op jit(solution)/shard_map/step_columns/pallas_call | solution.py:378
  33.9 0.1 collective-permute-start.10
  34.0 0.1 collective-permute-start.9
  34.1 0.1 list_mask.5.refs_4_
  34.2 1.1 %compose_maps.4.refs_5_.r_0_ = f32[640,80]{1,0:T(8,128)S(1)} custom-call(f32[144,80]{1,0:T(8,128)S(1)} %get-tuple-element.38.s, f32[144,80]{1,0:T(8,128)S(1)} %get-tuple-element.39.i, f32[4,8,256]{2,1,0:T(8,128)S(1)} %get-tuple-element.35.c.refs_3_, f32[640,80]{1,0:T(8,128)S(1)} %compose_maps.3.refs_5_.r_0_), custom_call_target="tpu_custom_call" | custom-call | flops 1000000 | bytes 100000 | tf_op jit(solution)/shard_map/compose_maps/pallas_call | solution.py:347
  35.3 3.3 %collective-permute-done.10.refs_2_ = f32[80,88]{1,0:T(8,128)S(1)} collective-permute-done((f32[80,88]{1,0:T(8,128)S(1)}, f32[80,88]{1,0:T(8,128)S(1)}, u32[]{:S(2)}, u32[]{:S(2)}) %collective-permute-start.10) | collective-permute-done | bytes 28192 | tf_op jit(solution)/shard_map/ppermute | solution.py:268
  38.6 0.0 collective-permute-done.9.refs_1_
  38.6 0.7 %step_columns.5 = (f32[48,88]{1,0:T(8,128)S(1)}, f32[144,80]{1,0:T(8,128)S(1)}, f32[144,80]{1,0:T(8,128)S(1)}) custom-call(f32[80,88]{1,0:T(8,128)S(1)} %get-tuple-element.36.refs_0_, f32[80,88]{1,0:T(8,128)S(1)} %collective-permute-done.9.refs_1_, f32[80,88]{1,0:T(8,128)S(1)} %collective-permute-done.10.refs_2_, ...), custom_call_target="tpu_custom_call" | custom-call | tf_op jit(solution)/shard_map/step_columns/pallas_call | solution.py:378
  39.4 0.1 collective-permute-start.12
  39.5 0.1 collective-permute-start.11
  39.6 1.1 %compose_maps.5.refs_4_ = f32[640,80]{1,0:T(8,128)S(1)} custom-call(f32[144,80]{1,0:T(8,128)S(1)} %get-tuple-element.41.s, f32[144,80]{1,0:T(8,128)S(1)} %get-tuple-element.42.i, f32[4,8,256]{2,1,0:T(8,128)S(1)} %get-tuple-element.35.c.refs_3_, f32[640,80]{1,0:T(8,128)S(1)} %compose_maps.4.refs_5_.r_0_), custom_call_target="tpu_custom_call" | custom-call | flops 1000000 | bytes 100000 | tf_op jit(solution)/shard_map/compose_maps/pallas_call | solution.py:347
  40.7 3.2 %collective-permute-done.12.refs_2_ = f32[48,88]{1,0:T(8,128)S(1)} collective-permute-done((f32[48,88]{1,0:T(8,128)S(1)}, f32[48,88]{1,0:T(8,128)S(1)}, u32[]{:S(2)}, u32[]{:S(2)}) %collective-permute-start.12) | collective-permute-done | bytes 16928 | tf_op jit(solution)/shard_map/ppermute | solution.py:268
  43.9 0.0 collective-permute-done.11.refs_1_
  43.9 0.0 copy-done
  43.9 3.1 %apply_maps.1 = f32[80,8192]{1,0:T(8,128)} custom-call(f32[48,88]{1,0:T(8,128)S(1)} %get-tuple-element.40.refs_0_, f32[48,88]{1,0:T(8,128)S(1)} %collective-permute-done.11.refs_1_, f32[48,88]{1,0:T(8,128)S(1)} %collective-permute-done.12.refs_2_, f32[4,8,256]{2,1,0:T(8,128)S(1)} %get-tuple-element.35.c.refs_3_, f32[640,80]{1,0:T(8,128)S(1)} %compose_maps.5.refs_4_, ...), custom_call_target="tpu_custom_call" | custom-call | tf_op jit(solution)/shard_map/apply_maps/pallas_call | solution.py:389
  (2 shorter events, 0.0 us)
Async XLA Ops:
  0.0 23.7 %copy-start.3 = (f32[4,8,2048]{2,1,0:T(8,128)S(1)}, f32[4,8,2048]{2,1,0:T(8,128)}, u32[]{:S(2)}) copy-start(f32[4,8,2048]{2,1,0:T(8,128)} %weights.1) | copy-start | bytes 786436
  0.0 23.7 %copy-start.2 = (s32[4,8,2048]{2,1,0:T(8,128)S(1)}, s32[4,8,2048]{2,1,0:T(8,128)}, u32[]{:S(2)}) copy-start(s32[4,8,2048]{2,1,0:T(8,128)} %blocks.1) | copy-start | bytes 786436
  3.4 5.1 %collective-permute-start.1 = (f32[64,88]{1,0:T(8,128)}, f32[64,88]{1,0:T(8,128)S(1)}, u32[]{:S(2)}, u32[]{:S(2)}) collective-permute-start(f32[64,88]{1,0:T(8,128)} %gather_columns.1.refs_0_), channel_id=1, source_target_pairs={{0,96},{1,97},{2,98},{3,99},{4,100},{5,101},{6,102},{7,103},{8,104... | collective-permute-start | bytes 67592 | tf_op jit(solution)/shard_map/ppermute | solution.py:268
  6.6 5.3 %collective-permute-start = (f32[64,88]{1,0:T(8,128)}, f32[64,88]{1,0:T(8,128)S(1)}, u32[]{:S(2)}, u32[]{:S(2)}) collective-permute-start(f32[64,88]{1,0:T(8,128)} %gather_columns.1.refs_0_), channel_id=1, source_target_pairs={{0,32},{1,33},{2,34},{3,35},{4,36},{5,37},{6,38},{7,39},{8,40},{9,... | collective-permute-start | bytes 67592 | tf_op jit(solution)/shard_map/ppermute | solution.py:268
  11.9 0.8 %copy-start.1 = (f32[64,88]{1,0:T(8,128)S(1)}, f32[64,88]{1,0:T(8,128)}, u32[]{:S(2)}) copy-start(f32[64,88]{1,0:T(8,128)} %gather_columns.1.refs_0_) | copy-start | bytes 67588
  12.7 7.2 %collective-permute-start.2 = (f32[96,88]{1,0:T(8,128)S(1)}, f32[96,88]{1,0:T(8,128)S(1)}, u32[]{:S(2)}, u32[]{:S(2)}) collective-permute-start(f32[96,88]{1,0:T(8,128)S(1)} %get-tuple-element.24), channel_id=1, source_target_pairs={{0,16},{1,17},{2,18},{3,19},{4,20},{5,21},{6,22},{7,23},{8,24},{9,... | collective-permute-start | bytes 101384 | tf_op jit(solution)/shard_map/ppermute | solution.py:268
  16.7 5.3 %collective-permute-start.3 = (f32[96,88]{1,0:T(8,128)S(1)}, f32[96,88]{1,0:T(8,128)S(1)}, u32[]{:S(2)}, u32[]{:S(2)}) collective-permute-start(f32[96,88]{1,0:T(8,128)S(1)} %get-tuple-element.25), channel_id=1, source_target_pairs={{0,8},{1,9},{2,10},{3,11},{4,12},{5,13},{6,14},{7,15},{8,16},{9,17... | collective-permute-start | bytes 101384 | tf_op jit(solution)/shard_map/ppermute | solution.py:268
  17.7 4.3 %collective-permute-start.4 = (f32[96,88]{1,0:T(8,128)S(1)}, f32[96,88]{1,0:T(8,128)S(1)}, u32[]{:S(2)}, u32[]{:S(2)}) collective-permute-start(f32[96,88]{1,0:T(8,128)S(1)} %get-tuple-element.26), channel_id=1, source_target_pairs={{0,24},{1,25},{2,26},{3,27},{4,28},{5,29},{6,30},{7,31},{8,0},{9,1... | collective-permute-start | bytes 101384 | tf_op jit(solution)/shard_map/ppermute | solution.py:268
  22.0 5.1 %collective-permute-start.6 = (f32[144,88]{1,0:T(8,128)S(1)}, f32[144,88]{1,0:T(8,128)S(1)}, u32[]{:S(2)}, u32[]{:S(2)}) collective-permute-start(f32[144,88]{1,0:T(8,128)S(1)} %get-tuple-element.27.refs_0_), channel_id=1, source_target_pairs={{0,7},{1,2},{2,1},{3,4},{4,3},{5,6},{6,5},{7,0},{8,15},{9,10},{10,... | collective-permute-start | bytes 152072 | tf_op jit(solution)/shard_map/ppermute | solution.py:268
  22.1 5.0 %collective-permute-start.5 = (f32[144,88]{1,0:T(8,128)S(1)}, f32[144,88]{1,0:T(8,128)S(1)}, u32[]{:S(2)}, u32[]{:S(2)}) collective-permute-start(f32[144,88]{1,0:T(8,128)S(1)} %get-tuple-element.27.refs_0_), channel_id=1, source_target_pairs={{0,1},{1,0},{2,3},{3,2},{4,5},{5,4},{6,7},{7,6},{8,9},{9,8},{10,11... | collective-permute-start | bytes 152072 | tf_op jit(solution)/shard_map/ppermute | solution.py:268
  24.4 19.5 %copy-start = (f32[80,8192]{1,0:T(8,128)S(1)}, f32[80,8192]{1,0:T(8,128)}, u32[]{:S(2)}) copy-start(f32[80,8192]{1,0:T(8,128)} %refs_5_.1) | copy-start | bytes 7864324
  28.1 4.9 %collective-permute-start.8 = (f32[112,88]{1,0:T(8,128)S(1)}, f32[112,88]{1,0:T(8,128)S(1)}, u32[]{:S(2)}, u32[]{:S(2)}) collective-permute-start(f32[112,88]{1,0:T(8,128)S(1)} %get-tuple-element.31.refs_0_), channel_id=1, source_target_pairs={{0,7},{1,2},{2,1},{3,4},{4,3},{5,6},{6,5},{7,0},{8,15},{9,10},{10,... | collective-permute-start | bytes 118280 | tf_op jit(solution)/shard_map/ppermute | solution.py:268
  28.2 4.8 %collective-permute-start.7 = (f32[112,88]{1,0:T(8,128)S(1)}, f32[112,88]{1,0:T(8,128)S(1)}, u32[]{:S(2)}, u32[]{:S(2)}) collective-permute-start(f32[112,88]{1,0:T(8,128)S(1)} %get-tuple-element.31.refs_0_), channel_id=1, source_target_pairs={{0,1},{1,0},{2,3},{3,2},{4,5},{5,4},{6,7},{7,6},{8,9},{9,8},{10,11... | collective-permute-start | bytes 118280 | tf_op jit(solution)/shard_map/ppermute | solution.py:268
  33.9 4.7 %collective-permute-start.10 = (f32[80,88]{1,0:T(8,128)S(1)}, f32[80,88]{1,0:T(8,128)S(1)}, u32[]{:S(2)}, u32[]{:S(2)}) collective-permute-start(f32[80,88]{1,0:T(8,128)S(1)} %get-tuple-element.36.refs_0_), channel_id=1, source_target_pairs={{0,7},{1,2},{2,1},{3,4},{4,3},{5,6},{6,5},{7,0},{8,15},{9,10},{10,... | collective-permute-start | bytes 84488 | tf_op jit(solution)/shard_map/ppermute | solution.py:268
  34.0 4.6 %collective-permute-start.9 = (f32[80,88]{1,0:T(8,128)S(1)}, f32[80,88]{1,0:T(8,128)S(1)}, u32[]{:S(2)}, u32[]{:S(2)}) collective-permute-start(f32[80,88]{1,0:T(8,128)S(1)} %get-tuple-element.36.refs_0_), channel_id=1, source_target_pairs={{0,1},{1,0},{2,3},{3,2},{4,5},{5,4},{6,7},{7,6},{8,9},{9,8},{10,11... | collective-permute-start | bytes 84488 | tf_op jit(solution)/shard_map/ppermute | solution.py:268
  39.4 4.5 %collective-permute-start.12 = (f32[48,88]{1,0:T(8,128)S(1)}, f32[48,88]{1,0:T(8,128)S(1)}, u32[]{:S(2)}, u32[]{:S(2)}) collective-permute-start(f32[48,88]{1,0:T(8,128)S(1)} %get-tuple-element.40.refs_0_), channel_id=1, source_target_pairs={{0,7},{1,2},{2,1},{3,4},{4,3},{5,6},{6,5},{7,0},{8,15},{9,10},{10,... | collective-permute-start | bytes 50696 | tf_op jit(solution)/shard_map/ppermute | solution.py:268
  39.5 4.5 %collective-permute-start.11 = (f32[48,88]{1,0:T(8,128)S(1)}, f32[48,88]{1,0:T(8,128)S(1)}, u32[]{:S(2)}, u32[]{:S(2)}) collective-permute-start(f32[48,88]{1,0:T(8,128)S(1)} %get-tuple-element.40.refs_0_), channel_id=1, source_target_pairs={{0,1},{1,0},{2,3},{3,2},{4,5},{5,4},{6,7},{7,6},{8,9},{9,8},{10,11... | collective-permute-start | bytes 50696 | tf_op jit(solution)/shard_map/ppermute | solution.py:268

commit v3 on v2

--- a/solution.py
+++ b/solution.py
@@ -8,6 +8,7 @@
 BLK = 1024
 EPS = 1e-05
 ZN = 4
+SLAB = 16
 PAD = 8
 F32 = jnp.float32
 BF16 = jnp.bfloat16
@@ -53,14 +54,14 @@
     n = batches * slots
     small = [(loc_in, loc), (count_in, count), (value_in, values), (error_in, error)]
     copies = [pltpu.make_async_copy(src, dst, sems.at[k]) for k, (src, dst) in enumerate(small)]
-    for k in range(ens.shape[1] // BLK):
-        at = pl.ds(k * BLK, BLK)
-        copies.append(pltpu.make_async_copy(ens_in.at[:, at], ens.at[:, at], sems.at[4 + k]))
+    for k in range(members // SLAB):
+        at = pl.ds(k * SLAB, SLAB)
+        copies.append(pltpu.make_async_copy(ens_in.at[at], ens.at[at], sems.at[4 + k]))
     for copy in copies:
         copy.start()
     device = lax.axis_index("gx") * lax.axis_size("gy") + lax.axis_index("gy")
     first = device * (ens.shape[1] // BLK)
-    lane = lax.broadcasted_iota(jnp.int32, (members, 128), 1)
+    lane = lax.broadcasted_iota(jnp.int32, (SLAB, 128), 1)
     lane8 = lax.broadcasted_iota(jnp.int32, (PAD, 128), 1)
     row8 = lax.broadcasted_iota(jnp.int32, (PAD, 128), 0)
     side = jnp.zeros((PAD, 128), F32)
@@ -68,20 +69,28 @@
         copy.wait()
     for j in range(n):
         b, k = j // slots, j % slots
-        block = (first + loc[b, k] // BLK).astype(F32)
+        block = (first + lax.shift_right_logical(loc[b, k], BLK.bit_length() - 1)).astype(F32)
         live = jnp.where(k < count[0, b], 1.0, 0.0).astype(F32)
         new = jnp.where(
             row8 == 0, block, jnp.where(row8 == 1, values[b, k], jnp.where(row8 == 2, error[b, k], live))
         )
         side = jnp.where(lane8 == j, new, side)
-    for copy in copies[4:]:
-        copy.wait()
-    acc = jnp.zeros((members, 128), F32)
-    for j in range(n):
-        c = loc[j // slots, j % slots]
-        tile = ens[:, pl.ds(pl.multiple_of((c // 128) * 128, 128), 128)]
-        acc = jnp.where(lane == j, pltpu.roll(tile, (j - c % 128 + 128) % 128, 1), acc)
-    out[...] = jnp.transpose(jnp.concatenate([acc, side], axis=0))[:n]
+    pieces = []
+    for k in range(members // SLAB):
+        copies[4 + k].wait()
+        acc = jnp.zeros((SLAB, 128), F32)
+        for j in range(n):
+            c = loc[j // slots, j % slots]
+            tile = ens[k * SLAB : (k + 1) * SLAB, pl.ds(pl.multiple_of(c & -128, 128), 128)]
+            acc = jnp.where(lane == j, pltpu.roll(tile, (j - c) & 127, 1), acc)
+        pieces.append(acc)
+    out[...] = jnp.transpose(jnp.concatenate(pieces + [side], axis=0))[:n]
+
+
+def fetch_kernel(src, dst, sem):
+    copy = pltpu.make_async_copy(src, dst, sem.at[0])
+    copy.start()
+    copy.wait()
 
 
 def pack_kernel(blocks, weights, list_blocks, list_weights, coef):
@@ -237,21 +246,37 @@
         left[:, members:] = rows[k:, members:]
 
 
-def final_kernel(batch, slots, own, swapped, crossed, coef, maps, ens, out, result, sems):
+def stacked(maps, state):
+    mh, ml = split(maps)
+    xh, xl = state
+    left = jnp.concatenate([mh, ml, mh], axis=0)
+    right = jnp.concatenate([xh, xh, xl], axis=0)
+    return lax.dot_general(left, right, TN, preferred_element_type=F32)
+
+
+def early_kernel(maps, ens, state, high, low):
+    members = ens.shape[0]
+    eye = unit(members)
+    for k in range(maps.shape[0] // members):
+        at = slice(k * BLK, (k + 1) * BLK)
+        x = ens[:, at]
+        y = x + stacked(maps[k * members : (k + 1) * members] - eye, split(x))
+        state[:, at] = y
+        high[:, at], low[:, at] = split(y)
+
+
+def final_kernel(batch, slots, own, swapped, crossed, coef, state, high, low, out, result, sems):
     nb = coef.shape[1]
-    members = ens.shape[0]
     scaled, increment = observe(gathered(own, swapped, crossed, slots))
-    whole = compose(batch, maps[...], scaled, increment, coef)
-    eye = unit(members)
+    nobs, members = scaled.shape
+    turned = jnp.transpose(scaled)
+    increment = split(increment)
+    gains = [dot3(split(turned * coef[batch, k : k + 1, :nobs]), increment, NN) for k in range(nb)]
     copies = []
     for k in range(nb):
-        dh, dl = split(whole[k * members : (k + 1) * members] - eye)
-        x = ens[:, k * BLK : (k + 1) * BLK]
-        xh, xl = split(x)
-        left = jnp.concatenate([dh, dl, dh], axis=0)
-        right = jnp.concatenate([xh, xh, xl], axis=0)
+        at = slice(k * BLK, (k + 1) * BLK)
+        result[:, at] = state[:, at] + stacked(gains[k], (high[:, at], low[:, at]))
         at = pl.ds(k * BLK, BLK)
-        result[:, at] = x + lax.dot_general(left, right, TN, preferred_element_type=F32)
         copies.append(pltpu.make_async_copy(result.at[:, at], out.at[:, at], sems.at[k]))
         copies[-1].start()
     for copy in copies:
@@ -292,7 +317,7 @@
             pltpu.SMEM((batches, slots), F32),
             pltpu.SMEM((batches, slots), F32),
             pltpu.VMEM((members, rows_here), F32),
-            pltpu.SemaphoreType.DMA((4 + nb,)),
+            pltpu.SemaphoreType.DMA((4 + members // SLAB,)),
         ],
         compiler_params=pltpu.CompilerParams(vmem_limit_bytes=64 * 1024 * 1024 - 2**21),
         name="gather_columns",
@@ -315,6 +340,16 @@
 
     south = permute(own, lambda i, j: (i + ZN, j))
     north = permute(own, lambda i, j: (i - ZN, j))
+    own = pl.pallas_call(
+        fetch_kernel,
+        out_shape=shape(n, wide),
+        in_specs=[hbm],
+        out_specs=vm,
+        scratch_shapes=[pltpu.SemaphoreType.DMA((1,))],
+        compiler_params=params,
+        cost_estimate=cost(1),
+        name="fetch_own",
+    )(own)
     across, up, down = pl.pallas_call(
         lambda *refs: along_z_kernel(slots, *refs),
         out_shape=(shape(6 * slots, wide), shape(n + 2 * slots, wide), shape(n + 2 * slots, wide)),
@@ -386,15 +421,25 @@
         here, center_s, center_i = res[0], res[-2], res[-1]
         rest = None if last else res[1]
 
+    half = jax.ShapeDtypeStruct((members, rows_here), BF16)
+    state = pl.pallas_call(
+        early_kernel,
+        out_shape=(shape(members, rows_here), half, half),
+        in_specs=[vm] * 2,
+        out_specs=(vm,) * 3,
+        compiler_params=params,
+        cost_estimate=cost(1),
+        name="apply_early_maps",
+    )(maps, ensemble)
     return pl.pallas_call(
         lambda *refs: final_kernel(batches - 1, slots, *refs),
         out_shape=shape(members, rows_here),
-        in_specs=[vm] * 6,
+        in_specs=[vm] * 7,
         out_specs=hbm,
         scratch_shapes=[pltpu.VMEM((members, rows_here), F32), pltpu.SemaphoreType.DMA((nb,))],
         compiler_params=params,
         name="apply_maps",
-    )(here, swapped, crossed, coef, maps, ensemble)
+    )(here, swapped, crossed, coef, *state)
 
 
 def solution(mesh):

time: 47.2 us -> 45.5 us (0.964)
  waiting for transfers between devices: 19.6 us -> 17.5 us
    ppermute x13, waiting for transfers between devices: 19.6 us -> 17.5 us  [permute(): return lax.ppermute(x, ('gx', 'gy'), pairs)]
    pallas_call x0 -> x2, Pallas kernels: none -> 1.08 us  [the longest x1 1.06 us: shards(): pl.pallas_call(early_kernel, out_shape=(shape(members, rows_here), half,...]
    pallas_call x1, Pallas kernels: 3.14 us -> 2.5 us  [shards(): pl.pallas_call(lambda *refs: final_kernel(batches - 1, slots, *refs), out...]
    pallas_call x1, Pallas kernels: 3.42 us -> 2.89 us  [shards(): pl.pallas_call(gather_kernel, out_shape=shape(n, wide), in_specs=[hbm] *...]
  transfers between devices with their start and end apart: 13 -> 13, of which waited for: 7 -> 7; matrix products, arithmetic and copies ran while one was open for 0% -> 0% of each run, Pallas kernels for 9% -> 12%
where the time goes in v3:
time: 45.5 us; the launch traced here: 45.3 us
  waiting for transfers between devices  17.5 us (38%)
  Pallas kernels  13.6 us (30%)
  starting transfers between devices  13 us (29%)
  local copies, waits for them, and re-layouts  0.84 us (2%)
    ppermute x13, waiting for transfers between devices, permute(): return lax.ppermute(x, ('gx', 'gy'), pairs)  17.5 us
    ppermute x13, starting transfers between devices, permute(): return lax.ppermute(x, ('gx', 'gy'), pairs)  13 us
    pallas_call x3, Pallas kernels, shards(): pl.pallas_call(body, out_shape=shape(nb * members, members), in_specs=[vm...  3.39 us
    pallas_call x1, Pallas kernels, shards(): pl.pallas_call(gather_kernel, out_shape=shape(n, wide), in_specs=[hbm] *...  2.89 us
    pallas_call x3, Pallas kernels, shards(): pl.pallas_call(body, out_shape=tuple(outs), in_specs=[vm] * 5 + [tie] * l...  2.66 us
    pallas_call x1, Pallas kernels, shards(): pl.pallas_call(lambda *refs: final_kernel(batches - 1, slots, *refs), out...  2.5 us
    pallas_call x1, Pallas kernels, shards(): pl.pallas_call(early_kernel, out_shape=(shape(members, rows_here), half,...  1.06 us
  transfers between devices with their start and end apart: 13, of which 7 were waited for; matrix products, arithmetic and copies ran while one was open for 0% of the time, Pallas kernels for 12%

profile of v3, /device:TPU:0, one launch (start us, length us, event | category | flops | bytes accessed | tf_op | source)
XLA Modules:
  0.0 45.3 jit_solution(3278921450423255397)
XLA Ops:
  0.0 0.0 copy-start.2
  0.0 0.0 copy-start.1
  0.0 2.9 %gather_columns.1.src = f32[64,88]{1,0:T(8,128)} custom-call(s32[4,16]{1,0:T(4,128)} %loc_in.1, s32[1,4]{1,0:T(1,128)} %bitcast.1, f32[4,16]{1,0:T(4,128)} %value_in.1, f32[4,16]{1,0:T(4,128)} %error_in.1, f32[80,8192]{1,0:T(8,128)} %ens.1), custom_call_target="tpu_custom_call" | custom-call | tf_op jit(solution)/shard_map/gather_columns/pallas_call | solution.py:309
  2.9 3.2 %collective-permute-start.1 = (f32[64,88]{1,0:T(8,128)}, f32[64,88]{1,0:T(8,128)S(1)}, u32[]{:S(2)}, u32[]{:S(2)}) collective-permute-start(f32[64,88]{1,0:T(8,128)} %gather_columns.1.src), channel_id=1, source_target_pairs={{0,96},{1,97},{2,98},{3,99},{4,100},{5,101},{6,102},{7,103},{8,104... | collective-permute-start | bytes 67592 | tf_op jit(solution)/shard_map/ppermute | solution.py:293
  6.1 0.0 collective-permute-start
  6.1 0.0 copy-start.3
  6.1 0.8 %copy-done.3 = f32[64,88]{1,0:T(8,128)S(1)} copy-done((f32[64,88]{1,0:T(8,128)S(1)}, f32[64,88]{1,0:T(8,128)}, u32[]{:S(2)}) %copy-start.3) | copy-done | bytes 22552
  6.9 1.1 %collective-permute-done.1.refs_2_ = f32[64,88]{1,0:T(8,128)S(1)} collective-permute-done((f32[64,88]{1,0:T(8,128)}, f32[64,88]{1,0:T(8,128)S(1)}, u32[]{:S(2)}, u32[]{:S(2)}) %collective-permute-start.1) | collective-permute-done | bytes 22560 | tf_op jit(solution)/shard_map/ppermute | solution.py:293
  8.0 3.4 %collective-permute-done.refs_1_ = f32[64,88]{1,0:T(8,128)S(1)} collective-permute-done((f32[64,88]{1,0:T(8,128)}, f32[64,88]{1,0:T(8,128)S(1)}, u32[]{:S(2)}, u32[]{:S(2)}) %collective-permute-start) | collective-permute-done | bytes 22560 | tf_op jit(solution)/shard_map/ppermute | solution.py:293
  11.4 4.0 %collective-permute-start.2 = (f32[96,88]{1,0:T(8,128)S(1)}, f32[96,88]{1,0:T(8,128)S(1)}, u32[]{:S(2)}, u32[]{:S(2)}) collective-permute-start(f32[96,88]{1,0:T(8,128)S(1)} %get-tuple-element.27), channel_id=1, source_target_pairs={{0,16},{1,17},{2,18},{3,19},{4,20},{5,21},{6,22},{7,23},{8,24},{9,... | collective-permute-start | bytes 101384 | tf_op jit(solution)/shard_map/ppermute | solution.py:293
  15.4 1.0 %collective-permute-start.3 = (f32[96,88]{1,0:T(8,128)S(1)}, f32[96,88]{1,0:T(8,128)S(1)}, u32[]{:S(2)}, u32[]{:S(2)}) collective-permute-start(f32[96,88]{1,0:T(8,128)S(1)} %get-tuple-element.28), channel_id=1, source_target_pairs={{0,8},{1,9},{2,10},{3,11},{4,12},{5,13},{6,14},{7,15},{8,16},{9,17... | collective-permute-start | bytes 101384 | tf_op jit(solution)/shard_map/ppermute | solution.py:293
  16.4 2.2 %collective-permute-start.4 = (f32[96,88]{1,0:T(8,128)S(1)}, f32[96,88]{1,0:T(8,128)S(1)}, u32[]{:S(2)}, u32[]{:S(2)}) collective-permute-start(f32[96,88]{1,0:T(8,128)S(1)} %get-tuple-element.29), channel_id=1, source_target_pairs={{0,24},{1,25},{2,26},{3,27},{4,28},{5,29},{6,30},{7,31},{8,0},{9,1... | collective-permute-start | bytes 101384 | tf_op jit(solution)/shard_map/ppermute | solution.py:293
  18.6 0.0 collective-permute-done.2.refs_3_
  18.6 2.1 %collective-permute-done.3.refs_4_ = f32[96,88]{1,0:T(8,128)S(1)} collective-permute-done((f32[96,88]{1,0:T(8,128)S(1)}, f32[96,88]{1,0:T(8,128)S(1)}, u32[]{:S(2)}, u32[]{:S(2)}) %collective-permute-start.3) | collective-permute-done | bytes 33824 | tf_op jit(solution)/shard_map/ppermute | solution.py:293
  20.7 0.0 collective-permute-done.4.refs_5_
  20.7 0.1 collective-permute-start.6
  20.8 1.6 %collective-permute-start.5 = (f32[144,88]{1,0:T(8,128)S(1)}, f32[144,88]{1,0:T(8,128)S(1)}, u32[]{:S(2)}, u32[]{:S(2)}) collective-permute-start(f32[144,88]{1,0:T(8,128)S(1)} %get-tuple-element.30.refs_0_), channel_id=1, source_target_pairs={{0,1},{1,0},{2,3},{3,2},{4,5},{5,4},{6,7},{7,6},{8,9},{9,8},{10,11... | collective-permute-start | bytes 152072 | tf_op jit(solution)/shard_map/ppermute | solution.py:293
  22.4 0.0 copy-done.2
  22.4 0.0 copy-done.1
  22.4 0.2 pack_lists.1
  22.6 0.4 list_mask.3.refs_4_
  23.1 0.0 copy-start
  23.1 2.7 %collective-permute-done.6.refs_2_ = f32[144,88]{1,0:T(8,128)S(1)} collective-permute-done((f32[144,88]{1,0:T(8,128)S(1)}, f32[144,88]{1,0:T(8,128)S(1)}, u32[]{:S(2)}, u32[]{:S(2)}) %collective-permute-start.6) | collective-permute-done | bytes 50720 | tf_op jit(solution)/shard_map/ppermute | solution.py:293
  25.8 0.0 collective-permute-done.5.refs_1_
  25.8 1.0 %step_columns.3 = (f32[112,88]{1,0:T(8,128)S(1)}, f32[128,88]{1,0:T(8,128)S(1)}, f32[144,80]{1,0:T(8,128)S(1)}, f32[144,80]{1,0:T(8,128)S(1)}) custom-call(f32[144,88]{1,0:T(8,128)S(1)} %get-tuple-element.30.refs_0_, f32[144,88]{1,0:T(8,128)S(1)} %collective-permute-done.5.refs_1_, f32[144,88]{1,0:T(8,128)S(1)} %collective-permute-done.6.refs_2_, ...), custom_call_target="tpu_custom_call" | custom-call | tf_op jit(solution)/shard_map/step_columns/pallas_call | solution.py:413
  26.8 0.1 collective-permute-start.8
  26.9 0.4 collective-permute-start.7
  27.3 0.2 list_mask.4.refs_4_
  27.5 1.1 %compose_maps.3.refs_5_.r_0_ = f32[640,80]{1,0:T(8,128)S(1)} custom-call(f32[144,80]{1,0:T(8,128)S(1)} %get-tuple-element.36.s, f32[144,80]{1,0:T(8,128)S(1)} %get-tuple-element.37.i, f32[4,8,256]{2,1,0:T(8,128)S(1)} %get-tuple-element.38.c.refs_3_), custom_call_target="tpu_custom_call" | custom-call | flops 1000000 | bytes 100000 | tf_op jit(solution)/shard_map/compose_maps/pallas_call | solution.py:382
  28.6 3.1 %collective-permute-done.8.refs_2_ = f32[112,88]{1,0:T(8,128)S(1)} collective-permute-done((f32[112,88]{1,0:T(8,128)S(1)}, f32[112,88]{1,0:T(8,128)S(1)}, u32[]{:S(2)}, u32[]{:S(2)}) %collective-permute-start.8) | collective-permute-done | bytes 39456 | tf_op jit(solution)/shard_map/ppermute | solution.py:293
  31.7 0.0 collective-permute-done.7.refs_1_
  31.7 0.9 %step_columns.4 = (f32[80,88]{1,0:T(8,128)S(1)}, f32[48,88]{1,0:T(8,128)S(1)}, f32[144,80]{1,0:T(8,128)S(1)}, f32[144,80]{1,0:T(8,128)S(1)}) custom-call(f32[112,88]{1,0:T(8,128)S(1)} %get-tuple-element.34.refs_0_, f32[112,88]{1,0:T(8,128)S(1)} %collective-permute-done.7.refs_1_, f32[112,88]{1,0:T(8,128)S(1)} %collective-permute-done.8.refs_2_, ...), custom_call_target="tpu_custom_call" | custom-call | tf_op jit(solution)/shard_map/step_columns/pallas_call | solution.py:413
  32.6 0.1 collective-permute-start.10
  32.7 0.1 collective-permute-start.9
  32.8 0.1 list_mask.5.refs_4_
  32.9 1.1 %compose_maps.4.refs_5_.r_0_ = f32[640,80]{1,0:T(8,128)S(1)} custom-call(f32[144,80]{1,0:T(8,128)S(1)} %get-tuple-element.41.s, f32[144,80]{1,0:T(8,128)S(1)} %get-tuple-element.42.i, f32[4,8,256]{2,1,0:T(8,128)S(1)} %get-tuple-element.38.c.refs_3_, f32[640,80]{1,0:T(8,128)S(1)} %compose_maps.3.refs_5_.r_0_), custom_call_target="tpu_custom_call" | custom-call | flops 1000000 | bytes 100000 | tf_op jit(solution)/shard_map/compose_maps/pallas_call | solution.py:382
  34.0 3.3 %collective-permute-done.10.refs_2_ = f32[80,88]{1,0:T(8,128)S(1)} collective-permute-done((f32[80,88]{1,0:T(8,128)S(1)}, f32[80,88]{1,0:T(8,128)S(1)}, u32[]{:S(2)}, u32[]{:S(2)}) %collective-permute-start.10) | collective-permute-done | bytes 28192 | tf_op jit(solution)/shard_map/ppermute | solution.py:293
  37.3 0.0 collective-permute-done.9.refs_1_
  37.3 0.7 %step_columns.5 = (f32[48,88]{1,0:T(8,128)S(1)}, f32[144,80]{1,0:T(8,128)S(1)}, f32[144,80]{1,0:T(8,128)S(1)}) custom-call(f32[80,88]{1,0:T(8,128)S(1)} %get-tuple-element.39.refs_0_, f32[80,88]{1,0:T(8,128)S(1)} %collective-permute-done.9.refs_1_, f32[80,88]{1,0:T(8,128)S(1)} %collective-permute-done.10.refs_2_, ...), custom_call_target="tpu_custom_call" | custom-call | tf_op jit(solution)/shard_map/step_columns/pallas_call | solution.py:413
  38.1 0.1 collective-permute-start.12
  38.2 0.3 collective-permute-start.11
  38.4 1.1 %compose_maps.5.maps = f32[640,80]{1,0:T(8,128)S(1)} custom-call(f32[144,80]{1,0:T(8,128)S(1)} %get-tuple-element.44.s, f32[144,80]{1,0:T(8,128)S(1)} %get-tuple-element.45.i, f32[4,8,256]{2,1,0:T(8,128)S(1)} %get-tuple-element.38.c.refs_3_, f32[640,80]{1,0:T(8,128)S(1)} %compose_maps.4.refs_5_.r_0_), custom_call_target="tpu_custom_call" | custom-call | flops 1000000 | bytes 100000 | tf_op jit(solution)/shard_map/compose_maps/pallas_call | solution.py:382
  39.6 0.0 copy-done
  39.6 1.1 %apply_early_maps.1 = (f32[80,8192]{1,0:T(8,128)S(1)}, bf16[80,8192]{1,0:T(8,128)(2,1)S(1)}, bf16[80,8192]{1,0:T(8,128)(2,1)S(1)}) custom-call(f32[640,80]{1,0:T(8,128)S(1)} %compose_maps.5.maps, f32[80,8192]{1,0:T(8,128)S(1)} %copy-done), custom_call_target="tpu_custom_call" | custom-call | flops 1000000 | bytes 100000 | tf_op jit(solution)/shard_map/apply_early_maps/pallas_call | solution.py:425
  40.7 2.0 %collective-permute-done.12.refs_2_ = f32[48,88]{1,0:T(8,128)S(1)} collective-permute-done((f32[48,88]{1,0:T(8,128)S(1)}, f32[48,88]{1,0:T(8,128)S(1)}, u32[]{:S(2)}, u32[]{:S(2)}) %collective-permute-start.12) | collective-permute-done | bytes 16928 | tf_op jit(solution)/shard_map/ppermute | solution.py:293
  42.6 0.0 collective-permute-done.11.refs_1_
  42.6 2.5 %apply_maps.1 = f32[80,8192]{1,0:T(8,128)} custom-call(f32[48,88]{1,0:T(8,128)S(1)} %get-tuple-element.43.refs_0_, f32[48,88]{1,0:T(8,128)S(1)} %collective-permute-done.11.refs_1_, f32[48,88]{1,0:T(8,128)S(1)} %collective-permute-done.12.refs_2_, f32[4,8,256]{2,1,0:T(8,128)S(1)} %get-tuple-element.38.c.refs_3_, f32[80,8192]{1,0:T(8,128)S(1)} %get-tuple-element.46.refs_4_, ...), custom_call_target="tpu_custom_call" | custom-call | tf_op jit(solution)/shard_map/apply_maps/pallas_call | solution.py:434
  (3 shorter events, 0.1 us)
Async XLA Ops:
  0.0 22.4 %copy-start.2 = (f32[4,8,2048]{2,1,0:T(8,128)S(1)}, f32[4,8,2048]{2,1,0:T(8,128)}, u32[]{:S(2)}) copy-start(f32[4,8,2048]{2,1,0:T(8,128)} %weights.1) | copy-start | bytes 786436
  0.0 22.4 %copy-start.1 = (s32[4,8,2048]{2,1,0:T(8,128)S(1)}, s32[4,8,2048]{2,1,0:T(8,128)}, u32[]{:S(2)}) copy-start(s32[4,8,2048]{2,1,0:T(8,128)} %blocks.1) | copy-start | bytes 786436
  2.9 5.1 %collective-permute-start.1 = (f32[64,88]{1,0:T(8,128)}, f32[64,88]{1,0:T(8,128)S(1)}, u32[]{:S(2)}, u32[]{:S(2)}) collective-permute-start(f32[64,88]{1,0:T(8,128)} %gather_columns.1.src), channel_id=1, source_target_pairs={{0,96},{1,97},{2,98},{3,99},{4,100},{5,101},{6,102},{7,103},{8,104... | collective-permute-start | bytes 67592 | tf_op jit(solution)/shard_map/ppermute | solution.py:293
  6.1 5.3 %collective-permute-start = (f32[64,88]{1,0:T(8,128)}, f32[64,88]{1,0:T(8,128)S(1)}, u32[]{:S(2)}, u32[]{:S(2)}) collective-permute-start(f32[64,88]{1,0:T(8,128)} %gather_columns.1.src), channel_id=1, source_target_pairs={{0,32},{1,33},{2,34},{3,35},{4,36},{5,37},{6,38},{7,39},{8,40},{9,... | collective-permute-start | bytes 67592 | tf_op jit(solution)/shard_map/ppermute | solution.py:293
  6.1 0.8 %copy-start.3 = (f32[64,88]{1,0:T(8,128)S(1)}, f32[64,88]{1,0:T(8,128)}, u32[]{:S(2)}) copy-start(f32[64,88]{1,0:T(8,128)} %gather_columns.1.src) | copy-start | bytes 67588
  11.4 7.2 %collective-permute-start.2 = (f32[96,88]{1,0:T(8,128)S(1)}, f32[96,88]{1,0:T(8,128)S(1)}, u32[]{:S(2)}, u32[]{:S(2)}) collective-permute-start(f32[96,88]{1,0:T(8,128)S(1)} %get-tuple-element.27), channel_id=1, source_target_pairs={{0,16},{1,17},{2,18},{3,19},{4,20},{5,21},{6,22},{7,23},{8,24},{9,... | collective-permute-start | bytes 101384 | tf_op jit(solution)/shard_map/ppermute | solution.py:293
  15.4 5.3 %collective-permute-start.3 = (f32[96,88]{1,0:T(8,128)S(1)}, f32[96,88]{1,0:T(8,128)S(1)}, u32[]{:S(2)}, u32[]{:S(2)}) collective-permute-start(f32[96,88]{1,0:T(8,128)S(1)} %get-tuple-element.28), channel_id=1, source_target_pairs={{0,8},{1,9},{2,10},{3,11},{4,12},{5,13},{6,14},{7,15},{8,16},{9,17... | collective-permute-start | bytes 101384 | tf_op jit(solution)/shard_map/ppermute | solution.py:293
  16.4 4.3 %collective-permute-start.4 = (f32[96,88]{1,0:T(8,128)S(1)}, f32[96,88]{1,0:T(8,128)S(1)}, u32[]{:S(2)}, u32[]{:S(2)}) collective-permute-start(f32[96,88]{1,0:T(8,128)S(1)} %get-tuple-element.29), channel_id=1, source_target_pairs={{0,24},{1,25},{2,26},{3,27},{4,28},{5,29},{6,30},{7,31},{8,0},{9,1... | collective-permute-start | bytes 101384 | tf_op jit(solution)/shard_map/ppermute | solution.py:293
  20.7 5.1 %collective-permute-start.6 = (f32[144,88]{1,0:T(8,128)S(1)}, f32[144,88]{1,0:T(8,128)S(1)}, u32[]{:S(2)}, u32[]{:S(2)}) collective-permute-start(f32[144,88]{1,0:T(8,128)S(1)} %get-tuple-element.30.refs_0_), channel_id=1, source_target_pairs={{0,7},{1,2},{2,1},{3,4},{4,3},{5,6},{6,5},{7,0},{8,15},{9,10},{10,... | collective-permute-start | bytes 152072 | tf_op jit(solution)/shard_map/ppermute | solution.py:293
  20.8 5.0 %collective-permute-start.5 = (f32[144,88]{1,0:T(8,128)S(1)}, f32[144,88]{1,0:T(8,128)S(1)}, u32[]{:S(2)}, u32[]{:S(2)}) collective-permute-start(f32[144,88]{1,0:T(8,128)S(1)} %get-tuple-element.30.refs_0_), channel_id=1, source_target_pairs={{0,1},{1,0},{2,3},{3,2},{4,5},{5,4},{6,7},{7,6},{8,9},{9,8},{10,11... | collective-permute-start | bytes 152072 | tf_op jit(solution)/shard_map/ppermute | solution.py:293
  23.1 16.5 %copy-start = (f32[80,8192]{1,0:T(8,128)S(1)}, f32[80,8192]{1,0:T(8,128)}, u32[]{:S(2)}) copy-start(f32[80,8192]{1,0:T(8,128)} %ens.1) | copy-start | bytes 7864324
  26.8 4.9 %collective-permute-start.8 = (f32[112,88]{1,0:T(8,128)S(1)}, f32[112,88]{1,0:T(8,128)S(1)}, u32[]{:S(2)}, u32[]{:S(2)}) collective-permute-start(f32[112,88]{1,0:T(8,128)S(1)} %get-tuple-element.34.refs_0_), channel_id=1, source_target_pairs={{0,7},{1,2},{2,1},{3,4},{4,3},{5,6},{6,5},{7,0},{8,15},{9,10},{10,... | collective-permute-start | bytes 118280 | tf_op jit(solution)/shard_map/ppermute | solution.py:293
  26.9 4.8 %collective-permute-start.7 = (f32[112,88]{1,0:T(8,128)S(1)}, f32[112,88]{1,0:T(8,128)S(1)}, u32[]{:S(2)}, u32[]{:S(2)}) collective-permute-start(f32[112,88]{1,0:T(8,128)S(1)} %get-tuple-element.34.refs_0_), channel_id=1, source_target_pairs={{0,1},{1,0},{2,3},{3,2},{4,5},{5,4},{6,7},{7,6},{8,9},{9,8},{10,11... | collective-permute-start | bytes 118280 | tf_op jit(solution)/shard_map/ppermute | solution.py:293
  32.6 4.7 %collective-permute-start.10 = (f32[80,88]{1,0:T(8,128)S(1)}, f32[80,88]{1,0:T(8,128)S(1)}, u32[]{:S(2)}, u32[]{:S(2)}) collective-permute-start(f32[80,88]{1,0:T(8,128)S(1)} %get-tuple-element.39.refs_0_), channel_id=1, source_target_pairs={{0,7},{1,2},{2,1},{3,4},{4,3},{5,6},{6,5},{7,0},{8,15},{9,10},{10,... | collective-permute-start | bytes 84488 | tf_op jit(solution)/shard_map/ppermute | solution.py:293
  32.7 4.6 %collective-permute-start.9 = (f32[80,88]{1,0:T(8,128)S(1)}, f32[80,88]{1,0:T(8,128)S(1)}, u32[]{:S(2)}, u32[]{:S(2)}) collective-permute-start(f32[80,88]{1,0:T(8,128)S(1)} %get-tuple-element.39.refs_0_), channel_id=1, source_target_pairs={{0,1},{1,0},{2,3},{3,2},{4,5},{5,4},{6,7},{7,6},{8,9},{9,8},{10,11... | collective-permute-start | bytes 84488 | tf_op jit(solution)/shard_map/ppermute | solution.py:293
  38.1 4.5 %collective-permute-start.12 = (f32[48,88]{1,0:T(8,128)S(1)}, f32[48,88]{1,0:T(8,128)S(1)}, u32[]{:S(2)}, u32[]{:S(2)}) collective-permute-start(f32[48,88]{1,0:T(8,128)S(1)} %get-tuple-element.43.refs_0_), channel_id=1, source_target_pairs={{0,7},{1,2},{2,1},{3,4},{4,3},{5,6},{6,5},{7,0},{8,15},{9,10},{10,... | collective-permute-start | bytes 50696 | tf_op jit(solution)/shard_map/ppermute | solution.py:293
  38.2 4.5 %collective-permute-start.11 = (f32[48,88]{1,0:T(8,128)S(1)}, f32[48,88]{1,0:T(8,128)S(1)}, u32[]{:S(2)}, u32[]{:S(2)}) collective-permute-start(f32[48,88]{1,0:T(8,128)S(1)} %get-tuple-element.43.refs_0_), channel_id=1, source_target_pairs={{0,1},{1,0},{2,3},{3,2},{4,5},{5,4},{6,7},{7,6},{8,9},{9,8},{10,11... | collective-permute-start | bytes 50696 | tf_op jit(solution)/shard_map/ppermute | solution.py:293

commit v4 on v3

--- a/solution.py
+++ b/solution.py
@@ -137,20 +137,31 @@
             coef[b, :, t * 128 : (t + 1) * 128] = held_c[t]
 
 
-def along_z_kernel(slots, own, south, north, across, up, down):
-    z = lax.axis_index("gx") % ZN
-    mine, below, above = own[...], south[...], north[...]
-    n = mine.shape[0]
-    up[:n] = jnp.where(z == ZN - 1, below, mine)
-    up[n:] = jnp.where(z == ZN - 1, mine, above)[: 2 * slots]
-    down[:n] = jnp.where(z == 0, above, mine)
-    down[n:] = jnp.where(z == 0, mine, below)[: 2 * slots]
+def by_parity(odd, a, b):
+    return jnp.where(odd, b, a), jnp.where(odd, a, b)
+
+
+def along_z_kernel(slots, own, inner, outer, across, away, beside):
+    gx = lax.axis_index("gx")
+    z, odd_y = gx % ZN, gx // ZN % 2 == 1
+    mine = own[...]
+    above, below = by_parity(odd_y, inner[...], outer[...])
+    up = jnp.concatenate(
+        [jnp.where(z == ZN - 1, below, mine), jnp.where(z == ZN - 1, mine, above)[: 2 * slots]], axis=0
+    )
+    down = jnp.concatenate(
+        [jnp.where(z == 0, above, mine), jnp.where(z == 0, mine, below)[: 2 * slots]], axis=0
+    )
     across[: 3 * slots] = jnp.where(z < 2, mine, below)[: 3 * slots]
     across[3 * slots :] = jnp.where(z < 2, above, mine)[: 3 * slots]
-
-
-def window_kernel(batches, slots, own, south, north, across, up, down, first, rest):
+    beside[...], away[...] = by_parity(z % 2 == 1, up, down)
+
+
+def window_kernel(batches, slots, own, inner, outer, across, away, beside, first, rest):
     n = batches * slots
+    gx = lax.axis_index("gx")
+    north, south = by_parity(gx // ZN % 2 == 1, inner[:slots], outer[:slots])
+    down, up = by_parity(gx % 2 == 1, beside[...], away[...])
     source = {
         0: (own, 0),
         -4: (south, 0),
@@ -338,8 +349,12 @@
         name="pack_lists",
     )(blocks, weights)
 
-    south = permute(own, lambda i, j: (i + ZN, j))
-    north = permute(own, lambda i, j: (i - ZN, j))
+    pair_y = lambda odd: (lambda i, j: (i + ZN if (i // ZN + odd) % 2 == 0 else i - ZN, j))
+    pair_z = lambda odd: (
+        lambda i, j: (i // ZN * ZN + (i + (1 if (i + odd) % 2 == 0 else ZN - 1)) % ZN, j)
+    )
+    outer = permute(own, pair_y(1))
+    inner = permute(own, pair_y(0))
     own = pl.pallas_call(
         fetch_kernel,
         out_shape=shape(n, wide),
@@ -350,18 +365,17 @@
         cost_estimate=cost(1),
         name="fetch_own",
     )(own)
-    across, up, down = pl.pallas_call(
+    across, away, beside = pl.pallas_call(
         lambda *refs: along_z_kernel(slots, *refs),
         out_shape=(shape(6 * slots, wide), shape(n + 2 * slots, wide), shape(n + 2 * slots, wide)),
         in_specs=[vm] * 3,
         out_specs=(vm,) * 3,
         compiler_params=params,
         name="select_along_z",
-    )(own, south, north)
-    turn = lambda k: (lambda i, j: (i // ZN * ZN + (i + k) % ZN, j))
-    across = permute(across, turn(2))
-    up = permute(up, turn(1))
-    down = permute(down, turn(ZN - 1))
+    )(own, inner, outer)
+    across = permute(across, lambda i, j: (i // ZN * ZN + (i + 2) % ZN, j))
+    away = permute(away, pair_z(1))
+    beside = permute(beside, pair_z(0))
     total = sum(width(b, batches) for b in range(1, batches)) * slots
     here, rest = pl.pallas_call(
         lambda *refs: window_kernel(batches, slots, *refs),
@@ -370,7 +384,7 @@
         out_specs=(vm, vm),
         compiler_params=params,
         name="lay_out_window",
-    )(own, south, north, across, up, down)
+    )(own, inner, outer, across, away, beside)
 
     maps = None
     for b in range(batches):

time: 45.5 us -> 44.3 us (0.974)
  starting transfers between devices: 13 us -> 11 us
  waiting for transfers between devices: 17.5 us -> 18.4 us
    ppermute x13, starting transfers between devices: 13 us -> 11 us  [permute(): return lax.ppermute(x, ('gx', 'gy'), pairs)]
    ppermute x13, waiting for transfers between devices: 17.5 us -> 18.4 us  [permute(): return lax.ppermute(x, ('gx', 'gy'), pairs)]
  transfers between devices with their start and end apart: 13 -> 13, of which waited for: 7 -> 8; matrix products, arithmetic and copies ran while one was open for 0% -> 0% of each run, Pallas kernels for 12% -> 12%
where the time goes in v4:
time: 44.3 us; the launch traced here: 44.1 us
  waiting for transfers between devices  18.4 us (42%)
  Pallas kernels  13.6 us (31%)
  starting transfers between devices  11 us (25%)
  local copies, waits for them, and re-layouts  0.8 us (2%)
    ppermute x13, waiting for transfers between devices, permute(): return lax.ppermute(x, ('gx', 'gy'), pairs)  18.4 us
    ppermute x13, starting transfers between devices, permute(): return lax.ppermute(x, ('gx', 'gy'), pairs)  11 us
    pallas_call x3, Pallas kernels, shards(): pl.pallas_call(body, out_shape=shape(nb * members, members), in_specs=[vm...  3.4 us
    pallas_call x1, Pallas kernels, shards(): pl.pallas_call(gather_kernel, out_shape=shape(n, wide), in_specs=[hbm] *...  2.89 us
    pallas_call x3, Pallas kernels, shards(): pl.pallas_call(body, out_shape=tuple(outs), in_specs=[vm] * 5 + [tie] * l...  2.66 us
    pallas_call x1, Pallas kernels, shards(): pl.pallas_call(lambda *refs: final_kernel(batches - 1, slots, *refs), out...  2.5 us
    pallas_call x1, Pallas kernels, shards(): pl.pallas_call(early_kernel, out_shape=(shape(members, rows_here), half,...  1.06 us
  transfers between devices with their start and end apart: 13, of which 8 were waited for; matrix products, arithmetic and copies ran while one was open for 0% of the time, Pallas kernels for 12%

profile of v4, /device:TPU:0, one launch (start us, length us, event | category | flops | bytes accessed | tf_op | source)
XLA Modules:
  0.0 44.1 jit_solution(6322301305879879073)
XLA Ops:
  0.0 0.0 copy-start.2
  0.0 0.0 copy-start.1
  0.0 2.9 %gather_columns.1.src = f32[64,88]{1,0:T(8,128)} custom-call(s32[4,16]{1,0:T(4,128)} %loc_in.1, s32[1,4]{1,0:T(1,128)} %bitcast.1, f32[4,16]{1,0:T(4,128)} %value_in.1, f32[4,16]{1,0:T(4,128)} %error_in.1, f32[80,8192]{1,0:T(8,128)} %ens.1), custom_call_target="tpu_custom_call" | custom-call | tf_op jit(solution)/shard_map/gather_columns/pallas_call | solution.py:320
  2.9 3.2 %collective-permute-start.1 = (f32[64,88]{1,0:T(8,128)}, f32[64,88]{1,0:T(8,128)S(1)}, u32[]{:S(2)}, u32[]{:S(2)}) collective-permute-start(f32[64,88]{1,0:T(8,128)} %gather_columns.1.src), channel_id=1, source_target_pairs={{0,96},{1,97},{2,98},{3,99},{4,100},{5,101},{6,102},{7,103},{8,104... | collective-permute-start | bytes 67592 | tf_op jit(solution)/shard_map/ppermute | solution.py:304
  6.1 0.1 collective-permute-start
  6.2 0.0 copy-start.3
  6.2 0.8 %copy-done.3 = f32[64,88]{1,0:T(8,128)S(1)} copy-done((f32[64,88]{1,0:T(8,128)S(1)}, f32[64,88]{1,0:T(8,128)}, u32[]{:S(2)}) %copy-start.3) | copy-done | bytes 22552
  7.0 1.3 %collective-permute-done.1.refs_2_ = f32[64,88]{1,0:T(8,128)S(1)} collective-permute-done((f32[64,88]{1,0:T(8,128)}, f32[64,88]{1,0:T(8,128)S(1)}, u32[]{:S(2)}, u32[]{:S(2)}) %collective-permute-start.1) | collective-permute-done | bytes 22560 | tf_op jit(solution)/shard_map/ppermute | solution.py:304
  8.3 1.9 %collective-permute-done.refs_1_ = f32[64,88]{1,0:T(8,128)S(1)} collective-permute-done((f32[64,88]{1,0:T(8,128)}, f32[64,88]{1,0:T(8,128)S(1)}, u32[]{:S(2)}, u32[]{:S(2)}) %collective-permute-start) | collective-permute-done | bytes 22560 | tf_op jit(solution)/shard_map/ppermute | solution.py:304
  10.2 4.0 %collective-permute-start.2 = (f32[96,88]{1,0:T(8,128)S(1)}, f32[96,88]{1,0:T(8,128)S(1)}, u32[]{:S(2)}, u32[]{:S(2)}) collective-permute-start(f32[96,88]{1,0:T(8,128)S(1)} %get-tuple-element.27), channel_id=1, source_target_pairs={{0,16},{1,17},{2,18},{3,19},{4,20},{5,21},{6,22},{7,23},{8,24},{9,... | collective-permute-start | bytes 101384 | tf_op jit(solution)/shard_map/ppermute | solution.py:304
  14.2 0.7 %collective-permute-start.3 = (f32[96,88]{1,0:T(8,128)S(1)}, f32[96,88]{1,0:T(8,128)S(1)}, u32[]{:S(2)}, u32[]{:S(2)}) collective-permute-start(f32[96,88]{1,0:T(8,128)S(1)} %get-tuple-element.28), channel_id=1, source_target_pairs={{0,24},{1,25},{2,26},{3,27},{4,28},{5,29},{6,30},{7,31},{8,16},{9,... | collective-permute-start | bytes 101384 | tf_op jit(solution)/shard_map/ppermute | solution.py:304
  14.9 0.3 collective-permute-start.4
  15.2 1.1 %collective-permute-done.2.refs_3_ = f32[96,88]{1,0:T(8,128)S(1)} collective-permute-done((f32[96,88]{1,0:T(8,128)S(1)}, f32[96,88]{1,0:T(8,128)S(1)}, u32[]{:S(2)}, u32[]{:S(2)}) %collective-permute-start.2) | collective-permute-done | bytes 33824 | tf_op jit(solution)/shard_map/ppermute | solution.py:304
  16.3 3.2 %collective-permute-done.3.refs_4_ = f32[96,88]{1,0:T(8,128)S(1)} collective-permute-done((f32[96,88]{1,0:T(8,128)S(1)}, f32[96,88]{1,0:T(8,128)S(1)}, u32[]{:S(2)}, u32[]{:S(2)}) %collective-permute-start.3) | collective-permute-done | bytes 33824 | tf_op jit(solution)/shard_map/ppermute | solution.py:304
  19.5 0.0 collective-permute-done.4.refs_5_
  19.5 0.1 collective-permute-start.6
  19.6 1.6 %collective-permute-start.5 = (f32[144,88]{1,0:T(8,128)S(1)}, f32[144,88]{1,0:T(8,128)S(1)}, u32[]{:S(2)}, u32[]{:S(2)}) collective-permute-start(f32[144,88]{1,0:T(8,128)S(1)} %get-tuple-element.30.refs_0_), channel_id=1, source_target_pairs={{0,1},{1,0},{2,3},{3,2},{4,5},{5,4},{6,7},{7,6},{8,9},{9,8},{10,11... | collective-permute-start | bytes 152072 | tf_op jit(solution)/shard_map/ppermute | solution.py:304
  21.2 0.0 copy-done.2
  21.2 0.0 copy-done.1
  21.2 0.2 pack_lists.1
  21.5 0.4 list_mask.3.refs_4_
  21.9 0.0 copy-start
  21.9 2.7 %collective-permute-done.6.refs_2_ = f32[144,88]{1,0:T(8,128)S(1)} collective-permute-done((f32[144,88]{1,0:T(8,128)S(1)}, f32[144,88]{1,0:T(8,128)S(1)}, u32[]{:S(2)}, u32[]{:S(2)}) %collective-permute-start.6) | collective-permute-done | bytes 50720 | tf_op jit(solution)/shard_map/ppermute | solution.py:304
  24.6 0.0 collective-permute-done.5.refs_1_
  24.6 1.0 %step_columns.3 = (f32[112,88]{1,0:T(8,128)S(1)}, f32[128,88]{1,0:T(8,128)S(1)}, f32[144,80]{1,0:T(8,128)S(1)}, f32[144,80]{1,0:T(8,128)S(1)}) custom-call(f32[144,88]{1,0:T(8,128)S(1)} %get-tuple-element.30.refs_0_, f32[144,88]{1,0:T(8,128)S(1)} %collective-permute-done.5.refs_1_, f32[144,88]{1,0:T(8,128)S(1)} %collective-permute-done.6.refs_2_, ...), custom_call_target="tpu_custom_call" | custom-call | tf_op jit(solution)/shard_map/step_columns/pallas_call | solution.py:427
  25.6 0.1 collective-permute-start.8
  25.7 0.4 collective-permute-start.7
  26.1 0.2 list_mask.4.refs_4_
  26.3 1.1 %compose_maps.3.refs_5_.r_0_ = f32[640,80]{1,0:T(8,128)S(1)} custom-call(f32[144,80]{1,0:T(8,128)S(1)} %get-tuple-element.36.s, f32[144,80]{1,0:T(8,128)S(1)} %get-tuple-element.37.i, f32[4,8,256]{2,1,0:T(8,128)S(1)} %get-tuple-element.38.c.refs_3_), custom_call_target="tpu_custom_call" | custom-call | flops 1000000 | bytes 100000 | tf_op jit(solution)/shard_map/compose_maps/pallas_call | solution.py:396
  27.4 3.1 %collective-permute-done.8.refs_2_ = f32[112,88]{1,0:T(8,128)S(1)} collective-permute-done((f32[112,88]{1,0:T(8,128)S(1)}, f32[112,88]{1,0:T(8,128)S(1)}, u32[]{:S(2)}, u32[]{:S(2)}) %collective-permute-start.8) | collective-permute-done | bytes 39456 | tf_op jit(solution)/shard_map/ppermute | solution.py:304
  30.5 0.0 collective-permute-done.7.refs_1_
  30.5 0.9 %step_columns.4 = (f32[80,88]{1,0:T(8,128)S(1)}, f32[48,88]{1,0:T(8,128)S(1)}, f32[144,80]{1,0:T(8,128)S(1)}, f32[144,80]{1,0:T(8,128)S(1)}) custom-call(f32[112,88]{1,0:T(8,128)S(1)} %get-tuple-element.34.refs_0_, f32[112,88]{1,0:T(8,128)S(1)} %collective-permute-done.7.refs_1_, f32[112,88]{1,0:T(8,128)S(1)} %collective-permute-done.8.refs_2_, ...), custom_call_target="tpu_custom_call" | custom-call | tf_op jit(solution)/shard_map/step_columns/pallas_call | solution.py:427
  31.4 0.1 collective-permute-start.10
  31.5 0.1 collective-permute-start.9
  31.6 0.1 list_mask.5.refs_4_
  31.7 1.1 %compose_maps.4.refs_5_.r_0_ = f32[640,80]{1,0:T(8,128)S(1)} custom-call(f32[144,80]{1,0:T(8,128)S(1)} %get-tuple-element.41.s, f32[144,80]{1,0:T(8,128)S(1)} %get-tuple-element.42.i, f32[4,8,256]{2,1,0:T(8,128)S(1)} %get-tuple-element.38.c.refs_3_, f32[640,80]{1,0:T(8,128)S(1)} %compose_maps.3.refs_5_.r_0_), custom_call_target="tpu_custom_call" | custom-call | flops 1000000 | bytes 100000 | tf_op jit(solution)/shard_map/compose_maps/pallas_call | solution.py:396
  32.9 3.3 %collective-permute-done.10.refs_2_ = f32[80,88]{1,0:T(8,128)S(1)} collective-permute-done((f32[80,88]{1,0:T(8,128)S(1)}, f32[80,88]{1,0:T(8,128)S(1)}, u32[]{:S(2)}, u32[]{:S(2)}) %collective-permute-start.10) | collective-permute-done | bytes 28192 | tf_op jit(solution)/shard_map/ppermute | solution.py:304
  36.1 0.0 collective-permute-done.9.refs_1_
  36.1 0.7 %step_columns.5 = (f32[48,88]{1,0:T(8,128)S(1)}, f32[144,80]{1,0:T(8,128)S(1)}, f32[144,80]{1,0:T(8,128)S(1)}) custom-call(f32[80,88]{1,0:T(8,128)S(1)} %get-tuple-element.39.refs_0_, f32[80,88]{1,0:T(8,128)S(1)} %collective-permute-done.9.refs_1_, f32[80,88]{1,0:T(8,128)S(1)} %collective-permute-done.10.refs_2_, ...), custom_call_target="tpu_custom_call" | custom-call | tf_op jit(solution)/shard_map/step_columns/pallas_call | solution.py:427
  36.9 0.1 collective-permute-start.12
  37.0 0.3 collective-permute-start.11
  37.3 1.1 %compose_maps.5.maps = f32[640,80]{1,0:T(8,128)S(1)} custom-call(f32[144,80]{1,0:T(8,128)S(1)} %get-tuple-element.44.s, f32[144,80]{1,0:T(8,128)S(1)} %get-tuple-element.45.i, f32[4,8,256]{2,1,0:T(8,128)S(1)} %get-tuple-element.38.c.refs_3_, f32[640,80]{1,0:T(8,128)S(1)} %compose_maps.4.refs_5_.r_0_), custom_call_target="tpu_custom_call" | custom-call | flops 1000000 | bytes 100000 | tf_op jit(solution)/shard_map/compose_maps/pallas_call | solution.py:396
  38.4 0.0 copy-done
  38.4 1.1 %apply_early_maps.1 = (f32[80,8192]{1,0:T(8,128)S(1)}, bf16[80,8192]{1,0:T(8,128)(2,1)S(1)}, bf16[80,8192]{1,0:T(8,128)(2,1)S(1)}) custom-call(f32[640,80]{1,0:T(8,128)S(1)} %compose_maps.5.maps, f32[80,8192]{1,0:T(8,128)S(1)} %copy-done), custom_call_target="tpu_custom_call" | custom-call | flops 1000000 | bytes 100000 | tf_op jit(solution)/shard_map/apply_early_maps/pallas_call | solution.py:439
  39.5 2.0 %collective-permute-done.12.refs_2_ = f32[48,88]{1,0:T(8,128)S(1)} collective-permute-done((f32[48,88]{1,0:T(8,128)S(1)}, f32[48,88]{1,0:T(8,128)S(1)}, u32[]{:S(2)}, u32[]{:S(2)}) %collective-permute-start.12) | collective-permute-done | bytes 16928 | tf_op jit(solution)/shard_map/ppermute | solution.py:304
  41.4 0.0 collective-permute-done.11.refs_1_
  41.4 2.5 %apply_maps.1 = f32[80,8192]{1,0:T(8,128)} custom-call(f32[48,88]{1,0:T(8,128)S(1)} %get-tuple-element.43.refs_0_, f32[48,88]{1,0:T(8,128)S(1)} %collective-permute-done.11.refs_1_, f32[48,88]{1,0:T(8,128)S(1)} %collective-permute-done.12.refs_2_, f32[4,8,256]{2,1,0:T(8,128)S(1)} %get-tuple-element.38.c.refs_3_, f32[80,8192]{1,0:T(8,128)S(1)} %get-tuple-element.46.refs_4_, ...), custom_call_target="tpu_custom_call" | custom-call | tf_op jit(solution)/shard_map/apply_maps/pallas_call | solution.py:448
  (3 shorter events, 0.1 us)
Async XLA Ops:
  0.0 21.2 %copy-start.2 = (f32[4,8,2048]{2,1,0:T(8,128)S(1)}, f32[4,8,2048]{2,1,0:T(8,128)}, u32[]{:S(2)}) copy-start(f32[4,8,2048]{2,1,0:T(8,128)} %weights.1) | copy-start | bytes 786436
  0.0 21.2 %copy-start.1 = (s32[4,8,2048]{2,1,0:T(8,128)S(1)}, s32[4,8,2048]{2,1,0:T(8,128)}, u32[]{:S(2)}) copy-start(s32[4,8,2048]{2,1,0:T(8,128)} %blocks.1) | copy-start | bytes 786436
  2.9 5.4 %collective-permute-start.1 = (f32[64,88]{1,0:T(8,128)}, f32[64,88]{1,0:T(8,128)S(1)}, u32[]{:S(2)}, u32[]{:S(2)}) collective-permute-start(f32[64,88]{1,0:T(8,128)} %gather_columns.1.src), channel_id=1, source_target_pairs={{0,96},{1,97},{2,98},{3,99},{4,100},{5,101},{6,102},{7,103},{8,104... | collective-permute-start | bytes 67592 | tf_op jit(solution)/shard_map/ppermute | solution.py:304
  6.1 4.1 %collective-permute-start = (f32[64,88]{1,0:T(8,128)}, f32[64,88]{1,0:T(8,128)S(1)}, u32[]{:S(2)}, u32[]{:S(2)}) collective-permute-start(f32[64,88]{1,0:T(8,128)} %gather_columns.1.src), channel_id=1, source_target_pairs={{0,32},{1,33},{2,34},{3,35},{4,36},{5,37},{6,38},{7,39},{8,40},{9,... | collective-permute-start | bytes 67592 | tf_op jit(solution)/shard_map/ppermute | solution.py:304
  6.2 0.8 %copy-start.3 = (f32[64,88]{1,0:T(8,128)S(1)}, f32[64,88]{1,0:T(8,128)}, u32[]{:S(2)}) copy-start(f32[64,88]{1,0:T(8,128)} %gather_columns.1.src) | copy-start | bytes 67588
  10.2 6.0 %collective-permute-start.2 = (f32[96,88]{1,0:T(8,128)S(1)}, f32[96,88]{1,0:T(8,128)S(1)}, u32[]{:S(2)}, u32[]{:S(2)}) collective-permute-start(f32[96,88]{1,0:T(8,128)S(1)} %get-tuple-element.27), channel_id=1, source_target_pairs={{0,16},{1,17},{2,18},{3,19},{4,20},{5,21},{6,22},{7,23},{8,24},{9,... | collective-permute-start | bytes 101384 | tf_op jit(solution)/shard_map/ppermute | solution.py:304
  14.2 5.3 %collective-permute-start.3 = (f32[96,88]{1,0:T(8,128)S(1)}, f32[96,88]{1,0:T(8,128)S(1)}, u32[]{:S(2)}, u32[]{:S(2)}) collective-permute-start(f32[96,88]{1,0:T(8,128)S(1)} %get-tuple-element.28), channel_id=1, source_target_pairs={{0,24},{1,25},{2,26},{3,27},{4,28},{5,29},{6,30},{7,31},{8,16},{9,... | collective-permute-start | bytes 101384 | tf_op jit(solution)/shard_map/ppermute | solution.py:304
  14.9 4.6 %collective-permute-start.4 = (f32[96,88]{1,0:T(8,128)S(1)}, f32[96,88]{1,0:T(8,128)S(1)}, u32[]{:S(2)}, u32[]{:S(2)}) collective-permute-start(f32[96,88]{1,0:T(8,128)S(1)} %get-tuple-element.29), channel_id=1, source_target_pairs={{0,8},{1,9},{2,10},{3,11},{4,12},{5,13},{6,14},{7,15},{8,0},{9,1},... | collective-permute-start | bytes 101384 | tf_op jit(solution)/shard_map/ppermute | solution.py:304
  19.5 5.1 %collective-permute-start.6 = (f32[144,88]{1,0:T(8,128)S(1)}, f32[144,88]{1,0:T(8,128)S(1)}, u32[]{:S(2)}, u32[]{:S(2)}) collective-permute-start(f32[144,88]{1,0:T(8,128)S(1)} %get-tuple-element.30.refs_0_), channel_id=1, source_target_pairs={{0,7},{1,2},{2,1},{3,4},{4,3},{5,6},{6,5},{7,0},{8,15},{9,10},{10,... | collective-permute-start | bytes 152072 | tf_op jit(solution)/shard_map/ppermute | solution.py:304
  19.6 5.0 %collective-permute-start.5 = (f32[144,88]{1,0:T(8,128)S(1)}, f32[144,88]{1,0:T(8,128)S(1)}, u32[]{:S(2)}, u32[]{:S(2)}) collective-permute-start(f32[144,88]{1,0:T(8,128)S(1)} %get-tuple-element.30.refs_0_), channel_id=1, source_target_pairs={{0,1},{1,0},{2,3},{3,2},{4,5},{5,4},{6,7},{7,6},{8,9},{9,8},{10,11... | collective-permute-start | bytes 152072 | tf_op jit(solution)/shard_map/ppermute | solution.py:304
  21.9 16.5 %copy-start = (f32[80,8192]{1,0:T(8,128)S(1)}, f32[80,8192]{1,0:T(8,128)}, u32[]{:S(2)}) copy-start(f32[80,8192]{1,0:T(8,128)} %ens.1) | copy-start | bytes 7864324
  25.6 4.9 %collective-permute-start.8 = (f32[112,88]{1,0:T(8,128)S(1)}, f32[112,88]{1,0:T(8,128)S(1)}, u32[]{:S(2)}, u32[]{:S(2)}) collective-permute-start(f32[112,88]{1,0:T(8,128)S(1)} %get-tuple-element.34.refs_0_), channel_id=1, source_target_pairs={{0,7},{1,2},{2,1},{3,4},{4,3},{5,6},{6,5},{7,0},{8,15},{9,10},{10,... | collective-permute-start | bytes 118280 | tf_op jit(solution)/shard_map/ppermute | solution.py:304
  25.7 4.8 %collective-permute-start.7 = (f32[112,88]{1,0:T(8,128)S(1)}, f32[112,88]{1,0:T(8,128)S(1)}, u32[]{:S(2)}, u32[]{:S(2)}) collective-permute-start(f32[112,88]{1,0:T(8,128)S(1)} %get-tuple-element.34.refs_0_), channel_id=1, source_target_pairs={{0,1},{1,0},{2,3},{3,2},{4,5},{5,4},{6,7},{7,6},{8,9},{9,8},{10,11... | collective-permute-start | bytes 118280 | tf_op jit(solution)/shard_map/ppermute | solution.py:304
  31.4 4.7 %collective-permute-start.10 = (f32[80,88]{1,0:T(8,128)S(1)}, f32[80,88]{1,0:T(8,128)S(1)}, u32[]{:S(2)}, u32[]{:S(2)}) collective-permute-start(f32[80,88]{1,0:T(8,128)S(1)} %get-tuple-element.39.refs_0_), channel_id=1, source_target_pairs={{0,7},{1,2},{2,1},{3,4},{4,3},{5,6},{6,5},{7,0},{8,15},{9,10},{10,... | collective-permute-start | bytes 84488 | tf_op jit(solution)/shard_map/ppermute | solution.py:304
  31.5 4.6 %collective-permute-start.9 = (f32[80,88]{1,0:T(8,128)S(1)}, f32[80,88]{1,0:T(8,128)S(1)}, u32[]{:S(2)}, u32[]{:S(2)}) collective-permute-start(f32[80,88]{1,0:T(8,128)S(1)} %get-tuple-element.39.refs_0_), channel_id=1, source_target_pairs={{0,1},{1,0},{2,3},{3,2},{4,5},{5,4},{6,7},{7,6},{8,9},{9,8},{10,11... | collective-permute-start | bytes 84488 | tf_op jit(solution)/shard_map/ppermute | solution.py:304
  36.9 4.5 %collective-permute-start.12 = (f32[48,88]{1,0:T(8,128)S(1)}, f32[48,88]{1,0:T(8,128)S(1)}, u32[]{:S(2)}, u32[]{:S(2)}) collective-permute-start(f32[48,88]{1,0:T(8,128)S(1)} %get-tuple-element.43.refs_0_), channel_id=1, source_target_pairs={{0,7},{1,2},{2,1},{3,4},{4,3},{5,6},{6,5},{7,0},{8,15},{9,10},{10,... | collective-permute-start | bytes 50696 | tf_op jit(solution)/shard_map/ppermute | solution.py:304
  37.0 4.5 %collective-permute-start.11 = (f32[48,88]{1,0:T(8,128)S(1)}, f32[48,88]{1,0:T(8,128)S(1)}, u32[]{:S(2)}, u32[]{:S(2)}) collective-permute-start(f32[48,88]{1,0:T(8,128)S(1)} %get-tuple-element.43.refs_0_), channel_id=1, source_target_pairs={{0,1},{1,0},{2,3},{3,2},{4,5},{5,4},{6,7},{7,6},{8,9},{9,8},{10,11... | collective-permute-start | bytes 50696 | tf_op jit(solution)/shard_map/ppermute | solution.py:304

commit v5 on v4

--- a/solution.py
+++ b/solution.py
@@ -238,23 +238,18 @@
     out[...] = compose(batch, start, scaled[...], increment[...], coef)
 
 
-def step_kernel(slots, own, swapped, crossed, rest, mask, nxt, left, center_s, center_i):
+def step_kernel(slots, begin, end, own, swapped, crossed, rest, mask, out, center_s=None, center_i=None):
     members = rest.shape[1] - PAD
     scaled, increment = observe(gathered(own, swapped, crossed, slots))
     nobs = scaled.shape[0]
-    mid = nobs // (6 * slots) * 3 * slots
-    center_s[...] = scaled[mid - 3 * slots : mid + 6 * slots]
-    center_i[...] = increment[mid - 3 * slots : mid + 6 * slots]
-    rows = rest[...]
-    x = rows[:, :members]
-    p = dot3(split(x), split(scaled), NT) * mask[:, :nobs]
-    x = x + dot3(split(p), split(increment), NN)
-    k = nxt.shape[0]
-    nxt[:, :members] = x[:k]
-    nxt[:, members:] = rows[:k, members:]
-    if left is not None:
-        left[:, :members] = x[k:]
-        left[:, members:] = rows[k:, members:]
+    if center_s is not None:
+        mid = nobs // (6 * slots) * 3 * slots
+        center_s[...] = scaled[mid - 3 * slots : mid + 6 * slots]
+        center_i[...] = increment[mid - 3 * slots : mid + 6 * slots]
+    x = rest[begin:end, :members]
+    p = dot3(split(x), split(scaled), NT) * mask[begin:end, :nobs]
+    out[:, :members] = x + dot3(split(p), split(increment), NN)
+    out[:, members:] = rest[begin:end, members:]
 
 
 def stacked(maps, state):
@@ -416,24 +411,27 @@
             name="list_mask",
         )(rest, list_blocks, list_weights)
         k = width(b + 1, batches) * slots
-        outs = [shape(k, wide), shape(9 * slots, members), shape(9 * slots, members)]
+        given = (here, swapped, crossed, rest, mask)
+        centers = (shape(9 * slots, members),) * 2
+
+        def step(begin, end, more, after):
+            return pl.pallas_call(
+                lambda *refs: step_kernel(slots, begin, end, *refs[:5], *refs[5 + len(after) :]),
+                out_shape=(shape(end - begin, wide),) + more,
+                in_specs=[vm] * 5 + [tie] * len(after),
+                out_specs=(vm,) * (1 + len(more)),
+                compiler_params=params,
+                cost_estimate=cost(1),
+                name="step_columns",
+            )(*given, *after)
+
+        after = () if maps is None else (maps,)
         last = rest.shape[0] == k
-        if not last:
-            outs.insert(1, shape(rest.shape[0] - k, wide))
-            body = lambda *refs: step_kernel(slots, *refs[:5], *refs[-4:])
+        if last:
+            here, center_s, center_i = step(0, k, centers, after)
         else:
-            body = lambda *refs: step_kernel(slots, *refs[:5], refs[-3], None, *refs[-2:])
-        after = () if maps is None else (maps,)
-        res = pl.pallas_call(
-            body,
-            out_shape=tuple(outs),
-            in_specs=[vm] * 5 + [tie] * len(after),
-            out_specs=(vm,) * len(outs),
-            compiler_params=params,
-            name="step_columns",
-        )(here, swapped, crossed, rest, mask, *after)
-        here, center_s, center_i = res[0], res[-2], res[-1]
-        rest = None if last else res[1]
+            here, = step(0, k, (), after)
+            rest, center_s, center_i = step(k, rest.shape[0], centers, ())
 
     half = jax.ShapeDtypeStruct((members, rows_here), BF16)
     state = pl.pallas_call(

time: 44.3 us -> 44 us (level)
  waiting for transfers between devices: 18.4 us -> 16.4 us
  Pallas kernels: 13.6 us -> 14.9 us
    ppermute x13, waiting for transfers between devices: 18.4 us -> 16.4 us  [permute(): return lax.ppermute(x, ('gx', 'gy'), pairs)]
    pallas_call x3 -> x5, Pallas kernels: 2.66 us -> 4.02 us  [step(): pl.pallas_call(lambda *refs: step_kernel(slots, begin, end, *refs[:5], *r...]
  transfers between devices with their start and end apart: 13 -> 13, of which waited for: 8 -> 8; matrix products, arithmetic and copies ran while one was open for 0% -> 0% of each run, Pallas kernels for 12% -> 16%
where the time goes in v5:
time: 44 us; the launch traced here: 43.9 us
  waiting for transfers between devices  16.4 us (37%)
  Pallas kernels  14.9 us (34%)
  starting transfers between devices  11.4 us (26%)
  local copies, waits for them, and re-layouts  0.8 us (2%)
    ppermute x13, waiting for transfers between devices, permute(): return lax.ppermute(x, ('gx', 'gy'), pairs)  16.4 us
    ppermute x13, starting transfers between devices, permute(): return lax.ppermute(x, ('gx', 'gy'), pairs)  11.4 us
    pallas_call x5, Pallas kernels, step(): pl.pallas_call(lambda *refs: step_kernel(slots, begin, end, *refs[:5], *r...  4.02 us
    pallas_call x3, Pallas kernels, shards(): pl.pallas_call(body, out_shape=shape(nb * members, members), in_specs=[vm...  3.39 us
    pallas_call x1, Pallas kernels, shards(): pl.pallas_call(gather_kernel, out_shape=shape(n, wide), in_specs=[hbm] *...  2.89 us
    pallas_call x1, Pallas kernels, shards(): pl.pallas_call(lambda *refs: final_kernel(batches - 1, slots, *refs), out...  2.5 us
    pallas_call x1, Pallas kernels, shards(): pl.pallas_call(early_kernel, out_shape=(shape(members, rows_here), half,...  1.06 us
  transfers between devices with their start and end apart: 13, of which 8 were waited for; matrix products, arithmetic and copies ran while one was open for 0% of the time, Pallas kernels for 16%

profile of v5, /device:TPU:0, one launch (start us, length us, event | category | flops | bytes accessed | tf_op | source)
XLA Modules:
  0.0 43.9 jit_solution(14200224958353634046)
XLA Ops:
  0.0 0.0 copy-start.2
  0.0 2.9 %gather_columns.1.src = f32[64,88]{1,0:T(8,128)} custom-call(s32[4,16]{1,0:T(4,128)} %loc_in.1, s32[1,4]{1,0:T(1,128)} %bitcast.1, f32[4,16]{1,0:T(4,128)} %value_in.1, f32[4,16]{1,0:T(4,128)} %error_in.1, f32[80,8192]{1,0:T(8,128)} %ens.1), custom_call_target="tpu_custom_call" | custom-call | tf_op jit(solution)/shard_map/gather_columns/pallas_call | solution.py:315
  2.9 3.2 %collective-permute-start.1 = (f32[64,88]{1,0:T(8,128)}, f32[64,88]{1,0:T(8,128)S(1)}, u32[]{:S(2)}, u32[]{:S(2)}) collective-permute-start(f32[64,88]{1,0:T(8,128)} %gather_columns.1.src), channel_id=1, source_target_pairs={{0,96},{1,97},{2,98},{3,99},{4,100},{5,101},{6,102},{7,103},{8,104... | collective-permute-start | bytes 67592 | tf_op jit(solution)/shard_map/ppermute | solution.py:299
  6.1 0.1 collective-permute-start
  6.2 0.0 copy-start.3
  6.2 0.8 %copy-done.3 = f32[64,88]{1,0:T(8,128)S(1)} copy-done((f32[64,88]{1,0:T(8,128)S(1)}, f32[64,88]{1,0:T(8,128)}, u32[]{:S(2)}) %copy-start.3) | copy-done | bytes 22552
  7.0 1.3 %collective-permute-done.1.refs_2_ = f32[64,88]{1,0:T(8,128)S(1)} collective-permute-done((f32[64,88]{1,0:T(8,128)}, f32[64,88]{1,0:T(8,128)S(1)}, u32[]{:S(2)}, u32[]{:S(2)}) %collective-permute-start.1) | collective-permute-done | bytes 22560 | tf_op jit(solution)/shard_map/ppermute | solution.py:299
  8.3 1.9 %collective-permute-done.refs_1_ = f32[64,88]{1,0:T(8,128)S(1)} collective-permute-done((f32[64,88]{1,0:T(8,128)}, f32[64,88]{1,0:T(8,128)S(1)}, u32[]{:S(2)}, u32[]{:S(2)}) %collective-permute-start) | collective-permute-done | bytes 22560 | tf_op jit(solution)/shard_map/ppermute | solution.py:299
  10.2 4.0 %collective-permute-start.2 = (f32[96,88]{1,0:T(8,128)S(1)}, f32[96,88]{1,0:T(8,128)S(1)}, u32[]{:S(2)}, u32[]{:S(2)}) collective-permute-start(f32[96,88]{1,0:T(8,128)S(1)} %get-tuple-element.25), channel_id=1, source_target_pairs={{0,16},{1,17},{2,18},{3,19},{4,20},{5,21},{6,22},{7,23},{8,24},{9,... | collective-permute-start | bytes 101384 | tf_op jit(solution)/shard_map/ppermute | solution.py:299
  14.2 0.7 %collective-permute-start.3 = (f32[96,88]{1,0:T(8,128)S(1)}, f32[96,88]{1,0:T(8,128)S(1)}, u32[]{:S(2)}, u32[]{:S(2)}) collective-permute-start(f32[96,88]{1,0:T(8,128)S(1)} %get-tuple-element.26), channel_id=1, source_target_pairs={{0,24},{1,25},{2,26},{3,27},{4,28},{5,29},{6,30},{7,31},{8,16},{9,... | collective-permute-start | bytes 101384 | tf_op jit(solution)/shard_map/ppermute | solution.py:299
  14.9 0.3 collective-permute-start.4
  15.2 1.1 %collective-permute-done.2.refs_3_ = f32[96,88]{1,0:T(8,128)S(1)} collective-permute-done((f32[96,88]{1,0:T(8,128)S(1)}, f32[96,88]{1,0:T(8,128)S(1)}, u32[]{:S(2)}, u32[]{:S(2)}) %collective-permute-start.2) | collective-permute-done | bytes 33824 | tf_op jit(solution)/shard_map/ppermute | solution.py:299
  16.3 3.2 %collective-permute-done.3.refs_4_ = f32[96,88]{1,0:T(8,128)S(1)} collective-permute-done((f32[96,88]{1,0:T(8,128)S(1)}, f32[96,88]{1,0:T(8,128)S(1)}, u32[]{:S(2)}, u32[]{:S(2)}) %collective-permute-start.3) | collective-permute-done | bytes 33824 | tf_op jit(solution)/shard_map/ppermute | solution.py:299
  19.5 0.0 collective-permute-done.4.refs_5_
  19.5 0.1 collective-permute-start.6
  19.6 1.6 %collective-permute-start.5 = (f32[144,88]{1,0:T(8,128)S(1)}, f32[144,88]{1,0:T(8,128)S(1)}, u32[]{:S(2)}, u32[]{:S(2)}) collective-permute-start(f32[144,88]{1,0:T(8,128)S(1)} %get-tuple-element.28.refs_0_), channel_id=1, source_target_pairs={{0,1},{1,0},{2,3},{3,2},{4,5},{5,4},{6,7},{7,6},{8,9},{9,8},{10,11... | collective-permute-start | bytes 152072 | tf_op jit(solution)/shard_map/ppermute | solution.py:299
  21.2 0.0 copy-done.2
  21.2 0.0 copy-done.1
  21.2 0.2 pack_lists.1
  21.5 0.4 list_mask.3.refs_4_
  21.9 2.7 %collective-permute-done.6.refs_2_ = f32[144,88]{1,0:T(8,128)S(1)} collective-permute-done((f32[144,88]{1,0:T(8,128)S(1)}, f32[144,88]{1,0:T(8,128)S(1)}, u32[]{:S(2)}, u32[]{:S(2)}) %collective-permute-start.6) | collective-permute-done | bytes 50720 | tf_op jit(solution)/shard_map/ppermute | solution.py:299
  24.6 0.0 collective-permute-done.5.refs_1_
  24.6 0.9 %step_columns.5.refs_0_ = f32[112,88]{1,0:T(8,128)S(1)} custom-call(f32[144,88]{1,0:T(8,128)S(1)} %get-tuple-element.28.refs_0_, f32[144,88]{1,0:T(8,128)S(1)} %collective-permute-done.5.refs_1_, f32[144,88]{1,0:T(8,128)S(1)} %collective-permute-done.6.refs_2_, f32[240,88]{1,0:T(8,128)S(1)} %get-tuple-element.29.refs_0_.refs_3_, f32[240,512]{1,0:T(8,128)S(1)} %list_mask.3.refs_4_), custom_call_target="tpu_custom_call" | custom-call | flops 1000000 | bytes 100000 | tf_op jit(solution)/shard_map/step_columns/pallas_call | solution.py:418
  25.5 0.0 copy-start
  25.5 0.1 collective-permute-start.8
  25.6 0.4 collective-permute-start.7
  25.9 0.9 %step_columns.6 = (f32[128,88]{1,0:T(8,128)S(1)}, f32[144,80]{1,0:T(8,128)S(1)}, f32[144,80]{1,0:T(8,128)S(1)}) custom-call(f32[144,88]{1,0:T(8,128)S(1)} %get-tuple-element.28.refs_0_, f32[144,88]{1,0:T(8,128)S(1)} %collective-permute-done.5.refs_1_, f32[144,88]{1,0:T(8,128)S(1)} %collective-permute-done.6.refs_2_, ...), custom_call_target="tpu_custom_call" | custom-call | flops 1000000 | bytes 100000 | tf_op jit(solution)/shard_map/step_columns/pallas_call | solution.py:418
  26.8 0.2 list_mask.4.refs_4_
  27.0 1.1 %compose_maps.3.refs_5_.r_0_ = f32[640,80]{1,0:T(8,128)S(1)} custom-call(f32[144,80]{1,0:T(8,128)S(1)} %get-tuple-element.33.s, f32[144,80]{1,0:T(8,128)S(1)} %get-tuple-element.34.i, f32[4,8,256]{2,1,0:T(8,128)S(1)} %get-tuple-element.35.c.refs_3_), custom_call_target="tpu_custom_call" | custom-call | flops 1000000 | bytes 100000 | tf_op jit(solution)/shard_map/compose_maps/pallas_call | solution.py:391
  28.2 2.2 %collective-permute-done.8.refs_2_ = f32[112,88]{1,0:T(8,128)S(1)} collective-permute-done((f32[112,88]{1,0:T(8,128)S(1)}, f32[112,88]{1,0:T(8,128)S(1)}, u32[]{:S(2)}, u32[]{:S(2)}) %collective-permute-start.8) | collective-permute-done | bytes 39456 | tf_op jit(solution)/shard_map/ppermute | solution.py:299
  30.4 0.0 collective-permute-done.7.refs_1_
  30.4 0.8 %step_columns.7.refs_0_ = f32[80,88]{1,0:T(8,128)S(1)} custom-call(f32[112,88]{1,0:T(8,128)S(1)} %step_columns.5.refs_0_, f32[112,88]{1,0:T(8,128)S(1)} %collective-permute-done.7.refs_1_, f32[112,88]{1,0:T(8,128)S(1)} %collective-permute-done.8.refs_2_, f32[128,88]{1,0:T(8,128)S(1)} %get-tuple-element.32.refs_0_.refs_3_, f32[128,384]{1,0:T(8,128)S(1)} %list_mask.4.refs_4_, ...), custom_call_target="tpu_custom_call" | custom-call | flops 1000000 | bytes 100000 | tf_op jit(solution)/shard_map/step_columns/pallas_call | solution.py:418
  31.2 0.5 %collective-permute-start.10 = (f32[80,88]{1,0:T(8,128)S(1)}, f32[80,88]{1,0:T(8,128)S(1)}, u32[]{:S(2)}, u32[]{:S(2)}) collective-permute-start(f32[80,88]{1,0:T(8,128)S(1)} %step_columns.7.refs_0_), channel_id=1, source_target_pairs={{0,7},{1,2},{2,1},{3,4},{4,3},{5,6},{6,5},{7,0},{8,15},{9,10},{10,... | collective-permute-start | bytes 84488 | tf_op jit(solution)/shard_map/ppermute | solution.py:299
  31.6 0.0 collective-permute-start.9
  31.6 0.8 %step_columns.8 = (f32[48,88]{1,0:T(8,128)S(1)}, f32[144,80]{1,0:T(8,128)S(1)}, f32[144,80]{1,0:T(8,128)S(1)}) custom-call(f32[112,88]{1,0:T(8,128)S(1)} %step_columns.5.refs_0_, f32[112,88]{1,0:T(8,128)S(1)} %collective-permute-done.7.refs_1_, f32[112,88]{1,0:T(8,128)S(1)} %collective-permute-done.8.refs_2_, ...), custom_call_target="tpu_custom_call" | custom-call | flops 1000000 | bytes 100000 | tf_op jit(solution)/shard_map/step_columns/pallas_call | solution.py:418
  32.4 0.1 list_mask.5.refs_4_
  32.5 1.1 %compose_maps.4.refs_5_.r_0_ = f32[640,80]{1,0:T(8,128)S(1)} custom-call(f32[144,80]{1,0:T(8,128)S(1)} %get-tuple-element.37.s, f32[144,80]{1,0:T(8,128)S(1)} %get-tuple-element.38.i, f32[4,8,256]{2,1,0:T(8,128)S(1)} %get-tuple-element.35.c.refs_3_, f32[640,80]{1,0:T(8,128)S(1)} %compose_maps.3.refs_5_.r_0_), custom_call_target="tpu_custom_call" | custom-call | flops 1000000 | bytes 100000 | tf_op jit(solution)/shard_map/compose_maps/pallas_call | solution.py:391
  33.7 2.2 %collective-permute-done.10.refs_2_ = f32[80,88]{1,0:T(8,128)S(1)} collective-permute-done((f32[80,88]{1,0:T(8,128)S(1)}, f32[80,88]{1,0:T(8,128)S(1)}, u32[]{:S(2)}, u32[]{:S(2)}) %collective-permute-start.10) | collective-permute-done | bytes 28192 | tf_op jit(solution)/shard_map/ppermute | solution.py:299
  35.9 0.0 collective-permute-done.9.refs_1_
  35.9 0.7 %step_columns.9 = (f32[48,88]{1,0:T(8,128)S(1)}, f32[144,80]{1,0:T(8,128)S(1)}, f32[144,80]{1,0:T(8,128)S(1)}) custom-call(f32[80,88]{1,0:T(8,128)S(1)} %step_columns.7.refs_0_, f32[80,88]{1,0:T(8,128)S(1)} %collective-permute-done.9.refs_1_, f32[80,88]{1,0:T(8,128)S(1)} %collective-permute-done.10.refs_2_, f32[48,88]{1,0:T(8,128)S(1)} %get-tuple-element.36.refs_0_.refs_3_, ...), custom_call_target="tpu_custom_call" | custom-call | flops 1000000 | bytes 100000 | tf_op jit(solution)/shard_map/step_columns/pallas_call | solution.py:418
  36.6 0.5 %collective-permute-start.12 = (f32[48,88]{1,0:T(8,128)S(1)}, f32[48,88]{1,0:T(8,128)S(1)}, u32[]{:S(2)}, u32[]{:S(2)}) collective-permute-start(f32[48,88]{1,0:T(8,128)S(1)} %get-tuple-element.39.refs_0_), channel_id=1, source_target_pairs={{0,7},{1,2},{2,1},{3,4},{4,3},{5,6},{6,5},{7,0},{8,15},{9,10},{10,... | collective-permute-start | bytes 50696 | tf_op jit(solution)/shard_map/ppermute | solution.py:299
  37.1 0.0 collective-permute-start.11
  37.1 1.1 %compose_maps.5.maps = f32[640,80]{1,0:T(8,128)S(1)} custom-call(f32[144,80]{1,0:T(8,128)S(1)} %get-tuple-element.40.s, f32[144,80]{1,0:T(8,128)S(1)} %get-tuple-element.41.i, f32[4,8,256]{2,1,0:T(8,128)S(1)} %get-tuple-element.35.c.refs_3_, f32[640,80]{1,0:T(8,128)S(1)} %compose_maps.4.refs_5_.r_0_), custom_call_target="tpu_custom_call" | custom-call | flops 1000000 | bytes 100000 | tf_op jit(solution)/shard_map/compose_maps/pallas_call | solution.py:391
  38.3 0.0 copy-done
  38.3 1.1 %apply_early_maps.1 = (f32[80,8192]{1,0:T(8,128)S(1)}, bf16[80,8192]{1,0:T(8,128)(2,1)S(1)}, bf16[80,8192]{1,0:T(8,128)(2,1)S(1)}) custom-call(f32[640,80]{1,0:T(8,128)S(1)} %compose_maps.5.maps, f32[80,8192]{1,0:T(8,128)S(1)} %copy-done), custom_call_target="tpu_custom_call" | custom-call | flops 1000000 | bytes 100000 | tf_op jit(solution)/shard_map/apply_early_maps/pallas_call | solution.py:437
  39.3 1.8 %collective-permute-done.12.refs_2_ = f32[48,88]{1,0:T(8,128)S(1)} collective-permute-done((f32[48,88]{1,0:T(8,128)S(1)}, f32[48,88]{1,0:T(8,128)S(1)}, u32[]{:S(2)}, u32[]{:S(2)}) %collective-permute-start.12) | collective-permute-done | bytes 16928 | tf_op jit(solution)/shard_map/ppermute | solution.py:299
  41.2 0.0 collective-permute-done.11.refs_1_
  41.2 2.5 %apply_maps.1 = f32[80,8192]{1,0:T(8,128)} custom-call(f32[48,88]{1,0:T(8,128)S(1)} %get-tuple-element.39.refs_0_, f32[48,88]{1,0:T(8,128)S(1)} %collective-permute-done.11.refs_1_, f32[48,88]{1,0:T(8,128)S(1)} %collective-permute-done.12.refs_2_, f32[4,8,256]{2,1,0:T(8,128)S(1)} %get-tuple-element.35.c.refs_3_, f32[80,8192]{1,0:T(8,128)S(1)} %get-tuple-element.42.refs_4_, ...), custom_call_target="tpu_custom_call" | custom-call | tf_op jit(solution)/shard_map/apply_maps/pallas_call | solution.py:446
  (4 shorter events, 0.1 us)
Async XLA Ops:
  0.0 21.2 %copy-start.2 = (f32[4,8,2048]{2,1,0:T(8,128)S(1)}, f32[4,8,2048]{2,1,0:T(8,128)}, u32[]{:S(2)}) copy-start(f32[4,8,2048]{2,1,0:T(8,128)} %weights.1) | copy-start | bytes 786436
  0.0 21.2 %copy-start.1 = (s32[4,8,2048]{2,1,0:T(8,128)S(1)}, s32[4,8,2048]{2,1,0:T(8,128)}, u32[]{:S(2)}) copy-start(s32[4,8,2048]{2,1,0:T(8,128)} %blocks.1) | copy-start | bytes 786436
  2.9 5.4 %collective-permute-start.1 = (f32[64,88]{1,0:T(8,128)}, f32[64,88]{1,0:T(8,128)S(1)}, u32[]{:S(2)}, u32[]{:S(2)}) collective-permute-start(f32[64,88]{1,0:T(8,128)} %gather_columns.1.src), channel_id=1, source_target_pairs={{0,96},{1,97},{2,98},{3,99},{4,100},{5,101},{6,102},{7,103},{8,104... | collective-permute-start | bytes 67592 | tf_op jit(solution)/shard_map/ppermute | solution.py:299
  6.1 4.1 %collective-permute-start = (f32[64,88]{1,0:T(8,128)}, f32[64,88]{1,0:T(8,128)S(1)}, u32[]{:S(2)}, u32[]{:S(2)}) collective-permute-start(f32[64,88]{1,0:T(8,128)} %gather_columns.1.src), channel_id=1, source_target_pairs={{0,32},{1,33},{2,34},{3,35},{4,36},{5,37},{6,38},{7,39},{8,40},{9,... | collective-permute-start | bytes 67592 | tf_op jit(solution)/shard_map/ppermute | solution.py:299
  6.2 0.8 %copy-start.3 = (f32[64,88]{1,0:T(8,128)S(1)}, f32[64,88]{1,0:T(8,128)}, u32[]{:S(2)}) copy-start(f32[64,88]{1,0:T(8,128)} %gather_columns.1.src) | copy-start | bytes 67588
  10.2 6.0 %collective-permute-start.2 = (f32[96,88]{1,0:T(8,128)S(1)}, f32[96,88]{1,0:T(8,128)S(1)}, u32[]{:S(2)}, u32[]{:S(2)}) collective-permute-start(f32[96,88]{1,0:T(8,128)S(1)} %get-tuple-element.25), channel_id=1, source_target_pairs={{0,16},{1,17},{2,18},{3,19},{4,20},{5,21},{6,22},{7,23},{8,24},{9,... | collective-permute-start | bytes 101384 | tf_op jit(solution)/shard_map/ppermute | solution.py:299
  14.2 5.3 %collective-permute-start.3 = (f32[96,88]{1,0:T(8,128)S(1)}, f32[96,88]{1,0:T(8,128)S(1)}, u32[]{:S(2)}, u32[]{:S(2)}) collective-permute-start(f32[96,88]{1,0:T(8,128)S(1)} %get-tuple-element.26), channel_id=1, source_target_pairs={{0,24},{1,25},{2,26},{3,27},{4,28},{5,29},{6,30},{7,31},{8,16},{9,... | collective-permute-start | bytes 101384 | tf_op jit(solution)/shard_map/ppermute | solution.py:299
  14.9 4.6 %collective-permute-start.4 = (f32[96,88]{1,0:T(8,128)S(1)}, f32[96,88]{1,0:T(8,128)S(1)}, u32[]{:S(2)}, u32[]{:S(2)}) collective-permute-start(f32[96,88]{1,0:T(8,128)S(1)} %get-tuple-element.27), channel_id=1, source_target_pairs={{0,8},{1,9},{2,10},{3,11},{4,12},{5,13},{6,14},{7,15},{8,0},{9,1},... | collective-permute-start | bytes 101384 | tf_op jit(solution)/shard_map/ppermute | solution.py:299
  19.5 5.1 %collective-permute-start.6 = (f32[144,88]{1,0:T(8,128)S(1)}, f32[144,88]{1,0:T(8,128)S(1)}, u32[]{:S(2)}, u32[]{:S(2)}) collective-permute-start(f32[144,88]{1,0:T(8,128)S(1)} %get-tuple-element.28.refs_0_), channel_id=1, source_target_pairs={{0,7},{1,2},{2,1},{3,4},{4,3},{5,6},{6,5},{7,0},{8,15},{9,10},{10,... | collective-permute-start | bytes 152072 | tf_op jit(solution)/shard_map/ppermute | solution.py:299
  19.6 5.0 %collective-permute-start.5 = (f32[144,88]{1,0:T(8,128)S(1)}, f32[144,88]{1,0:T(8,128)S(1)}, u32[]{:S(2)}, u32[]{:S(2)}) collective-permute-start(f32[144,88]{1,0:T(8,128)S(1)} %get-tuple-element.28.refs_0_), channel_id=1, source_target_pairs={{0,1},{1,0},{2,3},{3,2},{4,5},{5,4},{6,7},{7,6},{8,9},{9,8},{10,11... | collective-permute-start | bytes 152072 | tf_op jit(solution)/shard_map/ppermute | solution.py:299
  25.5 12.8 %copy-start = (f32[80,8192]{1,0:T(8,128)S(1)}, f32[80,8192]{1,0:T(8,128)}, u32[]{:S(2)}) copy-start(f32[80,8192]{1,0:T(8,128)} %ens.1) | copy-start | bytes 7864324
  25.5 4.9 %collective-permute-start.8 = (f32[112,88]{1,0:T(8,128)S(1)}, f32[112,88]{1,0:T(8,128)S(1)}, u32[]{:S(2)}, u32[]{:S(2)}) collective-permute-start(f32[112,88]{1,0:T(8,128)S(1)} %step_columns.5.refs_0_), channel_id=1, source_target_pairs={{0,7},{1,2},{2,1},{3,4},{4,3},{5,6},{6,5},{7,0},{8,15},{9,10},{10,... | collective-permute-start | bytes 118280 | tf_op jit(solution)/shard_map/ppermute | solution.py:299
  25.6 4.8 %collective-permute-start.7 = (f32[112,88]{1,0:T(8,128)S(1)}, f32[112,88]{1,0:T(8,128)S(1)}, u32[]{:S(2)}, u32[]{:S(2)}) collective-permute-start(f32[112,88]{1,0:T(8,128)S(1)} %step_columns.5.refs_0_), channel_id=1, source_target_pairs={{0,1},{1,0},{2,3},{3,2},{4,5},{5,4},{6,7},{7,6},{8,9},{9,8},{10,11... | collective-permute-start | bytes 118280 | tf_op jit(solution)/shard_map/ppermute | solution.py:299
  31.2 4.7 %collective-permute-start.10 = (f32[80,88]{1,0:T(8,128)S(1)}, f32[80,88]{1,0:T(8,128)S(1)}, u32[]{:S(2)}, u32[]{:S(2)}) collective-permute-start(f32[80,88]{1,0:T(8,128)S(1)} %step_columns.7.refs_0_), channel_id=1, source_target_pairs={{0,7},{1,2},{2,1},{3,4},{4,3},{5,6},{6,5},{7,0},{8,15},{9,10},{10,... | collective-permute-start | bytes 84488 | tf_op jit(solution)/shard_map/ppermute | solution.py:299
  31.6 4.2 %collective-permute-start.9 = (f32[80,88]{1,0:T(8,128)S(1)}, f32[80,88]{1,0:T(8,128)S(1)}, u32[]{:S(2)}, u32[]{:S(2)}) collective-permute-start(f32[80,88]{1,0:T(8,128)S(1)} %step_columns.7.refs_0_), channel_id=1, source_target_pairs={{0,1},{1,0},{2,3},{3,2},{4,5},{5,4},{6,7},{7,6},{8,9},{9,8},{10,11... | collective-permute-start | bytes 84488 | tf_op jit(solution)/shard_map/ppermute | solution.py:299
  36.6 4.5 %collective-permute-start.12 = (f32[48,88]{1,0:T(8,128)S(1)}, f32[48,88]{1,0:T(8,128)S(1)}, u32[]{:S(2)}, u32[]{:S(2)}) collective-permute-start(f32[48,88]{1,0:T(8,128)S(1)} %get-tuple-element.39.refs_0_), channel_id=1, source_target_pairs={{0,7},{1,2},{2,1},{3,4},{4,3},{5,6},{6,5},{7,0},{8,15},{9,10},{10,... | collective-permute-start | bytes 50696 | tf_op jit(solution)/shard_map/ppermute | solution.py:299
  37.1 4.1 %collective-permute-start.11 = (f32[48,88]{1,0:T(8,128)S(1)}, f32[48,88]{1,0:T(8,128)S(1)}, u32[]{:S(2)}, u32[]{:S(2)}) collective-permute-start(f32[48,88]{1,0:T(8,128)S(1)} %get-tuple-element.39.refs_0_), channel_id=1, source_target_pairs={{0,1},{1,0},{2,3},{3,2},{4,5},{5,4},{6,7},{7,6},{8,9},{9,8},{10,11... | collective-permute-start | bytes 50696 | tf_op jit(solution)/shard_map/ppermute | solution.py:299
